TPU v7x, 32 devices: a whole 2x2x4 slice. The times are simulated.
32 devices in a mesh: groups: 2 (over y), seq: 16 (over z, x, core).
Axes of the slice: x: 2, y: 2, z: 4, core: 2. Of those that a mesh axis runs over, the one named last changes fastest.
Arguments:
- pool_kv: bfloat16 [3072, 1024], P(('groups', 'seq')), parts along dimension 0, may hold values from -6 to 6
- pool_slot: int32 [32], P('groups'), parts along dimension 0, may hold values from 0 to 15, each once
- passage_order: int32 [32], P('groups'), parts along dimension 0, may hold values from 0 to 15, each once
- passage_start: int32 [32], P('groups'), parts along dimension 0, may hold values from 0 to 6784, as said below
- recompute_pos: int32 [32, 56], P('groups'), parts along dimension 0, may hold values from 0 to 383, as said below
- page_table: int32 [3072], P('groups'), parts along dimension 0, may hold values from 0 to 1535, as said below
- fresh_q: bfloat16 [1792, 1024], P(('groups', 'seq')), parts along dimension 0, may hold values from -64 to 64
- fresh_kv: bfloat16 [1792, 256], P(('groups', 'seq')), parts along dimension 0, may hold values from -64 to 64
Outputs:
- attended: bfloat16 [1792, 1024], P(('groups', 'seq')), parts along dimension 0
- decode_cache: bfloat16 [3072, 1024], P(('groups', 'seq')), parts along dimension 0
There are 2 independent parts, one for each index of `groups`. A program takes and returns all parts, laid end to end along the dimension named above; each array names one. Nothing has to cross between parts.
Inputs may be any that keep to these rules, and one draw needn't show every extreme that they name: `passage_start`: increases by at least 384 from one passage to the next; the first is 0 and the last is (15) * 384 + 1024. `recompute_pos`: each row holds 56 different positions of its passage in increasing order. `page_table`: every row of the decode cache receives exactly one page; of the 96 pages of one passage at most 6 go to the 96 rows of one owner, and that many do for some owner.
All inputs are finite; a program needn't handle non-finite values.
Results may differ from a plain program's by a relative error of at most 0.0075.
The roundings to bfloat16 on the way count: a program that leaves them out, or rounds other values in their place, can miss the bound.
Values may be sent and summed in bfloat16 or wider, within the bound.
No kernel may reach another device: no remote copies, remote signals or barrier semaphores. Data moves between devices by JAX's collectives and lax.ppermute only.
A program may use at most 256 MiB of HBM per device.

v0:
```python
from functools import partial

import jax
import jax.numpy as jnp
from jax import lax
from jax.sharding import PartitionSpec as P

GROUP = 8
PAGE = 4


ROPE_BASE = 500000.0


def rotate_pos(vector, positions):
    half_dim = vector.shape[-1] // 2
    frequency = ROPE_BASE ** (-(jnp.arange(half_dim, dtype=jnp.float32) * (2.0 / vector.shape[-1])))
    angles = positions.astype(jnp.float32)[..., None] * frequency
    cosine = jnp.cos(angles)
    sine = jnp.sin(angles)
    lower_half = vector[..., :half_dim]
    upper_half = vector[..., half_dim:]
    return jnp.concatenate(
        [lower_half * cosine - upper_half * sine, upper_half * cosine + lower_half * sine], axis=-1
    )


def attend(running, query_rows, query_pos, key_part, value_part, key_pos, usable):
    peak_score, weight_sum, weighted = running
    score_scale = key_part.shape[1] ** (-0.5)
    scores = jnp.dot(query_rows, key_part.T, preferred_element_type=jnp.float32) * score_scale
    allowed = key_pos[None, :] <= query_pos[:, None]
    new_peak = jnp.maximum(peak_score, jnp.max(jnp.where(allowed, scores, -jnp.inf), axis=1))
    weights = jnp.where(allowed, jnp.exp(scores - new_peak[:, None]), 0.0)
    weight_sum = jnp.sum(weights, axis=1)
    weighted = jnp.dot(weights.astype(jnp.bfloat16), value_part, preferred_element_type=jnp.float32)
    return (new_peak, weight_sum, weighted)


def visit(running, prepared, key_part, value_part, key_pos):
    result = []
    for (query_rows, query_pos), group_state in zip(prepared, running):
        advance = partial(
            attend,
            query_rows=query_rows,
            query_pos=query_pos,
            key_part=key_part,
            value_part=value_part,
            key_pos=key_pos,
            usable=None,
        )
        group_state = advance(group_state)
        result.append(group_state)
    return tuple(result)


def shards(
    pool_kv, pool_slot, passage_order, passage_start, recompute_pos, page_table, fresh_q, fresh_kv
):
    seq_count = lax.axis_size("seq")
    my_index = lax.axis_index("seq")
    page_count = pool_kv.shape[0]
    row_width = pool_kv.shape[1]
    head_dim = fresh_kv.shape[1] // 2
    sel_count = fresh_q.shape[0]
    tok_count = page_count * PAGE
    capacity = max(1, page_count // seq_count)
    passage_ids = jnp.arange(seq_count, dtype=jnp.int32)
    page_ids = jnp.arange(page_count, dtype=jnp.int32)
    slot_holder = jnp.zeros((seq_count,), jnp.int32).at[pool_slot].set(passage_ids)
    passage_place = jnp.zeros((seq_count,), jnp.int32).at[passage_order].set(passage_ids)
    held_spot = page_ids * seq_count + my_index
    receiver = passage_place[slot_holder[held_spot // page_count]]
    outgoing = (
        jnp.zeros((seq_count * capacity, row_width), pool_kv.dtype)
        .at[receiver * capacity + page_ids % capacity]
        .set(pool_kv)
    )
    arrived = lax.all_to_all(outgoing, "seq", split_axis=0, concat_axis=0, tiled=True)
    wanted = pool_slot[passage_order[my_index]] * page_count + page_ids
    cached = arrived[wanted % seq_count * capacity + wanted // seq_count % capacity].reshape(
        tok_count, 2, head_dim
    )
    start_pos = passage_start[my_index]
    picked = recompute_pos[my_index]
    fresh_pos = start_pos + picked
    shifted = rotate_pos(
        cached[:, 0, :].astype(jnp.float32), jnp.broadcast_to(start_pos, (tok_count,))
    )
    fresh_keys = rotate_pos(fresh_kv[:, :head_dim].astype(jnp.float32), fresh_pos).astype(
        jnp.bfloat16
    )
    key_rows = shifted.astype(jnp.bfloat16).at[picked].set(fresh_keys)
    value_rows = cached[:, 1, :].at[picked].set(fresh_kv[:, head_dim:])
    blended = jnp.stack([key_rows, value_rows], axis=1)
    page_rows = blended.reshape(page_count, row_width)
    my_table = lax.dynamic_slice_in_dim(page_table, my_index * page_count, page_count)
    owners = my_table // page_count
    before = page_ids[None, :] < page_ids[:, None]
    rank_out = jnp.sum(jnp.logical_and(owners[None, :] == owners[:, None], before), axis=1)
    outgoing_pages = (
        jnp.zeros((seq_count * capacity, row_width), page_rows.dtype)
        .at[owners * capacity + rank_out]
        .set(page_rows)
    )
    landed = lax.all_to_all(outgoing_pages, "seq", split_axis=0, concat_axis=0, tiled=True)
    total_pages = seq_count * page_count
    page_source = (
        jnp.zeros((total_pages,), jnp.int32)
        .at[page_table]
        .set(jnp.arange(total_pages, dtype=jnp.int32))
    )
    my_sources = lax.dynamic_slice_in_dim(page_source, my_index * page_count, page_count)
    source_dev = my_sources // page_count
    source_page = my_sources % page_count
    source_owners = (page_table // page_count).reshape(seq_count, page_count)[source_dev]
    rank_in = jnp.sum(
        jnp.logical_and(source_owners == my_index, page_ids[None, :] < source_page[:, None]), axis=1
    )
    decode_cache = landed[source_dev * capacity + rank_in]
    queries = rotate_pos(
        fresh_q.reshape(sel_count, GROUP, head_dim).astype(jnp.float32), fresh_pos[:, None]
    ).astype(jnp.bfloat16)
    query_pos = my_index * tok_count + picked
    groups = [(queries, query_pos)]
    prepared = [
        (group_rows.reshape(-1, head_dim), jnp.repeat(positions, GROUP))
        for group_rows, positions in groups
    ]
    initial = []
    for group_rows, positions in prepared:
        row_count = group_rows.shape[0]
        initial.append(
            (
                jnp.full((row_count,), -1e30, jnp.float32),
                jnp.zeros((row_count,), jnp.float32),
                jnp.zeros((row_count, head_dim), jnp.float32),
            )
        )
    initial = tuple(initial)
    flat_rows = blended.reshape(tok_count, 2 * head_dim)
    piece = lax.all_gather(flat_rows, "seq", axis=0, tiled=True)
    key_pos = jnp.arange(piece.shape[0], dtype=jnp.int32)
    finals = visit(initial, prepared, piece[:, :head_dim], piece[:, head_dim:], key_pos)
    outputs = []
    for group_state in finals:
        outputs.append((group_state[2] / group_state[1][:, None]).astype(jnp.bfloat16))
    attended = outputs[0].reshape(sel_count, GROUP * head_dim)
    return (attended, decode_cache)


def solution(mesh):
    placed = (
        P(("groups", "seq"), None),
        P("groups"),
        P("groups"),
        P("groups"),
        P("groups", None),
        P("groups"),
        P(("groups", "seq"), None),
        P(("groups", "seq"), None),
    )
    return jax.shard_map(
        shards,
        mesh=mesh,
        in_specs=placed,
        out_specs=(P(("groups", "seq"), None), P(("groups", "seq"), None)),
        check_vma=False,
    )
```

profile of v0, /device:TPU:0, one launch (start us, length us, event | category | flops | bytes accessed | tf_op | source)
XLA Modules:
  0.0 124.4 jit_solution(2867619107465769491)
XLA Ops:
  7.2 0.7 compare_select_fusion.9
  7.8 0.7 compare_select_fusion.10
  9.1 0.7 fusion.58
  10.5 0.7 fusion.57
  11.2 20.1 %fusion.46 = s32[96]{0:T(128)S(1)} fusion(s32[]{:T(128)} %bitcast.50, s32[]{:T(128)} %bitcast.23, s32[]{:T(128)} %bitcast.51, s32[]{:T(128)} %bitcast.24, s32[]{:T(128)} %bitcast.52, s32[]{:T(128)} %bitcast.25, s32[]{:T(128)} %bitcast.53, s32[]{:T(128)} %bitcast.26, s32[]{:T(128)} %bitcast.54, s32[]{:T(128)} %bitcast.27, s32[]{:T(128)} %bitcast.56, ...), kind=kLoop, calls=%fused_computation.127 | loop fusion | flops 8352 | bytes 516 | tf_op jit(solution)/shard_map/select_n | solution.py:77
  31.3 1.4 %scatter_custom_fusion.2 = bf16[96,1024]{1,0:T(8,128)(2,1)S(1)} fusion(s32[96]{0:T(128)S(1)} %fusion.46, bf16[96,1024]{1,0:T(8,128)(2,1)} %param.8, bf16[]{:T(256)} %constant.84.clone.1), kind=kCustom, calls=%fused_computation.38 | custom fusion | bytes 197120 | tf_op jit(solution)/shard_map/scatter | solution.py:77
  32.7 0.8 all_to_all.16
  33.5 7.4 %all-to-all-start = ((bf16[16,6,1024]{2,1,0:T(8,128)(2,1)}), bf16[16,6,1024]{2,1,0:T(8,128)(2,1)S(1)}, u32[]{:S(2)}, u32[]{:S(2)}) async-start(bf16[16,6,1024]{2,1,0:T(8,128)(2,1)} %all_to_all.16), calls=%async_computation | async-start | bytes 524288 | tf_op jit(solution)/shard_map/all_to_all | solution.py:79
  40.9 1.2 dynamic_slice.20
  44.1 1.2 dynamic_slice.21
  45.4 1.2 dynamic_slice.19
  47.3 0.7 fusion.48
  48.0 1.3 %add_bitcast_fusion = (s32[56]{0:T(128)S(1)}, f32[56]{0:T(128)S(1)}) fusion(s32[]{:T(128)S(6)} %mul.169, s32[16,56]{1,0:T(8,128)} %param.12, s32[]{:T(128)S(6)} %select_n.161, s32[]{:T(128)} %bitcast.1), kind=kLoop, calls=%fused_computation.132 | loop fusion | flops 168 | bytes 684 | tf_op jit(solution)/shard_map/add | solution.py:124
  49.4 0.7 slice_convert_fusion
  51.0 0.8 gather_fusion
  52.3 1.0 scatter_custom_fusion.4
  53.5 0.9 scatter_custom_fusion.3
  54.4 0.8 copy.17
  55.3 0.7 compare_select_fusion
  56.1 6.2 %scatter_custom_fusion.6 = s32[1536]{0:T(1024)S(1)} fusion(s32[1536]{0:T(1024)S(1)} %get-tuple-element.13, s32[1536]{0:T(1024)S(1)} %iota.45, s32[]{:T(128)} %constant.80.clone.1), kind=kCustom, calls=%fused_computation.65 | custom fusion | bytes 6148 | tf_op jit(solution)/shard_map/scatter | solution.py:111
  62.3 0.8 compare_select_fusion.2
  64.1 0.9 convert_bitcast_fusion
  65.4 1.1 scatter_custom_fusion.5
  66.4 0.8 all_to_all.19
  67.2 6.0 %all-to-all-start.1 = ((bf16[16,6,1024]{2,1,0:T(8,128)(2,1)}), bf16[16,6,1024]{2,1,0:T(8,128)(2,1)S(1)}, u32[]{:S(2)}, u32[]{:S(2)}) async-start(bf16[16,6,1024]{2,1,0:T(8,128)(2,1)} %all_to_all.19), calls=%async_computation.1 | async-start | bytes 524288 | tf_op jit(solution)/shard_map/all_to_all | solution.py:106
  73.6 10.1 %all-to-all-done.1 = bf16[16,6,1024]{2,1,0:T(8,128)(2,1)S(1)} async-done(((bf16[16,6,1024]{2,1,0:T(8,128)(2,1)}), bf16[16,6,1024]{2,1,0:T(8,128)(2,1)S(1)}, u32[]{:S(2)}, u32[]{:S(2)}) %all-to-all-start.1) | async-done | bytes 196640 | tf_op jit(solution)/shard_map/all_to_all | solution.py:106
  83.8 1.5 %gather_fusion.2 = bf16[96,1024]{1,0:T(8,128)(2,1)} fusion(bf16[96,1024]{1,0:T(8,128)(2,1)S(1)} %all_to_all.21, s32[1024]{0:T(1024)S(1)} %pad_clamp_fusion), kind=kCustom, calls=%fused_computation.2 | custom fusion | bytes 393600 | tf_op jit(solution)/shard_map/gather | solution.py:120
  85.2 22.2 %all-gather.2.cloned.1.call-done = bf16[6144,256]{0,1:T(8,128)(2,1)} async-done(((bf16[384,256]{0,1:T(8,128)(2,1)}), bf16[6144,256]{0,1:T(8,128)(2,1)}) %all-gather.2.cloned.1.call-update) | async-done | bytes 3145744 | tf_op jit(solution)/shard_map/all_gather | solution.py:142
  107.4 3.9 %select_reduce_fusion = (f32[448]{0:T(512)S(1)}, f32[448,6144]{1,0:T(8,128)S(1)}) fusion(s32[448]{0:T(512)S(1)} %le.16, bf16[6144,256]{0,1:T(8,128)(2,1)} %all-gather.2.cloned.1.call-done, bf16[448,64]{1,0:T(8,128)(2,1)S(1)} %get-tuple-element.5, bf16[448,64]{1,0:T(8,128)(2,1)S(1)} %get-tuple-element.4), kind=kOutput, calls=%fused_computation.11 | convolution fusion | flops 715882048 | bytes 12701184 | tf_op jit(solution)/shard_map/dot_general | solution.py:31
  111.3 3.0 %fusion = f32[448]{0:T(512)S(1)} fusion(f32[448,6144]{1,0:T(8,128)S(1)} %get-tuple-element.52, f32[448]{0:T(512)S(1)} %broadcast_maximum_fusion, s32[448]{0:T(512)S(1)} %le.16), kind=kLoop, calls=%fused_computation.13 | loop fusion | flops 13762112 | bytes 11015424 | tf_op jit(solution)/shard_map/reduce_sum | solution.py:35
  114.3 2.6 %fusion.12 = bf16[448,128]{1,0:T(8,128)(2,1)S(1)} fusion(bf16[6144,256]{0,1:T(8,128)(2,1)S(1)} %copy-done, f32[448,6144]{1,0:T(8,128)S(1)} %get-tuple-element.52, f32[448]{0:T(512)S(1)} %broadcast_maximum_fusion, s32[448]{0:T(512)S(1)} %le.16, f32[448]{0:T(512)S(1)} %fusion), kind=kOutput, calls=%fused_computation.20 | convolution fusion | flops 718520320 | bytes 12703744 | tf_op jit(solution)/shard_map/dot_general | solution.py:36
  116.9 0.7 reshape.365
  (38 shorter events, 4.2 us)
Async XLA Ops:
  33.5 17.4 %all-to-all-start = ((bf16[16,6,1024]{2,1,0:T(8,128)(2,1)}), bf16[16,6,1024]{2,1,0:T(8,128)(2,1)S(1)}, u32[]{:S(2)}, u32[]{:S(2)}) async-start(bf16[16,6,1024]{2,1,0:T(8,128)(2,1)} %all_to_all.16), calls=%async_computation | async-start | bytes 524288 | tf_op jit(solution)/shard_map/all_to_all | solution.py:79
  40.9 66.5 %all-gather.2.cloned.1.call-start = ((), (), s32[]{:S(2)}) async-start(), calls=%async_computation.2 | async-start | bytes 3342336 | tf_op jit(solution)/shard_map/all_gather | solution.py:142
  67.2 16.5 %all-to-all-start.1 = ((bf16[16,6,1024]{2,1,0:T(8,128)(2,1)}), bf16[16,6,1024]{2,1,0:T(8,128)(2,1)S(1)}, u32[]{:S(2)}, u32[]{:S(2)}) async-start(bf16[16,6,1024]{2,1,0:T(8,128)(2,1)} %all_to_all.19), calls=%async_computation.1 | async-start | bytes 524288 | tf_op jit(solution)/shard_map/all_to_all | solution.py:106
  107.4 6.9 %copy-start = (bf16[6144,256]{0,1:T(8,128)(2,1)S(1)}, bf16[6144,256]{0,1:T(8,128)(2,1)}, u32[]{:S(2)}) copy-start(bf16[6144,256]{0,1:T(8,128)(2,1)} %all-gather.2.cloned.1.call-done) | copy-start | bytes 9437188
Sparse Core Ops, SparseCore 0:
  55.4 51.9 all-gather.1
where the time goes:
time: 125 us; the launch traced here: 124 us
  waiting for transfers between devices  32.3 us (26%)
  other arithmetic  31.6 us (25%)
  local copies, waits for them, and re-layouts  23.2 us (19%)
  between operations  17.5 us (14%)
  starting transfers between devices  13.4 us (11%)
  matrix products  6.5 us (5%)
    all_gather x1, waiting for transfers between devices, shards(): piece = lax.all_gather(flat_rows, 'seq', axis=0, tiled=True)  22.2 us
    select_n x1, other arithmetic, shards(): outgoing = jnp.zeros((seq_count * capacity, row_width), pool_kv.dtype).at...  20.1 us
    all_to_all x1, waiting for transfers between devices, shards(): lax.all_to_all(outgoing_pages, 'seq', split_axis=0, concat_axis=0, tiled=...  10.1 us
    all_to_all x1, starting transfers between devices, shards(): lax.all_to_all(outgoing, 'seq', split_axis=0, concat_axis=0, tiled=True)  7.36 us
    scatter x1, local copies, waits for them, and re-layouts, shards(): page_source = jnp.zeros((total_pages,), jnp.int32).at[page_table].set(jnp...  6.18 us
    all_to_all x1, starting transfers between devices, shards(): lax.all_to_all(outgoing_pages, 'seq', split_axis=0, concat_axis=0, tiled=...  6 us
    dot_general x1, matrix products, attend(): jnp.dot(query_rows, key_part.T, preferred_element_type=jnp.float32)  3.86 us
    reduce_sum x1, other arithmetic, attend(): weight_sum = jnp.sum(weights, axis=1)  2.99 us
  transfers between devices with their start and end apart: 3, of which 2 were waited for; matrix products, arithmetic and copies ran while one was open for 16% of the time, Pallas kernels for 0%

commit v1 on v0

v1 whole, which is shorter than its diff:
```python
from functools import partial

import jax
import jax.numpy as jnp
import numpy as np
from jax import lax
from jax.experimental import pallas as pl
from jax.experimental.pallas import tpu as pltpu
from jax.sharding import PartitionSpec as P

GROUP = 8
PAGE = 4
ROPE_BASE = 500000.0
FAR = float(2**23)
MASKED = -1e30
LOWEST = -1e29
TILE = 16

f32 = jnp.float32
bf16 = jnp.bfloat16


def round_up(value, step):
    return -(-value // step) * step


def frequencies(head_dim):
    half = head_dim // 2
    index = np.arange(half, dtype=np.float32) * np.float32(2.0 / head_dim)
    one = np.power(np.float32(ROPE_BASE), -index).astype(np.float32)
    return np.concatenate([one, one])[None, :]


def ring_place(chip, chips):
    return jnp.where(chip % 2 == 0, chip // 2, chips - 1 - chip // 2)


def ring_chip(place, chips):
    return jnp.where(place < chips // 2, 2 * place, 2 * (chips - 1 - place) + 1)


def ring_order(chips):
    return list(range(0, chips, 2)) + list(range(chips - 1, 0, -2))


def ring_pairs(chips, shift):
    order = ring_order(chips)
    return [
        (order[p] * 2 + core, order[(p + shift) % chips] * 2 + core)
        for p in range(chips)
        for core in range(2)
    ]


def turned(vector, cosine, signed_sine):
    half = vector.shape[1] // 2
    return vector * cosine + pltpu.roll(vector, half, 1) * signed_sine


def prep_kernel(
    seq_count, slot_ref, order_ref, start_ref, freq_ref, picked_ref, pool_ref, q_ref, kv_ref,
    chunk_ref, queries_ref, fresh_ref, heads_ref,
):
    pages = pool_ref.shape[0]
    sel = kv_ref.shape[0]
    head_dim = freq_ref.shape[1]
    pair = 2 * head_dim
    extra = chunk_ref.shape[0] - pages
    me = lax.axis_index("seq")
    sign = jnp.where(lax.broadcasted_iota(jnp.int32, (1, head_dim), 1) < head_dim // 2, -1.0, 1.0)
    spot = lax.broadcasted_iota(jnp.int32, (pages, head_dim), 0) * seq_count + me

    def place(k, start):
        low = slot_ref[order_ref[k]] * pages
        return jnp.where(jnp.logical_and(spot >= low, spot < low + pages), start_ref[k], start)

    start = lax.fori_loop(0, seq_count, place, jnp.zeros((pages, head_dim), jnp.int32), unroll=8)
    angle = start.astype(f32) * freq_ref[...]
    cosine, sine = jnp.cos(angle), jnp.sin(angle) * sign
    for u in range(PAGE):
        keys = slice(u * pair, u * pair + head_dim)
        values = slice(u * pair + head_dim, (u + 1) * pair)
        chunk_ref[:pages, keys] = turned(pool_ref[:, keys].astype(f32), cosine, sine).astype(bf16)
        chunk_ref[:pages, values] = pool_ref[:, values]

    row = jnp.broadcast_to(picked_ref[pl.ds(me, 1), :].astype(f32), (sel, sel))
    same = lax.broadcasted_iota(jnp.int32, (sel, sel), 0) == lax.broadcasted_iota(
        jnp.int32, (sel, sel), 1
    )
    picked = jnp.sum(jnp.where(same, row, 0.0), axis=1, keepdims=True)
    angle = (picked + start_ref[me].astype(f32)) * freq_ref[...]
    cosine, sine = jnp.cos(angle), jnp.sin(angle) * sign
    fresh_ref[...] = jnp.zeros_like(fresh_ref)
    fresh_ref[:sel, :head_dim] = turned(kv_ref[:, :head_dim].astype(f32), cosine, sine)
    fresh_ref[:sel, head_dim:] = kv_ref[:, head_dim:].astype(f32)
    for u in range(PAGE):
        chunk_ref[pages:, u * pair : (u + 1) * pair] = fresh_ref[
            u * extra : (u + 1) * extra, :
        ].astype(bf16)
    for h in range(GROUP):
        head = q_ref[:, h * head_dim : (h + 1) * head_dim].astype(f32)
        heads_ref[h * sel : (h + 1) * sel, :] = turned(head, cosine, sine)
    queries_ref[...] = heads_ref[...].astype(bf16)


def chunk_rows(pieces):
    parts = []
    width = pieces[0].shape[1] // PAGE
    for u in range(PAGE):
        for piece in pieces:
            parts.append(piece[:, u * width : (u + 1) * width])
    return jnp.concatenate(parts, axis=0)


def visit_kernel(seq_count, steps, layout, first, last, *refs):
    piece_count = sum(layout)
    pieces = refs[:piece_count]
    own_q, other_q, meta_ref, limit_ref, wanted_ref = refs[piece_count : piece_count + 5]
    refs = refs[piece_count + 5 :]
    if not first:
        old_ref, old_pages_ref = refs[:2]
        refs = refs[2:]
    head_dim = own_q.shape[1]
    factor = float(head_dim**-0.5 * np.log2(np.e))
    chips = seq_count // 2
    me = lax.axis_index("seq")
    core, here = me % 2, ring_place(me // 2, chips)
    lanes = lax.broadcasted_iota(jnp.int32, meta_ref.shape, 1)
    blocks, places, at = [], [], 0
    for step, count in zip(steps, layout):
        source = ring_chip((here - step + chips) % chips, chips) * 2 + core
        places.append(
            jnp.sum(jnp.where(lanes == source, meta_ref[...], 0.0), axis=1, keepdims=True)
        )
        blocks.append(chunk_rows(pieces[at : at + count]))
        at += count
    blended = jnp.concatenate(blocks, axis=0) if len(blocks) > 1 else blocks[0]
    place = jnp.concatenate(places, axis=0) if len(places) > 1 else places[0]
    queries = jnp.concatenate([own_q[...], other_q[...]], axis=0)
    flipped = blended.T

    scores = lax.dot_general(
        blended[:, :head_dim], queries, (((1,), (1,)), ((), ())), preferred_element_type=f32
    )
    scores = jnp.where(place <= limit_ref[...], scores, MASKED)
    peak = jnp.max(scores, axis=0, keepdims=True)
    if first:
        new_peak = jnp.maximum(peak, LOWEST)
    else:
        old_peak = old_ref[head_dim : head_dim + 1, :]
        new_peak = jnp.maximum(peak, old_peak)
        fade = jnp.exp2((old_peak - new_peak) * factor)
    weights = jnp.exp2((scores - new_peak) * factor)
    total = jnp.sum(weights, axis=0, keepdims=True)
    mixed = jnp.dot(flipped[head_dim:, :], weights.astype(bf16), preferred_element_type=f32)
    chosen = jnp.where(place == wanted_ref[...], 1.0, 0.0).astype(bf16)
    picked = jnp.dot(flipped, chosen, preferred_element_type=f32)
    if not first:
        total = total + old_ref[head_dim + 1 : head_dim + 2, :] * fade
        mixed = mixed + old_ref[:head_dim, :] * fade
        picked = picked + old_pages_ref[...].astype(f32)
    picked = picked.astype(bf16)
    count = mixed.shape[1]
    tail = jnp.concatenate([new_peak, total, jnp.zeros((6, count), f32)], axis=0)
    if not last:
        new_ref, new_pages_ref = refs
        new_ref[:head_dim, :] = mixed
        new_ref[head_dim:, :] = tail
        new_pages_ref[...] = picked
    else:
        mine_ref, my_pages_ref, theirs_ref, their_pages_ref = refs
        half = count // 2
        mine_ref[:head_dim, :] = mixed[:, :half]
        mine_ref[head_dim:, :] = tail[:, :half]
        theirs_ref[:head_dim, :] = pltpu.roll(mixed, half, 1)[:, :half]
        theirs_ref[head_dim:, :] = pltpu.roll(tail, half, 1)[:, :half]
        wide = picked.shape[1] // 2
        my_pages_ref[...] = picked[:, :wide]
        their_pages_ref[...] = picked[:, wide:]


def join_kernel(mine_ref, my_pages_ref, got_ref, got_pages_ref, out_ref, pages_ref):
    head_dim = mine_ref.shape[0] - 8
    factor = float(head_dim**-0.5 * np.log2(np.e))
    peaks = [ref[head_dim : head_dim + 1, :] for ref in (mine_ref, got_ref)]
    top = jnp.maximum(peaks[0], peaks[1])
    fades = [jnp.exp2((peak - top) * factor) for peak in peaks]
    total = (
        mine_ref[head_dim + 1 : head_dim + 2, :] * fades[0]
        + got_ref[head_dim + 1 : head_dim + 2, :] * fades[1]
    )
    mixed = (mine_ref[:head_dim, :] * fades[0] + got_ref[:head_dim, :] * fades[1]) / total
    flat = mixed.T
    sel = out_ref.shape[0]
    for h in range(GROUP):
        out_ref[:, h * head_dim : (h + 1) * head_dim] = flat[h * sel : (h + 1) * sel, :].astype(
            bf16
        )
    pages = (my_pages_ref[...].astype(f32) + got_pages_ref[...].astype(f32)).T
    count = pages_ref.shape[0]
    pair = 2 * head_dim
    for u in range(PAGE):
        pages_ref[:, u * pair : (u + 1) * pair] = pages[u * count : (u + 1) * count, :].astype(
            bf16
        )


def shards(
    pool_kv, pool_slot, passage_order, passage_start, recompute_pos, page_table, fresh_q, fresh_kv
):
    seq_count = lax.axis_size("seq")
    chips = seq_count // 2
    me = lax.axis_index("seq")
    pages, width = pool_kv.shape
    sel = fresh_q.shape[0]
    head_dim = fresh_kv.shape[1] // 2
    tokens = pages * PAGE
    extra = round_up(-(-sel // PAGE), TILE)
    rows = pages + extra
    query_rows = sel * GROUP
    vmem = pl.BlockSpec(memory_space=pltpu.VMEM)
    smem = pl.BlockSpec(memory_space=pltpu.SMEM)
    params = pltpu.CompilerParams(vmem_limit_bytes=40 * 2**20)

    chunk, queries = pl.pallas_call(
        partial(prep_kernel, seq_count),
        out_shape=(
            jax.ShapeDtypeStruct((rows, width), bf16),
            jax.ShapeDtypeStruct((query_rows, head_dim), bf16),
        ),
        in_specs=[smem] * 3 + [vmem] * 5,
        out_specs=(vmem, vmem),
        scratch_shapes=[
            pltpu.VMEM((extra * PAGE, 2 * head_dim), f32),
            pltpu.VMEM((query_rows, head_dim), f32),
        ],
        compiler_params=params,
        name="prepare",
    )(
        pool_slot, passage_order, passage_start, jnp.asarray(frequencies(head_dim)),
        recompute_pos, pool_kv, fresh_q, fresh_kv,
    )

    passages = jnp.arange(seq_count, dtype=jnp.int32)
    spots = jnp.arange(tokens, dtype=jnp.int32)
    slots = jnp.sum(
        jnp.where(passage_order[:, None] == passages[None, :], pool_slot[None, :], 0), axis=1
    )
    replaced = jnp.any(recompute_pos[:, :, None] == spots[None, None, :], axis=1)
    natural = jnp.where(replaced, FAR, (passages[:, None] * tokens + spots[None, :]).astype(f32))
    by_slot = jnp.sum(
        jnp.where((slots[None, :] == passages[:, None])[:, :, None], natural[None], 0.0), axis=1
    )
    cached_place = by_slot.reshape(pages, seq_count, PAGE).transpose(2, 0, 1)
    fresh_place = jnp.pad(
        (recompute_pos + passages[:, None] * tokens).astype(f32),
        ((0, 0), (0, extra * PAGE - sel)),
        constant_values=FAR,
    )
    fresh_place = fresh_place.reshape(seq_count, PAGE, extra).transpose(1, 2, 0)
    meta = jnp.concatenate([cached_place, fresh_place], axis=1).reshape(PAGE * rows, seq_count)
    pair = jnp.stack([me, me ^ 1])
    limit = jnp.sum(
        jnp.where(
            pair[:, None, None] == passages[None, :, None],
            recompute_pos[None] + passages[None, :, None] * tokens,
            0,
        ),
        axis=1,
    ).astype(f32)
    limit = jnp.broadcast_to(limit[:, None, :], (2, GROUP, sel)).reshape(1, 2 * query_rows)
    page_ids = jnp.arange(pages, dtype=jnp.int32)
    request_pages = jnp.arange(page_table.shape[0], dtype=jnp.int32)
    owned = pair[:, None] * pages + page_ids[None, :]
    wanted = jnp.sum(
        jnp.where(page_table[None, None, :] == owned[:, :, None], request_pages[None, None, :], 0),
        axis=2,
    )
    wanted = wanted[:, None, :] * PAGE + jnp.arange(PAGE, dtype=jnp.int32)[None, :, None]
    wanted = wanted.astype(f32).reshape(1, 2 * tokens)

    swap = [(i, i ^ 1) for i in range(seq_count)]
    forward, backward = ring_pairs(chips, 1), ring_pairs(chips, -1)
    other_queries = lax.ppermute(queries, "seq", swap)

    state_shapes = (
        jax.ShapeDtypeStruct((head_dim + 8, 2 * query_rows), f32),
        jax.ShapeDtypeStruct((2 * head_dim, 2 * tokens), bf16),
    )
    last_shapes = (
        jax.ShapeDtypeStruct((head_dim + 8, query_rows), f32),
        jax.ShapeDtypeStruct((2 * head_dim, tokens), bf16),
    ) * 2

    def visit(state, arrivals, last=False):
        steps = [step for step, _ in arrivals]
        layout = [len(pieces) for _, pieces in arrivals]
        pieces = [piece for _, group in arrivals for piece in group]
        first = state is None
        operands = [*pieces, queries, other_queries, meta, limit, wanted]
        aliases = {}
        if not first:
            if not last:
                aliases = {len(operands): 0, len(operands) + 1: 1}
            operands += list(state)
        keys = PAGE * rows * len(steps)
        return pl.pallas_call(
            partial(visit_kernel, seq_count, steps, layout, first, last),
            out_shape=last_shapes if last else state_shapes,
            in_specs=[vmem] * len(operands),
            out_specs=(vmem,) * (4 if last else 2),
            input_output_aliases=aliases,
            compiler_params=params,
            cost_estimate=pl.CostEstimate(
                flops=4 * keys * head_dim * (2 * query_rows + 2 * tokens),
                bytes_accessed=4 * 2**20,
                transcendentals=keys * 2 * query_rows,
            ),
            name="visit",
        )(*operands)

    state = None
    ahead = behind = chunk
    arrivals = [(0, [chunk])]
    for step in range(1, chips // 2):
        ahead = lax.ppermute(ahead, "seq", forward)
        behind = lax.ppermute(behind, "seq", backward)
        state = visit(state, arrivals)
        arrivals = [(step, [ahead]), (-step, [behind])]
    cut = round_up(rows // 2, TILE)
    upper = lax.ppermute(ahead[:cut], "seq", forward)
    lower = lax.ppermute(behind[cut:], "seq", backward)
    state = visit(state, arrivals)
    mine, my_pages, theirs, their_pages = visit(state, [(chips // 2, [upper, lower])], last=True)
    got = lax.ppermute(theirs, "seq", swap)
    got_pages = lax.ppermute(their_pages, "seq", swap)
    return pl.pallas_call(
        join_kernel,
        out_shape=(
            jax.ShapeDtypeStruct((sel, GROUP * head_dim), bf16),
            jax.ShapeDtypeStruct((pages, width), bf16),
        ),
        in_specs=[vmem] * 4,
        out_specs=(vmem, vmem),
        compiler_params=params,
        name="join",
    )(mine, my_pages, got, got_pages)


def solution(mesh):
    placed = (
        P(("groups", "seq"), None),
        P("groups"),
        P("groups"),
        P("groups"),
        P("groups", None),
        P("groups"),
        P(("groups", "seq"), None),
        P(("groups", "seq"), None),
    )
    return jax.shard_map(
        shards,
        mesh=mesh,
        in_specs=placed,
        out_specs=(P(("groups", "seq"), None), P(("groups", "seq"), None)),
        check_vma=False,
    )
```

time: 125 us -> 39.9 us (0.32)
  other arithmetic: 31.6 us -> 2.26 us
  waiting for transfers between devices: 32.3 us -> 7.93 us
  between operations: 17.5 us -> 0.8 us
  local copies, waits for them, and re-layouts: 23.2 us -> 7.93 us
  Pallas kernels: 0 us -> 10.8 us
  matrix products: 6.5 us -> 0 us
  starting transfers between devices: 13.4 us -> 9.83 us
    select_n x9 -> x1, other arithmetic: 23.7 us -> 0.08 us  [shards(): jnp.where(replaced, FAR, (passages[:, None] * tokens + spots[None, :]).as...]
    all_gather x1 -> x0, waiting for transfers between devices: 22.2 us -> none  [shards(): piece = lax.all_gather(flat_rows, 'seq', axis=0, tiled=True)]
    all_to_all x2 -> x0, starting transfers between devices: 13.4 us -> none  [the longest x1 7.36 us: shards(): lax.all_to_all(outgoing, 'seq', split_axis=0, concat_axis=0, tiled=True)]
    scatter x6 -> x0, local copies, waits for them, and re-layouts: 10.9 us -> none  [the longest x1 6.18 us: shards(): page_source = jnp.zeros((total_pages,), jnp.int32).at[page_table].set(jnp...]
    pallas_call x0 -> x7, Pallas kernels: none -> 10.8 us  [the longest x5 8.88 us: visit(): pl.pallas_call(partial(visit_kernel, seq_count, steps, layout, first, las...]
    all_to_all x2 -> x0, waiting for transfers between devices: 10.1 us -> none  [the longest x1 10.1 us: shards(): lax.all_to_all(outgoing_pages, 'seq', split_axis=0, concat_axis=0, tiled=...]
    ppermute x0 -> x11, starting transfers between devices: none -> 9.83 us  [the longest x3 6.41 us: shards(): ahead = lax.ppermute(ahead, 'seq', forward)]
    ppermute x0 -> x11, waiting for transfers between devices: none -> 7.93 us  [the longest x3 6.58 us: shards(): ahead = lax.ppermute(ahead, 'seq', forward)]
  transfers between devices with their start and end apart: 3 -> 11, of which waited for: 2 -> 4; matrix products, arithmetic and copies ran while one was open for 16% -> 11% of each run, Pallas kernels for 0% -> 20%
where the time goes in v1:
time: 39.9 us; the launch traced here: 39.6 us
  Pallas kernels  10.8 us (27%)
  starting transfers between devices  9.83 us (25%)
  local copies, waits for them, and re-layouts  7.93 us (20%)
  waiting for transfers between devices  7.93 us (20%)
  other arithmetic  2.26 us (6%)
  between operations  0.8 us (2%)
    pallas_call x5, Pallas kernels, visit(): pl.pallas_call(partial(visit_kernel, seq_count, steps, layout, first, las...  8.88 us
    ppermute x3, waiting for transfers between devices, shards(): ahead = lax.ppermute(ahead, 'seq', forward)  6.58 us
    ppermute x3, starting transfers between devices, shards(): ahead = lax.ppermute(ahead, 'seq', forward)  6.41 us
    unnamed x18, local copies, waits for them, and re-layouts  5.88 us
    ppermute x1, starting transfers between devices, shards(): upper = lax.ppermute(ahead[:cut], 'seq', forward)  1.88 us
    ppermute x1, waiting for transfers between devices, shards(): got_pages = lax.ppermute(their_pages, 'seq', swap)  1.33 us
    pallas_call x1, Pallas kernels, shards(): pl.pallas_call(partial(prep_kernel, seq_count), out_shape=(jax.ShapeDtype...  1.09 us
    pallas_call x1, Pallas kernels, shards(): pl.pallas_call(join_kernel, out_shape=(jax.ShapeDtypeStruct((sel, GROUP *...  0.87 us
  transfers between devices with their start and end apart: 11, of which 4 were waited for; matrix products, arithmetic and copies ran while one was open for 11% of the time, Pallas kernels for 20%

profile of v1, /device:TPU:0, one launch (start us, length us, event | category | flops | bytes accessed | tf_op | source)
XLA Modules:
  0.0 39.6 jit_solution(16210431533087824860)
XLA Ops:
  0.6 0.9 %copy-done = bf16[96,1024]{1,0:T(8,128)(2,1)S(1)} copy-done((bf16[96,1024]{1,0:T(8,128)(2,1)S(1)}, bf16[96,1024]{1,0:T(8,128)(2,1)}, u32[]{:S(2)}) %copy-start) | copy-done | bytes 196632
  1.6 0.9 %copy-done.1 = bf16[56,1024]{1,0:T(8,128)(2,1)S(1)} copy-done((bf16[56,1024]{1,0:T(8,128)(2,1)S(1)}, bf16[56,1024]{1,0:T(8,128)(2,1)}, u32[]{:S(2)}) %copy-start.1) | copy-done | bytes 114712
  2.5 0.7 %copy-done.2 = s32[16,56]{1,0:T(8,128)S(1)} copy-done((s32[16,56]{1,0:T(8,128)S(1)}, s32[16,56]{1,0:T(8,128)}, u32[]{:S(2)}) %copy-start.2) | copy-done | bytes 3608
  3.2 0.7 %copy-done.3 = bf16[56,256]{1,0:T(8,128)(2,1)S(1)} copy-done((bf16[56,256]{1,0:T(8,128)(2,1)S(1)}, bf16[56,256]{1,0:T(8,128)(2,1)}, u32[]{:S(2)}) %copy-start.3) | copy-done | bytes 28696
  3.9 0.7 %copy-done.4 = s32[16]{0:T(128)S(1)} copy-done((s32[16]{0:T(128)S(1)}, s32[16]{0:T(128)}, u32[]{:S(2)}) %copy-start.4) | copy-done | bytes 88
  4.6 0.7 %copy-done.5 = s32[16]{0:T(128)S(1)} copy-done((s32[16]{0:T(128)S(1)}, s32[16]{0:T(128)}, u32[]{:S(2)}) %copy-start.5) | copy-done | bytes 88
  5.2 0.7 %copy-done.6 = s32[16]{0:T(128)S(1)} copy-done((s32[16]{0:T(128)S(1)}, s32[16]{0:T(128)}, u32[]{:S(2)}) %copy-start.6) | copy-done | bytes 88
  5.9 0.7 %copy-done.7 = f32[1,128]{1,0:T(1,128)S(1)} copy-done((f32[1,128]{1,0:T(1,128)S(1)}, f32[1,128]{1,0:T(1,128)}, u32[]{:S(2)}) %copy-start.7) | copy-done | bytes 536
  6.5 1.1 %prepare.1 = (bf16[112,1024]{1,0:T(8,128)(2,1)S(1)}, bf16[448,128]{1,0:T(8,128)(2,1)S(1)}) custom-call(s32[16]{0:T(128)S(1)} %copy-done.5, s32[16]{0:T(128)S(1)} %copy-done.6, s32[16]{0:T(128)S(1)} %copy-done.4, f32[1,128]{1,0:T(1,128)S(1)} %copy-done.7, s32[16,56]{1,0:T(8,128)S(1)} %copy-done.2, bf16[96,1024]{1,0:T(8,128)(2,1)S(1)} %copy-done, ...), custom_call_target="tpu_custom_call" | custom-call | tf_op jit(solution)/shard_map/prepare/pallas_call | solution.py:225
  7.6 3.1 %collective-permute-start = (bf16[112,1024]{1,0:T(8,128)(2,1)S(1)}, bf16[112,1024]{1,0:T(8,128)(2,1)S(1)}, u32[]{:S(2)}, u32[]{:S(2)}) collective-permute-start(bf16[112,1024]{1,0:T(8,128)(2,1)S(1)} %get-tuple-element.16.refs_0_), channel_id=1, source_target_pairs={{0,4},{1,5},{4,8},{5,9},{8,12},{9,13},{12,14},{13,15},{14,10},{15,... | collective-permute-start | bytes 688136 | tf_op jit(solution)/shard_map/ppermute | solution.py:326
  10.7 0.4 fusion
  11.3 0.8 %fusion.1 = (f32[16,56]{1,0:T(8,128)S(1)}, s32[16,56]{1,0:T(8,128)S(1)}) fusion(s32[16,56]{1,0:T(8,128)} %picked_ref.1, s32[16]{0:T(128)S(1)} %iota_multiply_fusion), kind=kLoop, calls=%fused_computation.18 | loop fusion | flops 1792 | bytes 10816 | tf_op jit(solution)/shard_map/convert_element_type | solution.py:256
  12.6 0.8 %reshape.172 = f32[96,16,4]{2,1,0:T(8,128)S(1)} reshape(f32[16,384]{1,0:T(8,128)S(1)} %select_reduce_fusion.1) | data formatting | bytes 49152 | tf_op jit(solution)/shard_map/reshape | solution.py:254
  13.5 0.3 select_reduce_fusion
  14.0 2.2 %collective-permute-done.refs_0_ = bf16[112,1024]{1,0:T(8,128)(2,1)S(1)} collective-permute-done((bf16[112,1024]{1,0:T(8,128)(2,1)S(1)}, bf16[112,1024]{1,0:T(8,128)(2,1)S(1)}, u32[]{:S(2)}, u32[]{:S(2)}) %collective-permute-start) | collective-permute-done | bytes 229408 | tf_op jit(solution)/shard_map/ppermute | solution.py:326
  16.2 1.8 %collective-permute-start.1 = (bf16[112,1024]{1,0:T(8,128)(2,1)S(1)}, bf16[112,1024]{1,0:T(8,128)(2,1)S(1)}, u32[]{:S(2)}, u32[]{:S(2)}) collective-permute-start(bf16[112,1024]{1,0:T(8,128)(2,1)S(1)} %collective-permute-done.refs_0_), channel_id=1, source_target_pairs={{0,4},{1,5},{4,8},{5,9},{8,12},{9,13},{12,14},{13,15},{14,10},{15,... | collective-permute-start | bytes 688136 | tf_op jit(solution)/shard_map/ppermute | solution.py:326
  18.0 0.2 collective-permute-start.5
  18.4 0.8 %copy.25 = f32[4,112,16]{2,1,0:T(8,128)S(1)} copy(f32[4,112,16]{0,2,1:T(8,128)S(1)} %pad_maximum_fusion) | data formatting | bytes 57344 | tf_op jit(solution)/shard_map/concatenate | solution.py:261
  19.2 3.8 %collective-permute-done.1.refs_0_ = bf16[112,1024]{1,0:T(8,128)(2,1)S(1)} collective-permute-done((bf16[112,1024]{1,0:T(8,128)(2,1)S(1)}, bf16[112,1024]{1,0:T(8,128)(2,1)S(1)}, u32[]{:S(2)}, u32[]{:S(2)}) %collective-permute-start.1) | collective-permute-done | bytes 229408 | tf_op jit(solution)/shard_map/ppermute | solution.py:326
  23.0 1.5 %collective-permute-start.2 = (bf16[112,1024]{1,0:T(8,128)(2,1)S(1)}, bf16[112,1024]{1,0:T(8,128)(2,1)S(1)}, u32[]{:S(2)}, u32[]{:S(2)}) collective-permute-start(bf16[112,1024]{1,0:T(8,128)(2,1)S(1)} %collective-permute-done.1.refs_0_), channel_id=1, source_target_pairs={{0,4},{1,5},{4,8},{5,9},{8,12},{9,13},{12,14},{13,15},{14,10},{15,... | collective-permute-start | bytes 688136 | tf_op jit(solution)/shard_map/ppermute | solution.py:326
  24.5 0.5 %collective-permute-start.6 = (bf16[112,1024]{1,0:T(8,128)(2,1)S(1)}, bf16[112,1024]{1,0:T(8,128)(2,1)S(1)}, u32[]{:S(2)}, u32[]{:S(2)}) collective-permute-start(bf16[112,1024]{1,0:T(8,128)(2,1)S(1)} %collective-permute-done.5.refs_1_), channel_id=1, source_target_pairs={{0,2},{1,3},{4,0},{5,1},{8,4},{9,5},{12,8},{13,9},{14,12},{15,13},... | collective-permute-start | bytes 688136 | tf_op jit(solution)/shard_map/ppermute | solution.py:327
  25.1 1.1 %visit.5 = (f32[136,896]{1,0:T(8,128)S(1)}, bf16[256,768]{1,0:T(8,128)(2,1)S(1)}) custom-call(bf16[112,1024]{1,0:T(8,128)(2,1)S(1)} %get-tuple-element.16.refs_0_, bf16[448,128]{1,0:T(8,128)(2,1)S(1)} %get-tuple-element.17.refs_1_.refs_2_, bf16[448,128]{1,0:T(8,128)(2,1)S(1)} %collective-permute-done.8.refs_2_.refs_3_, f32[448,16]{1,0:T(8,128)S(1)} %bitcast.5, ...), custom_call_target="tpu_custom_call" | custom-call | flops 381681664 | bytes 4194304 | tf_op jit(solution)/shard_map/visit/pallas_call | solution.py:307
  26.3 2.2 %visit.6 = (f32[136,896]{1,0:T(8,128)S(1)}, bf16[256,768]{1,0:T(8,128)(2,1)S(1)}) custom-call(bf16[112,1024]{1,0:T(8,128)(2,1)S(1)} %collective-permute-done.refs_0_, bf16[112,1024]{1,0:T(8,128)(2,1)S(1)} %collective-permute-done.4.refs_1_, bf16[448,128]{1,0:T(8,128)(2,1)S(1)} %get-tuple-element.17.refs_1_.refs_2_, ...), custom_call_target="tpu_custom_call", output_to_operand_aliasing={{0}: (7, {}), {1}: (8, {})} | custom-call | flops 763363328 | bytes 4194304 | tf_op jit(solution)/shard_map/visit/pallas_call | solution.py:307
  28.5 0.6 %collective-permute-done.2.refs_0_ = bf16[112,1024]{1,0:T(8,128)(2,1)S(1)} collective-permute-done((bf16[112,1024]{1,0:T(8,128)(2,1)S(1)}, bf16[112,1024]{1,0:T(8,128)(2,1)S(1)}, u32[]{:S(2)}, u32[]{:S(2)}) %collective-permute-start.2) | collective-permute-done | bytes 229408 | tf_op jit(solution)/shard_map/ppermute | solution.py:326
  29.1 1.9 %collective-permute-start.3 = (bf16[64,1024]{1,0:T(8,128)(2,1)S(1)}, bf16[64,1024]{1,0:T(8,128)(2,1)S(1)}, u32[]{:S(2)}, u32[]{:S(2)}) collective-permute-start(bf16[64,1024]{1,0:T(8,128)(2,1)S(1)} %slice.8), channel_id=1, source_target_pairs={{0,4},{1,5},{4,8},{5,9},{8,12},{9,13},{12,14},{13,15},{14,10},{15,... | collective-permute-start | bytes 393224 | tf_op jit(solution)/shard_map/ppermute | solution.py:331
  31.0 0.3 collective-permute-start.7
  31.2 2.2 %visit.7 = (f32[136,896]{1,0:T(8,128)S(1)}, bf16[256,768]{1,0:T(8,128)(2,1)S(1)}) custom-call(bf16[112,1024]{1,0:T(8,128)(2,1)S(1)} %collective-permute-done.1.refs_0_, bf16[112,1024]{1,0:T(8,128)(2,1)S(1)} %collective-permute-done.5.refs_1_, bf16[448,128]{1,0:T(8,128)(2,1)S(1)} %get-tuple-element.17.refs_1_.refs_2_, ...), custom_call_target="tpu_custom_call", output_to_operand_aliasing={{0}: (7, {}), {1}: (8, {})} | custom-call | flops 763363328 | bytes 4194304 | tf_op jit(solution)/shard_map/visit/pallas_call | solution.py:307
  33.4 2.2 %visit.8 = (f32[136,896]{1,0:T(8,128)S(1)}, bf16[256,768]{1,0:T(8,128)(2,1)S(1)}) custom-call(bf16[112,1024]{1,0:T(8,128)(2,1)S(1)} %collective-permute-done.2.refs_0_, bf16[112,1024]{1,0:T(8,128)(2,1)S(1)} %collective-permute-done.6.refs_1_, bf16[448,128]{1,0:T(8,128)(2,1)S(1)} %get-tuple-element.17.refs_1_.refs_2_, ...), custom_call_target="tpu_custom_call", output_to_operand_aliasing={{0}: (7, {}), {1}: (8, {})} | custom-call | flops 763363328 | bytes 4194304 | tf_op jit(solution)/shard_map/visit/pallas_call | solution.py:307
  35.7 1.1 %visit.9 = (f32[136,448]{1,0:T(8,128)S(1)}, bf16[256,384]{1,0:T(8,128)(2,1)S(1)}, f32[136,448]{1,0:T(8,128)S(1)}, bf16[256,384]{1,0:T(8,128)(2,1)S(1)}) custom-call(bf16[64,1024]{1,0:T(8,128)(2,1)S(1)} %collective-permute-done.3.refs_0_, bf16[48,1024]{1,0:T(8,128)(2,1)S(1)} %collective-permute-done.7.refs_1_, ...), custom_call_target="tpu_custom_call" | custom-call | flops 381681664 | bytes 4194304 | tf_op jit(solution)/shard_map/visit/pallas_call | solution.py:307
  36.9 0.5 %collective-permute-start.10 = (bf16[256,384]{1,0:T(8,128)(2,1)S(1)}, bf16[256,384]{1,0:T(8,128)(2,1)S(1)}, u32[]{:S(2)}, u32[]{:S(2)}) collective-permute-start(bf16[256,384]{1,0:T(8,128)(2,1)S(1)} %get-tuple-element.29), channel_id=1, source_target_pairs={{0,1},{1,0},{2,3},{3,2},{4,5},{5,4},{6,7},{7,6},{8,9},{9,8},{10,11... | collective-permute-start | bytes 589832 | tf_op jit(solution)/shard_map/ppermute | solution.py:336
  37.4 1.3 %collective-permute-done.10.got_pages_ref = bf16[256,384]{1,0:T(8,128)(2,1)S(1)} collective-permute-done((bf16[256,384]{1,0:T(8,128)(2,1)S(1)}, bf16[256,384]{1,0:T(8,128)(2,1)S(1)}, u32[]{:S(2)}, u32[]{:S(2)}) %collective-permute-start.10) | collective-permute-done | bytes 196640 | tf_op jit(solution)/shard_map/ppermute | solution.py:336
  38.7 0.9 %join.1 = (bf16[56,1024]{1,0:T(8,128)(2,1)}, bf16[96,1024]{1,0:T(8,128)(2,1)}) custom-call(f32[136,448]{1,0:T(8,128)S(1)} %get-tuple-element.26.mine_ref, bf16[256,384]{1,0:T(8,128)(2,1)S(1)} %get-tuple-element.27.my_pages_ref, f32[136,448]{1,0:T(8,128)S(1)} %collective-permute-done.9.got_ref, bf16[256,384]{1,0:T(8,128)(2,1)S(1)} %collective-permute-done.10.got_pages_ref), custom_call_target="tpu_custom_call" | custom-call | tf_op jit(solution)/shard_map/join/pallas_call | solution.py:337
  (41 shorter events, 1.4 us)
Async XLA Ops:
  0.6 0.9 %copy-start = (bf16[96,1024]{1,0:T(8,128)(2,1)S(1)}, bf16[96,1024]{1,0:T(8,128)(2,1)}, u32[]{:S(2)}) copy-start(bf16[96,1024]{1,0:T(8,128)(2,1)} %pool_ref.1) | copy-start | bytes 589828
  1.6 0.9 %copy-start.1 = (bf16[56,1024]{1,0:T(8,128)(2,1)S(1)}, bf16[56,1024]{1,0:T(8,128)(2,1)}, u32[]{:S(2)}) copy-start(bf16[56,1024]{1,0:T(8,128)(2,1)} %q_ref.1) | copy-start | bytes 344068
  2.5 0.7 %copy-start.2 = (s32[16,56]{1,0:T(8,128)S(1)}, s32[16,56]{1,0:T(8,128)}, u32[]{:S(2)}) copy-start(s32[16,56]{1,0:T(8,128)} %picked_ref.1) | copy-start | bytes 10756
  3.2 0.7 %copy-start.3 = (bf16[56,256]{1,0:T(8,128)(2,1)S(1)}, bf16[56,256]{1,0:T(8,128)(2,1)}, u32[]{:S(2)}) copy-start(bf16[56,256]{1,0:T(8,128)(2,1)} %kv_ref.1) | copy-start | bytes 86020
  3.9 0.7 %copy-start.4 = (s32[16]{0:T(128)S(1)}, s32[16]{0:T(128)}, u32[]{:S(2)}) copy-start(s32[16]{0:T(128)} %start_ref.1) | copy-start | bytes 196
  4.6 0.7 %copy-start.5 = (s32[16]{0:T(128)S(1)}, s32[16]{0:T(128)}, u32[]{:S(2)}) copy-start(s32[16]{0:T(128)} %slot_ref.1) | copy-start | bytes 196
  5.2 0.7 %copy-start.6 = (s32[16]{0:T(128)S(1)}, s32[16]{0:T(128)}, u32[]{:S(2)}) copy-start(s32[16]{0:T(128)} %order_ref.1) | copy-start | bytes 196
  5.9 0.7 %copy-start.7 = (f32[1,128]{1,0:T(1,128)S(1)}, f32[1,128]{1,0:T(1,128)}, u32[]{:S(2)}) copy-start(f32[1,128]{1,0:T(1,128)} %constant.9.clone.freq_ref) | copy-start | bytes 1540
  6.5 7.0 %copy-start.8 = (s32[1536]{0:T(1024)S(1)}, s32[1536]{0:T(1024)}, u32[]{:S(2)}) copy-start(s32[1536]{0:T(1024)} %param.14) | copy-start | bytes 18436
  7.6 8.6 %collective-permute-start = (bf16[112,1024]{1,0:T(8,128)(2,1)S(1)}, bf16[112,1024]{1,0:T(8,128)(2,1)S(1)}, u32[]{:S(2)}, u32[]{:S(2)}) collective-permute-start(bf16[112,1024]{1,0:T(8,128)(2,1)S(1)} %get-tuple-element.16.refs_0_), channel_id=1, source_target_pairs={{0,4},{1,5},{4,8},{5,9},{8,12},{9,13},{12,14},{13,15},{14,10},{15,... | collective-permute-start | bytes 688136 | tf_op jit(solution)/shard_map/ppermute | solution.py:326
  10.7 7.3 %collective-permute-start.4 = (bf16[112,1024]{1,0:T(8,128)(2,1)S(1)}, bf16[112,1024]{1,0:T(8,128)(2,1)S(1)}, u32[]{:S(2)}, u32[]{:S(2)}) collective-permute-start(bf16[112,1024]{1,0:T(8,128)(2,1)S(1)} %get-tuple-element.16.refs_0_), channel_id=1, source_target_pairs={{0,2},{1,3},{4,0},{5,1},{8,4},{9,5},{12,8},{13,9},{14,12},{15,13},... | collective-permute-start | bytes 688136 | tf_op jit(solution)/shard_map/ppermute | solution.py:327
  10.7 14.4 %collective-permute-start.8 = (bf16[448,128]{1,0:T(8,128)(2,1)S(1)}, bf16[448,128]{1,0:T(8,128)(2,1)S(1)}, u32[]{:S(2)}, u32[]{:S(2)}) collective-permute-start(bf16[448,128]{1,0:T(8,128)(2,1)S(1)} %get-tuple-element.17.refs_1_.refs_2_), channel_id=1, source_target_pairs={{0,1},{1,0},{2,3},{3,2},{4,5},{5,4},{6,7},{7,6},{8,9},{9,8},{10,11... | collective-permute-start | bytes 344072 | tf_op jit(solution)/shard_map/ppermute | solution.py:284
  16.2 6.8 %collective-permute-start.1 = (bf16[112,1024]{1,0:T(8,128)(2,1)S(1)}, bf16[112,1024]{1,0:T(8,128)(2,1)S(1)}, u32[]{:S(2)}, u32[]{:S(2)}) collective-permute-start(bf16[112,1024]{1,0:T(8,128)(2,1)S(1)} %collective-permute-done.refs_0_), channel_id=1, source_target_pairs={{0,4},{1,5},{4,8},{5,9},{8,12},{9,13},{12,14},{13,15},{14,10},{15,... | collective-permute-start | bytes 688136 | tf_op jit(solution)/shard_map/ppermute | solution.py:326
  18.0 6.5 %collective-permute-start.5 = (bf16[112,1024]{1,0:T(8,128)(2,1)S(1)}, bf16[112,1024]{1,0:T(8,128)(2,1)S(1)}, u32[]{:S(2)}, u32[]{:S(2)}) collective-permute-start(bf16[112,1024]{1,0:T(8,128)(2,1)S(1)} %collective-permute-done.4.refs_1_), channel_id=1, source_target_pairs={{0,2},{1,3},{4,0},{5,1},{8,4},{9,5},{12,8},{13,9},{14,12},{15,13},... | collective-permute-start | bytes 688136 | tf_op jit(solution)/shard_map/ppermute | solution.py:327
  23.0 6.0 %collective-permute-start.2 = (bf16[112,1024]{1,0:T(8,128)(2,1)S(1)}, bf16[112,1024]{1,0:T(8,128)(2,1)S(1)}, u32[]{:S(2)}, u32[]{:S(2)}) collective-permute-start(bf16[112,1024]{1,0:T(8,128)(2,1)S(1)} %collective-permute-done.1.refs_0_), channel_id=1, source_target_pairs={{0,4},{1,5},{4,8},{5,9},{8,12},{9,13},{12,14},{13,15},{14,10},{15,... | collective-permute-start | bytes 688136 | tf_op jit(solution)/shard_map/ppermute | solution.py:326
  24.5 6.4 %collective-permute-start.6 = (bf16[112,1024]{1,0:T(8,128)(2,1)S(1)}, bf16[112,1024]{1,0:T(8,128)(2,1)S(1)}, u32[]{:S(2)}, u32[]{:S(2)}) collective-permute-start(bf16[112,1024]{1,0:T(8,128)(2,1)S(1)} %collective-permute-done.5.refs_1_), channel_id=1, source_target_pairs={{0,2},{1,3},{4,0},{5,1},{8,4},{9,5},{12,8},{13,9},{14,12},{15,13},... | collective-permute-start | bytes 688136 | tf_op jit(solution)/shard_map/ppermute | solution.py:327
  29.1 6.6 %collective-permute-start.3 = (bf16[64,1024]{1,0:T(8,128)(2,1)S(1)}, bf16[64,1024]{1,0:T(8,128)(2,1)S(1)}, u32[]{:S(2)}, u32[]{:S(2)}) collective-permute-start(bf16[64,1024]{1,0:T(8,128)(2,1)S(1)} %slice.8), channel_id=1, source_target_pairs={{0,4},{1,5},{4,8},{5,9},{8,12},{9,13},{12,14},{13,15},{14,10},{15,... | collective-permute-start | bytes 393224 | tf_op jit(solution)/shard_map/ppermute | solution.py:331
  31.0 4.7 %collective-permute-start.7 = (bf16[48,1024]{1,0:T(8,128)(2,1)S(1)}, bf16[48,1024]{1,0:T(8,128)(2,1)S(1)}, u32[]{:S(2)}, u32[]{:S(2)}) collective-permute-start(bf16[48,1024]{1,0:T(8,128)(2,1)S(1)} %slice.9), channel_id=1, source_target_pairs={{0,2},{1,3},{4,0},{5,1},{8,4},{9,5},{12,8},{13,9},{14,12},{15,13},... | collective-permute-start | bytes 294920 | tf_op jit(solution)/shard_map/ppermute | solution.py:332
  36.8 1.9 %collective-permute-start.9 = (f32[136,448]{1,0:T(8,128)S(1)}, f32[136,448]{1,0:T(8,128)S(1)}, u32[]{:S(2)}, u32[]{:S(2)}) collective-permute-start(f32[136,448]{1,0:T(8,128)S(1)} %get-tuple-element.28), channel_id=1, source_target_pairs={{0,1},{1,0},{2,3},{3,2},{4,5},{5,4},{6,7},{7,6},{8,9},{9,8},{10,11... | collective-permute-start | bytes 731144 | tf_op jit(solution)/shard_map/ppermute | solution.py:335
  36.9 1.8 %collective-permute-start.10 = (bf16[256,384]{1,0:T(8,128)(2,1)S(1)}, bf16[256,384]{1,0:T(8,128)(2,1)S(1)}, u32[]{:S(2)}, u32[]{:S(2)}) collective-permute-start(bf16[256,384]{1,0:T(8,128)(2,1)S(1)} %get-tuple-element.29), channel_id=1, source_target_pairs={{0,1},{1,0},{2,3},{3,2},{4,5},{5,4},{6,7},{7,6},{8,9},{9,8},{10,11... | collective-permute-start | bytes 589832 | tf_op jit(solution)/shard_map/ppermute | solution.py:336

commit v2 on v1

--- a/solution.py
+++ b/solution.py
@@ -15,6 +15,9 @@
 MASKED = -1e30
 LOWEST = -1e29
 TILE = 16
+LANES = 128
+
+QUARTER = (1.5703125, 253 * 2.0**-19, 170 * 2.0**-27, float(np.pi / 2 - 1.5703125 - 253 * 2.0**-19 - 170 * 2.0**-27))
 
 f32 = jnp.float32
 bf16 = jnp.bfloat16
@@ -57,50 +60,148 @@
     return vector * cosine + pltpu.roll(vector, half, 1) * signed_sine
 
 
-def prep_kernel(
-    seq_count, slot_ref, order_ref, start_ref, freq_ref, picked_ref, pool_ref, q_ref, kv_ref,
-    chunk_ref, queries_ref, fresh_ref, heads_ref,
-):
+def cos_sin(angle):
+    turns = jnp.round(angle * float(2 / np.pi))
+    rest = angle
+    for part in QUARTER:
+        rest = rest - turns * part
+    square = rest * rest
+    sine = rest + rest * square * (
+        -1.6666654611e-1 + square * (8.3321608736e-3 - square * 1.9515295891e-4)
+    )
+    cosine = (
+        1.0
+        - 0.5 * square
+        + square
+        * square
+        * (4.166664568298827e-2 + square * (-1.388731625493765e-3 + square * 2.443315711809948e-5))
+    )
+    quadrant = turns.astype(jnp.int32) & 3
+    odd = (quadrant & 1) == 1
+    cos_value = jnp.where(odd, sine, cosine)
+    sin_value = jnp.where(odd, cosine, sine)
+    cos_value = jnp.where((quadrant == 1) | (quadrant == 2), -cos_value, cos_value)
+    sin_value = jnp.where(quadrant >= 2, -sin_value, sin_value)
+    return cos_value, sin_value
+
+
+def rotation(angle):
+    head_dim = angle.shape[1]
+    cosine, sine = cos_sin(angle)
+    lower = lax.broadcasted_iota(jnp.int32, angle.shape, 1) < head_dim // 2
+    return cosine, jnp.where(lower, -sine, sine)
+
+
+def fresh_rotation(row, start, frequency):
+    sel = row.shape[1]
+    wide = jnp.broadcast_to(row.astype(f32), (sel, sel))
+    same = lax.broadcasted_iota(jnp.int32, (sel, sel), 0) == lax.broadcasted_iota(
+        jnp.int32, (sel, sel), 1
+    )
+    picked = jnp.sum(jnp.where(same, wide, 0.0), axis=1, keepdims=True)
+    return rotation((picked + start.astype(f32)) * frequency)
+
+
+def fetch(sources, targets, sems):
+    copies = [
+        pltpu.make_async_copy(source, target, sems.at[i])
+        for i, (source, target) in enumerate(zip(sources, targets))
+    ]
+    for copy in copies:
+        copy.start()
+    return copies
+
+
+def prep_kernel(seq_count, *refs):
+    sources, (chunk_ref,), targets = refs[:7], refs[7:8], refs[8:15]
+    fresh_ref, sems = refs[15:]
+    copies = fetch(sources, targets, sems)
+    slot_ref, order_ref, start_ref, freq_ref, picked_ref, kv_ref, pool_ref = targets
     pages = pool_ref.shape[0]
     sel = kv_ref.shape[0]
     head_dim = freq_ref.shape[1]
     pair = 2 * head_dim
     extra = chunk_ref.shape[0] - pages
     me = lax.axis_index("seq")
-    sign = jnp.where(lax.broadcasted_iota(jnp.int32, (1, head_dim), 1) < head_dim // 2, -1.0, 1.0)
     spot = lax.broadcasted_iota(jnp.int32, (pages, head_dim), 0) * seq_count + me
+    for copy in copies[:-1]:
+        copy.wait()
 
     def place(k, start):
         low = slot_ref[order_ref[k]] * pages
         return jnp.where(jnp.logical_and(spot >= low, spot < low + pages), start_ref[k], start)
 
-    start = lax.fori_loop(0, seq_count, place, jnp.zeros((pages, head_dim), jnp.int32), unroll=8)
-    angle = start.astype(f32) * freq_ref[...]
-    cosine, sine = jnp.cos(angle), jnp.sin(angle) * sign
-    for u in range(PAGE):
-        keys = slice(u * pair, u * pair + head_dim)
-        values = slice(u * pair + head_dim, (u + 1) * pair)
-        chunk_ref[:pages, keys] = turned(pool_ref[:, keys].astype(f32), cosine, sine).astype(bf16)
-        chunk_ref[:pages, values] = pool_ref[:, values]
-
-    row = jnp.broadcast_to(picked_ref[pl.ds(me, 1), :].astype(f32), (sel, sel))
-    same = lax.broadcasted_iota(jnp.int32, (sel, sel), 0) == lax.broadcasted_iota(
-        jnp.int32, (sel, sel), 1
-    )
-    picked = jnp.sum(jnp.where(same, row, 0.0), axis=1, keepdims=True)
-    angle = (picked + start_ref[me].astype(f32)) * freq_ref[...]
-    cosine, sine = jnp.cos(angle), jnp.sin(angle) * sign
-    fresh_ref[...] = jnp.zeros_like(fresh_ref)
+    start = lax.fori_loop(0, seq_count, place, jnp.zeros((pages, head_dim), jnp.int32), unroll=16)
+    cosine, sine = fresh_rotation(picked_ref[pl.ds(me, 1), :], start_ref[me], freq_ref[...])
+    fresh_ref[sel:, :] = jnp.zeros((fresh_ref.shape[0] - sel, pair), f32)
     fresh_ref[:sel, :head_dim] = turned(kv_ref[:, :head_dim].astype(f32), cosine, sine)
     fresh_ref[:sel, head_dim:] = kv_ref[:, head_dim:].astype(f32)
     for u in range(PAGE):
         chunk_ref[pages:, u * pair : (u + 1) * pair] = fresh_ref[
             u * extra : (u + 1) * extra, :
         ].astype(bf16)
+
+    cosine, sine = rotation(start.astype(f32) * freq_ref[...])
+    copies[-1].wait()
+    for u in range(PAGE):
+        keys = slice(u * pair, u * pair + head_dim)
+        values = slice(u * pair + head_dim, (u + 1) * pair)
+        chunk_ref[:pages, keys] = turned(pool_ref[:, keys].astype(f32), cosine, sine).astype(bf16)
+        chunk_ref[:pages, values] = pool_ref[:, values]
+
+
+def plan_kernel(seq_count, tokens, *refs):
+    sources, (queries_ref, facts_ref), targets = refs[:6], refs[6:8], refs[8:14]
+    heads_ref, sems = refs[14:]
+    for copy in fetch(sources, targets, sems):
+        copy.wait()
+    slot_ref, order_ref, start_ref, freq_ref, picked_ref, q_ref = targets
+    me = lax.axis_index("seq")
+    sel = q_ref.shape[0]
+    head_dim = freq_ref.shape[1]
+
+    row = picked_ref[pl.ds(me, 1), :]
+    cosine, sine = fresh_rotation(row, start_ref[me], freq_ref[...])
     for h in range(GROUP):
         head = q_ref[:, h * head_dim : (h + 1) * head_dim].astype(f32)
         heads_ref[h * sel : (h + 1) * sel, :] = turned(head, cosine, sine)
     queries_ref[...] = heads_ref[...].astype(bf16)
+
+    other = me + 1 - 2 * (me % 2)
+    ours = (row + me * tokens).astype(f32)
+    theirs = (picked_ref[pl.ds(other, 1), :] + other * tokens).astype(f32)
+    both = jnp.concatenate([ours] * GROUP + [theirs] * GROUP, axis=1)
+    at = put_rows(facts_ref, seq_count, both)
+
+    shape = (seq_count, facts_ref.shape[1])
+    lanes = lax.broadcasted_iota(jnp.int32, shape, 1)
+    passages = lax.broadcasted_iota(jnp.int32, shape, 0)
+    begin = ((passages + 1) * tokens).astype(f32)
+    facts_ref[:seq_count, :] = jnp.where(lanes == shape[1] - 1, begin, FAR)
+    facts_ref[:seq_count, :sel] = picked_ref[...].astype(f32)
+
+    lanes = lax.broadcasted_iota(jnp.int32, (1, round_up(seq_count, shape[1])), 1)
+
+    def slot(k, row):
+        return jnp.where(lanes == k, slot_ref[order_ref[k]], row)
+
+    slots = lax.fori_loop(0, seq_count, slot, jnp.zeros(lanes.shape, jnp.int32), unroll=16)
+    put_rows(facts_ref, at, slots.astype(f32))
+
+
+def put_rows(ref, at, row):
+    width = ref.shape[1]
+    for i in range(row.shape[1] // width):
+        ref[at + i : at + i + 1, :] = row[:, i * width : (i + 1) * width]
+    return at + row.shape[1] // width
+
+
+def get_rows(ref, at, count):
+    return jnp.concatenate([ref[at + i : at + i + 1, :] for i in range(count)], axis=1)
+
+
+def fact_rows(seq_count, query_rows, width):
+    return seq_count, 2 * query_rows // width, round_up(seq_count, width) // width
 
 
 def chunk_rows(pieces):
@@ -112,28 +213,65 @@
     return jnp.concatenate(parts, axis=0)
 
 
-def visit_kernel(seq_count, steps, layout, first, last, *refs):
+def chunk_places(source, facts_ref, slots, rows, tokens, shared):
+    seq_count, width = slots.shape[1], facts_ref.shape[1]
+    pages = tokens // PAGE
+    extra = rows - pages
+    if shared is None:
+        spot = lax.broadcasted_iota(jnp.int32, (pages, seq_count), 0) * seq_count + source
+        low = slots * pages
+        held = jnp.where(jnp.logical_and(spot >= low, spot < low + pages), 1.0, 0.0)
+        shared = jnp.dot(
+            held, facts_ref[:seq_count, :], precision=lax.Precision.HIGHEST, preferred_element_type=f32
+        )
+    spot = lax.broadcasted_iota(jnp.int32, (pages, 1), 0) * seq_count + source
+    spot = spot.astype(f32)
+    page = spot - pages * jnp.floor((spot + 0.5) * (1.0 / pages))
+    begin = shared[:, width - 1 :] - tokens + page * PAGE
+    holder = jnp.floor(shared * (1.0 / PAGE))
+    bits = jnp.where(holder == page, jnp.exp2(shared - PAGE * holder), 0.0)
+    bits = jnp.sum(bits, axis=1, keepdims=True).astype(jnp.int32)
+    row = jnp.broadcast_to(facts_ref[pl.ds(source, 1), :], (extra * PAGE, width))
+    same = lax.broadcasted_iota(jnp.int32, row.shape, 0) == lax.broadcasted_iota(
+        jnp.int32, row.shape, 1
+    )
+    fresh = jnp.sum(jnp.where(same, row, 0.0), axis=1, keepdims=True)
+    fresh = fresh + (source * tokens).astype(f32)
+    parts = []
+    for u in range(PAGE):
+        parts.append(jnp.where(((bits >> u) & 1) == 1, FAR, begin + u))
+        parts.append(fresh[u * extra : (u + 1) * extra, :])
+    return jnp.concatenate(parts, axis=0), shared
+
+
+def visit_kernel(seq_count, tokens, steps, layout, first, last, *refs):
     piece_count = sum(layout)
     pieces = refs[:piece_count]
-    own_q, other_q, meta_ref, limit_ref, wanted_ref = refs[piece_count : piece_count + 5]
-    refs = refs[piece_count + 5 :]
+    own_q, other_q, facts_ref, wanted_ref = refs[piece_count : piece_count + 4]
+    refs = refs[piece_count + 4 :]
     if not first:
         old_ref, old_pages_ref = refs[:2]
         refs = refs[2:]
     head_dim = own_q.shape[1]
     factor = float(head_dim**-0.5 * np.log2(np.e))
     chips = seq_count // 2
+    pages = tokens // PAGE
     me = lax.axis_index("seq")
     core, here = me % 2, ring_place(me // 2, chips)
-    lanes = lax.broadcasted_iota(jnp.int32, meta_ref.shape, 1)
-    blocks, places, at = [], [], 0
+    table_rows, limit_rows, slot_rows = fact_rows(seq_count, own_q.shape[0], facts_ref.shape[1])
+    limit = get_rows(facts_ref, table_rows, limit_rows)
+    slots = get_rows(facts_ref, table_rows + limit_rows, slot_rows)[:, :seq_count].astype(jnp.int32)
+    blocks, places, at, shared = [], [], 0, None
     for step, count in zip(steps, layout):
         source = ring_chip((here - step + chips) % chips, chips) * 2 + core
-        places.append(
-            jnp.sum(jnp.where(lanes == source, meta_ref[...], 0.0), axis=1, keepdims=True)
-        )
-        blocks.append(chunk_rows(pieces[at : at + count]))
+        group = pieces[at : at + count]
         at += count
+        rows = sum(piece.shape[0] for piece in group)
+        if pages % seq_count:
+            shared = None
+        found, shared = chunk_places(source, facts_ref, slots, rows, tokens, shared)
+        places.append(found)
+        blocks.append(chunk_rows(group))
     blended = jnp.concatenate(blocks, axis=0) if len(blocks) > 1 else blocks[0]
     place = jnp.concatenate(places, axis=0) if len(places) > 1 else places[0]
     queries = jnp.concatenate([own_q[...], other_q[...]], axis=0)
@@ -142,7 +280,7 @@
     scores = lax.dot_general(
         blended[:, :head_dim], queries, (((1,), (1,)), ((), ())), preferred_element_type=f32
     )
-    scores = jnp.where(place <= limit_ref[...], scores, MASKED)
+    scores = jnp.where(place <= limit, scores, MASKED)
     peak = jnp.max(scores, axis=0, keepdims=True)
     if first:
         new_peak = jnp.maximum(peak, LOWEST)
@@ -219,56 +357,56 @@
     rows = pages + extra
     query_rows = sel * GROUP
     vmem = pl.BlockSpec(memory_space=pltpu.VMEM)
-    smem = pl.BlockSpec(memory_space=pltpu.SMEM)
     params = pltpu.CompilerParams(vmem_limit_bytes=40 * 2**20)
 
-    chunk, queries = pl.pallas_call(
+    anywhere = pl.BlockSpec(memory_space=pltpu.HBM)
+    frequency = jnp.asarray(frequencies(head_dim))
+
+    def gathered(kernel, in_smem, in_vmem, out_shape, scratch, name):
+        operands = [
+            pltpu.with_memory_space_constraint(x, pltpu.HBM) for x in (*in_smem, *in_vmem)
+        ]
+        return pl.pallas_call(
+            kernel,
+            out_shape=out_shape,
+            in_specs=[anywhere] * len(operands),
+            out_specs=jax.tree.map(lambda _: vmem, out_shape),
+            scratch_shapes=[
+                *[pltpu.SMEM(x.shape, x.dtype) for x in in_smem],
+                *[pltpu.VMEM(x.shape, x.dtype) for x in in_vmem],
+                scratch,
+                pltpu.SemaphoreType.DMA((len(operands),)),
+            ],
+            compiler_params=params,
+            cost_estimate=pl.CostEstimate(
+                flops=10**8, bytes_accessed=6 * 2**20, transcendentals=0
+            ),
+            name=name,
+        )(*operands)
+
+    chunk = gathered(
         partial(prep_kernel, seq_count),
-        out_shape=(
-            jax.ShapeDtypeStruct((rows, width), bf16),
+        [pool_slot, passage_order, passage_start],
+        [frequency, recompute_pos, fresh_kv, pool_kv],
+        jax.ShapeDtypeStruct((rows, width), bf16),
+        pltpu.VMEM((extra * PAGE, 2 * head_dim), f32),
+        "prepare",
+    )
+    fact_width = round_up(sel + 1, LANES)
+    fact_count = sum(fact_rows(seq_count, query_rows, fact_width))
+    queries, facts = gathered(
+        partial(plan_kernel, seq_count, tokens),
+        [pool_slot, passage_order, passage_start],
+        [frequency, recompute_pos, fresh_q],
+        (
             jax.ShapeDtypeStruct((query_rows, head_dim), bf16),
+            jax.ShapeDtypeStruct((round_up(fact_count, 8), fact_width), f32),
         ),
-        in_specs=[smem] * 3 + [vmem] * 5,
-        out_specs=(vmem, vmem),
-        scratch_shapes=[
-            pltpu.VMEM((extra * PAGE, 2 * head_dim), f32),
-            pltpu.VMEM((query_rows, head_dim), f32),
-        ],
-        compiler_params=params,
-        name="prepare",
-    )(
-        pool_slot, passage_order, passage_start, jnp.asarray(frequencies(head_dim)),
-        recompute_pos, pool_kv, fresh_q, fresh_kv,
-    )
-
-    passages = jnp.arange(seq_count, dtype=jnp.int32)
-    spots = jnp.arange(tokens, dtype=jnp.int32)
-    slots = jnp.sum(
-        jnp.where(passage_order[:, None] == passages[None, :], pool_slot[None, :], 0), axis=1
-    )
-    replaced = jnp.any(recompute_pos[:, :, None] == spots[None, None, :], axis=1)
-    natural = jnp.where(replaced, FAR, (passages[:, None] * tokens + spots[None, :]).astype(f32))
-    by_slot = jnp.sum(
-        jnp.where((slots[None, :] == passages[:, None])[:, :, None], natural[None], 0.0), axis=1
-    )
-    cached_place = by_slot.reshape(pages, seq_count, PAGE).transpose(2, 0, 1)
-    fresh_place = jnp.pad(
-        (recompute_pos + passages[:, None] * tokens).astype(f32),
-        ((0, 0), (0, extra * PAGE - sel)),
-        constant_values=FAR,
-    )
-    fresh_place = fresh_place.reshape(seq_count, PAGE, extra).transpose(1, 2, 0)
-    meta = jnp.concatenate([cached_place, fresh_place], axis=1).reshape(PAGE * rows, seq_count)
+        pltpu.VMEM((query_rows, head_dim), f32),
+        "plan",
+    )
+
     pair = jnp.stack([me, me ^ 1])
-    limit = jnp.sum(
-        jnp.where(
-            pair[:, None, None] == passages[None, :, None],
-            recompute_pos[None] + passages[None, :, None] * tokens,
-            0,
-        ),
-        axis=1,
-    ).astype(f32)
-    limit = jnp.broadcast_to(limit[:, None, :], (2, GROUP, sel)).reshape(1, 2 * query_rows)
     page_ids = jnp.arange(pages, dtype=jnp.int32)
     request_pages = jnp.arange(page_table.shape[0], dtype=jnp.int32)
     owned = pair[:, None] * pages + page_ids[None, :]
@@ -297,7 +435,7 @@
         layout = [len(pieces) for _, pieces in arrivals]
         pieces = [piece for _, group in arrivals for piece in group]
         first = state is None
-        operands = [*pieces, queries, other_queries, meta, limit, wanted]
+        operands = [*pieces, queries, other_queries, facts, wanted]
         aliases = {}
         if not first:
             if not last:
@@ -305,7 +443,7 @@
             operands += list(state)
         keys = PAGE * rows * len(steps)
         return pl.pallas_call(
-            partial(visit_kernel, seq_count, steps, layout, first, last),
+            partial(visit_kernel, seq_count, tokens, steps, layout, first, last),
             out_shape=last_shapes if last else state_shapes,
             in_specs=[vmem] * len(operands),
             out_specs=(vmem,) * (4 if last else 2),
@@ -326,6 +464,7 @@
         ahead = lax.ppermute(ahead, "seq", forward)
         behind = lax.ppermute(behind, "seq", backward)
         state = visit(state, arrivals)
+        ahead, state = lax.optimization_barrier((ahead, state))
         arrivals = [(step, [ahead]), (-step, [behind])]
     cut = round_up(rows // 2, TILE)
     upper = lax.ppermute(ahead[:cut], "seq", forward)

time: 39.9 us -> 34.3 us (0.86)
  local copies, waits for them, and re-layouts: 7.93 us -> 0.1 us
  waiting for transfers between devices: 7.93 us -> 10.1 us
  Pallas kernels: 10.8 us -> 12.8 us
  other arithmetic: 2.26 us -> 0.46 us
    unnamed x18 -> x2, local copies, waits for them, and re-layouts: 5.88 us -> 0.01 us
    ppermute x1, waiting for transfers between devices: 0.01 us -> 2.13 us  [shards(): lower = lax.ppermute(behind[cut:], 'seq', backward)]
    pallas_call x6 -> x7, Pallas kernels: 9.97 us -> 11.9 us  [the longest x5 9.52 us: visit(): pl.pallas_call(partial(visit_kernel, seq_count, tokens, steps, layout, fi...]
    reshape x4 -> x0, local copies, waits for them, and re-layouts: 1.15 us -> none  [the longest x1 0.8 us: shards(): cached_place = by_slot.reshape(pages, seq_count, PAGE).transpose(2, 0, 1)]
    concatenate x1 -> x0, local copies, waits for them, and re-layouts: 0.79 us -> none  [shards(): jnp.concatenate([cached_place, fresh_place], axis=1)]
    convert_element_type x2 -> x0, other arithmetic: 0.78 us -> none  [the longest x1 0.77 us: shards(): (recompute_pos + passages[:, None] * tokens).astype(f32)]
    ppermute x1, waiting for transfers between devices: 0.01 us -> 0.75 us  [shards(): other_queries = lax.ppermute(queries, 'seq', swap)]
    ppermute x3, waiting for transfers between devices: 6.58 us -> 5.86 us  [shards(): ahead = lax.ppermute(ahead, 'seq', forward)]
  transfers between devices with their start and end apart: 11 -> 11, of which waited for: 4 -> 6; matrix products, arithmetic and copies ran while one was open for 11% -> 2% of each run, Pallas kernels for 20% -> 27%
where the time goes in v2:
time: 34.3 us; the launch traced here: 34.1 us
  Pallas kernels  12.8 us (37%)
  waiting for transfers between devices  10.1 us (29%)
  starting transfers between devices  9.9 us (29%)
  between operations  0.74 us (2%)
  other arithmetic  0.46 us (1%)
    pallas_call x5, Pallas kernels, visit(): pl.pallas_call(partial(visit_kernel, seq_count, tokens, steps, layout, fi...  9.52 us
    ppermute x3, starting transfers between devices, shards(): ahead = lax.ppermute(ahead, 'seq', forward)  6.41 us
    ppermute x3, waiting for transfers between devices, shards(): ahead = lax.ppermute(ahead, 'seq', forward)  5.86 us
    pallas_call x2, Pallas kernels, gathered(): pl.pallas_call(kernel, out_shape=out_shape, in_specs=[anywhere] * len(ope...  2.43 us
    ppermute x1, waiting for transfers between devices, shards(): lower = lax.ppermute(behind[cut:], 'seq', backward)  2.13 us
    ppermute x1, starting transfers between devices, shards(): upper = lax.ppermute(ahead[:cut], 'seq', forward)  1.88 us
    ppermute x1, waiting for transfers between devices, shards(): got_pages = lax.ppermute(their_pages, 'seq', swap)  1.33 us
    pallas_call x1, Pallas kernels, shards(): pl.pallas_call(join_kernel, out_shape=(jax.ShapeDtypeStruct((sel, GROUP *...  0.88 us
  transfers between devices with their start and end apart: 11, of which 6 were waited for; matrix products, arithmetic and copies ran while one was open for 2% of the time, Pallas kernels for 27%

profile of v2, /device:TPU:0, one launch (start us, length us, event | category | flops | bytes accessed | tf_op | source)
XLA Modules:
  0.0 34.1 jit_solution(6272735377423904506)
XLA Ops:
  0.6 1.3 %prepare.1.refs_0_ = bf16[112,1024]{1,0:T(8,128)(2,1)S(1)} custom-call(s32[16]{0:T(128)} %refs_0_.3, s32[16]{0:T(128)} %refs_1_.3, s32[16]{0:T(128)} %refs_2_.3, f32[1,128]{1,0:T(1,128)} %constant.14.clone.refs_3_, s32[16,56]{1,0:T(8,128)} %refs_4_.3, bf16[56,256]{1,0:T(8,128)(2,1)} %refs_5_.2, bf16[96,1024]{1,0:T(8,128)(2,1)} %refs_6_.1), custom_call_target="tpu_custom_call" | custom-call | flops 100000000 | bytes 6291456 | tf_op jit(solution)/shard_map/prepare/pallas_call | solution.py:369
  1.9 3.1 %collective-permute-start = (bf16[112,1024]{1,0:T(8,128)(2,1)S(1)}, bf16[112,1024]{1,0:T(8,128)(2,1)S(1)}, u32[]{:S(2)}, u32[]{:S(2)}) collective-permute-start(bf16[112,1024]{1,0:T(8,128)(2,1)S(1)} %prepare.1.refs_0_), channel_id=1, source_target_pairs={{0,4},{1,5},{4,8},{5,9},{8,12},{9,13},{12,14},{13,15},{14,10},{15,... | collective-permute-start | bytes 688136 | tf_op jit(solution)/shard_map/ppermute | solution.py:464
  5.0 0.0 collective-permute-start.3
  5.0 1.2 %plan.1 = (bf16[448,128]{1,0:T(8,128)(2,1)S(1)}, f32[24,128]{1,0:T(8,128)S(1)}) custom-call(s32[16]{0:T(128)} %refs_0_.3, s32[16]{0:T(128)} %refs_1_.3, s32[16]{0:T(128)} %refs_2_.3, f32[1,128]{1,0:T(1,128)} %constant.14.clone.refs_3_, s32[16,56]{1,0:T(8,128)} %refs_4_.3, bf16[56,1024]{1,0:T(8,128)(2,1)} %refs_5_.3), custom_call_target="tpu_custom_call" | custom-call | flops 100000000 | bytes 6291456 | tf_op jit(solution)/shard_map/plan/pallas_call | solution.py:369
  6.2 0.1 collective-permute-start.1
  6.2 0.1 add_multiply_fusion
  6.3 0.1 iota_add_fusion
  6.4 0.3 select_reduce_fusion
  6.7 0.1 convert_element_type.14.refs_4_.refs_5_
  6.8 0.8 %collective-permute-done.1.refs_2_.refs_3_ = bf16[448,128]{1,0:T(8,128)(2,1)S(1)} collective-permute-done((bf16[448,128]{1,0:T(8,128)(2,1)S(1)}, bf16[448,128]{1,0:T(8,128)(2,1)S(1)}, u32[]{:S(2)}, u32[]{:S(2)}) %collective-permute-start.1) | collective-permute-done | bytes 114720 | tf_op jit(solution)/shard_map/ppermute | solution.py:422
  7.6 1.3 %visit.5 = (f32[136,896]{1,0:T(8,128)S(1)}, bf16[256,768]{1,0:T(8,128)(2,1)S(1)}) custom-call(bf16[112,1024]{1,0:T(8,128)(2,1)S(1)} %prepare.1.refs_0_, bf16[448,128]{1,0:T(8,128)(2,1)S(1)} %get-tuple-element.25.refs_1_.refs_2_, bf16[448,128]{1,0:T(8,128)(2,1)S(1)} %collective-permute-done.1.refs_2_.refs_3_, ...), custom_call_target="tpu_custom_call" | custom-call | flops 381681664 | bytes 4194304 | tf_op jit(solution)/shard_map/visit/pallas_call | solution.py:445
  8.9 1.6 %collective-permute-done.refs_0_ = bf16[112,1024]{1,0:T(8,128)(2,1)S(1)} collective-permute-done((bf16[112,1024]{1,0:T(8,128)(2,1)S(1)}, bf16[112,1024]{1,0:T(8,128)(2,1)S(1)}, u32[]{:S(2)}, u32[]{:S(2)}) %collective-permute-start) | collective-permute-done | bytes 229408 | tf_op jit(solution)/shard_map/ppermute | solution.py:464
  10.5 1.8 %collective-permute-start.2 = (bf16[112,1024]{1,0:T(8,128)(2,1)S(1)}, bf16[112,1024]{1,0:T(8,128)(2,1)S(1)}, u32[]{:S(2)}, u32[]{:S(2)}) collective-permute-start(bf16[112,1024]{1,0:T(8,128)(2,1)S(1)} %collective-permute-done.refs_0_), channel_id=1, source_target_pairs={{0,4},{1,5},{4,8},{5,9},{8,12},{9,13},{12,14},{13,15},{14,10},{15,... | collective-permute-start | bytes 688136 | tf_op jit(solution)/shard_map/ppermute | solution.py:464
  12.3 0.2 collective-permute-start.5
  12.5 2.3 %visit.6 = (f32[136,896]{1,0:T(8,128)S(1)}, bf16[256,768]{1,0:T(8,128)(2,1)S(1)}) custom-call(bf16[112,1024]{1,0:T(8,128)(2,1)S(1)} %collective-permute-done.refs_0_, bf16[112,1024]{1,0:T(8,128)(2,1)S(1)} %collective-permute-done.3.refs_1_, bf16[448,128]{1,0:T(8,128)(2,1)S(1)} %get-tuple-element.25.refs_1_.refs_2_, ...), custom_call_target="tpu_custom_call", output_to_operand_aliasing={{0}: (6, {}), {1}: (7, {})} | custom-call | flops 763363328 | bytes 4194304 | tf_op jit(solution)/shard_map/visit/pallas_call | solution.py:445
  14.8 2.5 %collective-permute-done.2.refs_0_ = bf16[112,1024]{1,0:T(8,128)(2,1)S(1)} collective-permute-done((bf16[112,1024]{1,0:T(8,128)(2,1)S(1)}, bf16[112,1024]{1,0:T(8,128)(2,1)S(1)}, u32[]{:S(2)}, u32[]{:S(2)}) %collective-permute-start.2) | collective-permute-done | bytes 229408 | tf_op jit(solution)/shard_map/ppermute | solution.py:464
  17.3 1.5 %collective-permute-start.4 = (bf16[112,1024]{1,0:T(8,128)(2,1)S(1)}, bf16[112,1024]{1,0:T(8,128)(2,1)S(1)}, u32[]{:S(2)}, u32[]{:S(2)}) collective-permute-start(bf16[112,1024]{1,0:T(8,128)(2,1)S(1)} %collective-permute-done.2.refs_0_), channel_id=1, source_target_pairs={{0,4},{1,5},{4,8},{5,9},{8,12},{9,13},{12,14},{13,15},{14,10},{15,... | collective-permute-start | bytes 688136 | tf_op jit(solution)/shard_map/ppermute | solution.py:464
  18.8 0.0 collective-permute-done.5.refs_1_
  18.8 0.5 %collective-permute-start.7 = (bf16[112,1024]{1,0:T(8,128)(2,1)S(1)}, bf16[112,1024]{1,0:T(8,128)(2,1)S(1)}, u32[]{:S(2)}, u32[]{:S(2)}) collective-permute-start(bf16[112,1024]{1,0:T(8,128)(2,1)S(1)} %collective-permute-done.5.refs_1_), channel_id=1, source_target_pairs={{0,2},{1,3},{4,0},{5,1},{8,4},{9,5},{12,8},{13,9},{14,12},{15,13},... | collective-permute-start | bytes 688136 | tf_op jit(solution)/shard_map/ppermute | solution.py:465
  19.3 2.3 %visit.7 = (f32[136,896]{1,0:T(8,128)S(1)}, bf16[256,768]{1,0:T(8,128)(2,1)S(1)}) custom-call(bf16[112,1024]{1,0:T(8,128)(2,1)S(1)} %collective-permute-done.2.refs_0_, bf16[112,1024]{1,0:T(8,128)(2,1)S(1)} %collective-permute-done.5.refs_1_, bf16[448,128]{1,0:T(8,128)(2,1)S(1)} %get-tuple-element.25.refs_1_.refs_2_, ...), custom_call_target="tpu_custom_call", output_to_operand_aliasing={{0}: (6, {}), {1}: (7, {})} | custom-call | flops 763363328 | bytes 4194304 | tf_op jit(solution)/shard_map/visit/pallas_call | solution.py:445
  21.6 1.8 %collective-permute-done.4.refs_0_ = bf16[112,1024]{1,0:T(8,128)(2,1)S(1)} collective-permute-done((bf16[112,1024]{1,0:T(8,128)(2,1)S(1)}, bf16[112,1024]{1,0:T(8,128)(2,1)S(1)}, u32[]{:S(2)}, u32[]{:S(2)}) %collective-permute-start.4) | collective-permute-done | bytes 229408 | tf_op jit(solution)/shard_map/ppermute | solution.py:464
  23.4 1.9 %collective-permute-start.6 = (bf16[64,1024]{1,0:T(8,128)(2,1)S(1)}, bf16[64,1024]{1,0:T(8,128)(2,1)S(1)}, u32[]{:S(2)}, u32[]{:S(2)}) collective-permute-start(bf16[64,1024]{1,0:T(8,128)(2,1)S(1)} %slice.6), channel_id=1, source_target_pairs={{0,4},{1,5},{4,8},{5,9},{8,12},{9,13},{12,14},{13,15},{14,10},{15,... | collective-permute-start | bytes 393224 | tf_op jit(solution)/shard_map/ppermute | solution.py:470
  25.3 0.0 collective-permute-done.7.refs_1_
  25.3 0.3 collective-permute-start.8
  25.5 2.3 %visit.8 = (f32[136,896]{1,0:T(8,128)S(1)}, bf16[256,768]{1,0:T(8,128)(2,1)S(1)}) custom-call(bf16[112,1024]{1,0:T(8,128)(2,1)S(1)} %collective-permute-done.4.refs_0_, bf16[112,1024]{1,0:T(8,128)(2,1)S(1)} %collective-permute-done.7.refs_1_, bf16[448,128]{1,0:T(8,128)(2,1)S(1)} %get-tuple-element.25.refs_1_.refs_2_, ...), custom_call_target="tpu_custom_call", output_to_operand_aliasing={{0}: (6, {}), {1}: (7, {})} | custom-call | flops 763363328 | bytes 4194304 | tf_op jit(solution)/shard_map/visit/pallas_call | solution.py:445
  27.8 2.1 %collective-permute-done.8.refs_1_ = bf16[48,1024]{1,0:T(8,128)(2,1)S(1)} collective-permute-done((bf16[48,1024]{1,0:T(8,128)(2,1)S(1)}, bf16[48,1024]{1,0:T(8,128)(2,1)S(1)}, u32[]{:S(2)}, u32[]{:S(2)}) %collective-permute-start.8) | collective-permute-done | bytes 98336 | tf_op jit(solution)/shard_map/ppermute | solution.py:471
  30.0 1.4 %visit.9 = (f32[136,448]{1,0:T(8,128)S(1)}, bf16[256,384]{1,0:T(8,128)(2,1)S(1)}, f32[136,448]{1,0:T(8,128)S(1)}, bf16[256,384]{1,0:T(8,128)(2,1)S(1)}) custom-call(bf16[64,1024]{1,0:T(8,128)(2,1)S(1)} %collective-permute-done.6.refs_0_, bf16[48,1024]{1,0:T(8,128)(2,1)S(1)} %collective-permute-done.8.refs_1_, ...), custom_call_target="tpu_custom_call" | custom-call | flops 381681664 | bytes 4194304 | tf_op jit(solution)/shard_map/visit/pallas_call | solution.py:445
  31.3 0.1 collective-permute-start.9
  31.4 0.5 %collective-permute-start.10 = (bf16[256,384]{1,0:T(8,128)(2,1)S(1)}, bf16[256,384]{1,0:T(8,128)(2,1)S(1)}, u32[]{:S(2)}, u32[]{:S(2)}) collective-permute-start(bf16[256,384]{1,0:T(8,128)(2,1)S(1)} %get-tuple-element.47), channel_id=1, source_target_pairs={{0,1},{1,0},{2,3},{3,2},{4,5},{5,4},{6,7},{7,6},{8,9},{9,8},{10,11... | collective-permute-start | bytes 589832 | tf_op jit(solution)/shard_map/ppermute | solution.py:475
  31.9 1.3 %collective-permute-done.10.got_pages_ref = bf16[256,384]{1,0:T(8,128)(2,1)S(1)} collective-permute-done((bf16[256,384]{1,0:T(8,128)(2,1)S(1)}, bf16[256,384]{1,0:T(8,128)(2,1)S(1)}, u32[]{:S(2)}, u32[]{:S(2)}) %collective-permute-start.10) | collective-permute-done | bytes 196640 | tf_op jit(solution)/shard_map/ppermute | solution.py:475
  33.2 0.0 collective-permute-done.9.got_ref
  33.2 0.9 %join.1 = (bf16[56,1024]{1,0:T(8,128)(2,1)}, bf16[96,1024]{1,0:T(8,128)(2,1)}) custom-call(f32[136,448]{1,0:T(8,128)S(1)} %get-tuple-element.44.mine_ref, bf16[256,384]{1,0:T(8,128)(2,1)S(1)} %get-tuple-element.45.my_pages_ref, f32[136,448]{1,0:T(8,128)S(1)} %collective-permute-done.9.got_ref, bf16[256,384]{1,0:T(8,128)(2,1)S(1)} %collective-permute-done.10.got_pages_ref), custom_call_target="tpu_custom_call" | custom-call | tf_op jit(solution)/shard_map/join/pallas_call | solution.py:476
  (8 shorter events, 0.0 us)
Async XLA Ops:
  0.6 5.8 %copy-start = (s32[1536]{0:T(1024)S(1)}, s32[1536]{0:T(1024)}, u32[]{:S(2)}) copy-start(s32[1536]{0:T(1024)} %param.14) | copy-start | bytes 18436
  1.9 8.6 %collective-permute-start = (bf16[112,1024]{1,0:T(8,128)(2,1)S(1)}, bf16[112,1024]{1,0:T(8,128)(2,1)S(1)}, u32[]{:S(2)}, u32[]{:S(2)}) collective-permute-start(bf16[112,1024]{1,0:T(8,128)(2,1)S(1)} %prepare.1.refs_0_), channel_id=1, source_target_pairs={{0,4},{1,5},{4,8},{5,9},{8,12},{9,13},{12,14},{13,15},{14,10},{15,... | collective-permute-start | bytes 688136 | tf_op jit(solution)/shard_map/ppermute | solution.py:464
  5.0 7.3 %collective-permute-start.3 = (bf16[112,1024]{1,0:T(8,128)(2,1)S(1)}, bf16[112,1024]{1,0:T(8,128)(2,1)S(1)}, u32[]{:S(2)}, u32[]{:S(2)}) collective-permute-start(bf16[112,1024]{1,0:T(8,128)(2,1)S(1)} %prepare.1.refs_0_), channel_id=1, source_target_pairs={{0,2},{1,3},{4,0},{5,1},{8,4},{9,5},{12,8},{13,9},{14,12},{15,13},... | collective-permute-start | bytes 688136 | tf_op jit(solution)/shard_map/ppermute | solution.py:465
  6.2 1.4 %collective-permute-start.1 = (bf16[448,128]{1,0:T(8,128)(2,1)S(1)}, bf16[448,128]{1,0:T(8,128)(2,1)S(1)}, u32[]{:S(2)}, u32[]{:S(2)}) collective-permute-start(bf16[448,128]{1,0:T(8,128)(2,1)S(1)} %get-tuple-element.25.refs_1_.refs_2_), channel_id=1, source_target_pairs={{0,1},{1,0},{2,3},{3,2},{4,5},{5,4},{6,7},{7,6},{8,9},{9,8},{10,11... | collective-permute-start | bytes 344072 | tf_op jit(solution)/shard_map/ppermute | solution.py:422
  10.5 6.8 %collective-permute-start.2 = (bf16[112,1024]{1,0:T(8,128)(2,1)S(1)}, bf16[112,1024]{1,0:T(8,128)(2,1)S(1)}, u32[]{:S(2)}, u32[]{:S(2)}) collective-permute-start(bf16[112,1024]{1,0:T(8,128)(2,1)S(1)} %collective-permute-done.refs_0_), channel_id=1, source_target_pairs={{0,4},{1,5},{4,8},{5,9},{8,12},{9,13},{12,14},{13,15},{14,10},{15,... | collective-permute-start | bytes 688136 | tf_op jit(solution)/shard_map/ppermute | solution.py:464
  12.3 6.5 %collective-permute-start.5 = (bf16[112,1024]{1,0:T(8,128)(2,1)S(1)}, bf16[112,1024]{1,0:T(8,128)(2,1)S(1)}, u32[]{:S(2)}, u32[]{:S(2)}) collective-permute-start(bf16[112,1024]{1,0:T(8,128)(2,1)S(1)} %collective-permute-done.3.refs_1_), channel_id=1, source_target_pairs={{0,2},{1,3},{4,0},{5,1},{8,4},{9,5},{12,8},{13,9},{14,12},{15,13},... | collective-permute-start | bytes 688136 | tf_op jit(solution)/shard_map/ppermute | solution.py:465
  17.3 6.1 %collective-permute-start.4 = (bf16[112,1024]{1,0:T(8,128)(2,1)S(1)}, bf16[112,1024]{1,0:T(8,128)(2,1)S(1)}, u32[]{:S(2)}, u32[]{:S(2)}) collective-permute-start(bf16[112,1024]{1,0:T(8,128)(2,1)S(1)} %collective-permute-done.2.refs_0_), channel_id=1, source_target_pairs={{0,4},{1,5},{4,8},{5,9},{8,12},{9,13},{12,14},{13,15},{14,10},{15,... | collective-permute-start | bytes 688136 | tf_op jit(solution)/shard_map/ppermute | solution.py:464
  18.8 6.5 %collective-permute-start.7 = (bf16[112,1024]{1,0:T(8,128)(2,1)S(1)}, bf16[112,1024]{1,0:T(8,128)(2,1)S(1)}, u32[]{:S(2)}, u32[]{:S(2)}) collective-permute-start(bf16[112,1024]{1,0:T(8,128)(2,1)S(1)} %collective-permute-done.5.refs_1_), channel_id=1, source_target_pairs={{0,2},{1,3},{4,0},{5,1},{8,4},{9,5},{12,8},{13,9},{14,12},{15,13},... | collective-permute-start | bytes 688136 | tf_op jit(solution)/shard_map/ppermute | solution.py:465
  23.4 6.6 %collective-permute-start.6 = (bf16[64,1024]{1,0:T(8,128)(2,1)S(1)}, bf16[64,1024]{1,0:T(8,128)(2,1)S(1)}, u32[]{:S(2)}, u32[]{:S(2)}) collective-permute-start(bf16[64,1024]{1,0:T(8,128)(2,1)S(1)} %slice.6), channel_id=1, source_target_pairs={{0,4},{1,5},{4,8},{5,9},{8,12},{9,13},{12,14},{13,15},{14,10},{15,... | collective-permute-start | bytes 393224 | tf_op jit(solution)/shard_map/ppermute | solution.py:470
  25.3 4.7 %collective-permute-start.8 = (bf16[48,1024]{1,0:T(8,128)(2,1)S(1)}, bf16[48,1024]{1,0:T(8,128)(2,1)S(1)}, u32[]{:S(2)}, u32[]{:S(2)}) collective-permute-start(bf16[48,1024]{1,0:T(8,128)(2,1)S(1)} %slice.8), channel_id=1, source_target_pairs={{0,2},{1,3},{4,0},{5,1},{8,4},{9,5},{12,8},{13,9},{14,12},{15,13},... | collective-permute-start | bytes 294920 | tf_op jit(solution)/shard_map/ppermute | solution.py:471
  31.3 1.9 %collective-permute-start.9 = (f32[136,448]{1,0:T(8,128)S(1)}, f32[136,448]{1,0:T(8,128)S(1)}, u32[]{:S(2)}, u32[]{:S(2)}) collective-permute-start(f32[136,448]{1,0:T(8,128)S(1)} %get-tuple-element.46), channel_id=1, source_target_pairs={{0,1},{1,0},{2,3},{3,2},{4,5},{5,4},{6,7},{7,6},{8,9},{9,8},{10,11... | collective-permute-start | bytes 731144 | tf_op jit(solution)/shard_map/ppermute | solution.py:474
  31.4 1.8 %collective-permute-start.10 = (bf16[256,384]{1,0:T(8,128)(2,1)S(1)}, bf16[256,384]{1,0:T(8,128)(2,1)S(1)}, u32[]{:S(2)}, u32[]{:S(2)}) collective-permute-start(bf16[256,384]{1,0:T(8,128)(2,1)S(1)} %get-tuple-element.47), channel_id=1, source_target_pairs={{0,1},{1,0},{2,3},{3,2},{4,5},{5,4},{6,7},{7,6},{8,9},{9,8},{10,11... | collective-permute-start | bytes 589832 | tf_op jit(solution)/shard_map/ppermute | solution.py:475

commit v3 on v2

--- a/solution.py
+++ b/solution.py
@@ -244,97 +244,134 @@
     return jnp.concatenate(parts, axis=0), shared
 
 
-def visit_kernel(seq_count, tokens, steps, layout, first, last, *refs):
-    piece_count = sum(layout)
-    pieces = refs[:piece_count]
-    own_q, other_q, facts_ref, wanted_ref = refs[piece_count : piece_count + 4]
-    refs = refs[piece_count + 4 :]
-    if not first:
-        old_ref, old_pages_ref = refs[:2]
-        refs = refs[2:]
-    head_dim = own_q.shape[1]
-    factor = float(head_dim**-0.5 * np.log2(np.e))
+def read_chunks(seq_count, tokens, arrivals, core, pieces, facts_ref, query_rows):
     chips = seq_count // 2
-    pages = tokens // PAGE
-    me = lax.axis_index("seq")
-    core, here = me % 2, ring_place(me // 2, chips)
-    table_rows, limit_rows, slot_rows = fact_rows(seq_count, own_q.shape[0], facts_ref.shape[1])
+    here = ring_place(lax.axis_index("seq") // 2, chips)
+    table_rows, limit_rows, slot_rows = fact_rows(seq_count, query_rows, facts_ref.shape[1])
     limit = get_rows(facts_ref, table_rows, limit_rows)
     slots = get_rows(facts_ref, table_rows + limit_rows, slot_rows)[:, :seq_count].astype(jnp.int32)
     blocks, places, at, shared = [], [], 0, None
-    for step, count in zip(steps, layout):
+    for step, count in arrivals:
         source = ring_chip((here - step + chips) % chips, chips) * 2 + core
         group = pieces[at : at + count]
         at += count
         rows = sum(piece.shape[0] for piece in group)
-        if pages % seq_count:
+        if (tokens // PAGE) % seq_count:
             shared = None
         found, shared = chunk_places(source, facts_ref, slots, rows, tokens, shared)
         places.append(found)
         blocks.append(chunk_rows(group))
     blended = jnp.concatenate(blocks, axis=0) if len(blocks) > 1 else blocks[0]
     place = jnp.concatenate(places, axis=0) if len(places) > 1 else places[0]
-    queries = jnp.concatenate([own_q[...], other_q[...]], axis=0)
+    return blended, place, limit
+
+
+def score_factor(head_dim):
+    return float(head_dim**-0.5 * np.log2(np.e))
+
+
+def attend(blended, place, queries, limit, wanted, old):
+    head_dim = queries.shape[1]
+    factor = score_factor(head_dim)
     flipped = blended.T
-
     scores = lax.dot_general(
         blended[:, :head_dim], queries, (((1,), (1,)), ((), ())), preferred_element_type=f32
     )
     scores = jnp.where(place <= limit, scores, MASKED)
-    peak = jnp.max(scores, axis=0, keepdims=True)
-    if first:
-        new_peak = jnp.maximum(peak, LOWEST)
-    else:
-        old_peak = old_ref[head_dim : head_dim + 1, :]
-        new_peak = jnp.maximum(peak, old_peak)
-        fade = jnp.exp2((old_peak - new_peak) * factor)
-    weights = jnp.exp2((scores - new_peak) * factor)
+    peak = jnp.maximum(jnp.max(scores, axis=0, keepdims=True), LOWEST if old is None else old[0])
+    weights = jnp.exp2((scores - peak) * factor)
     total = jnp.sum(weights, axis=0, keepdims=True)
     mixed = jnp.dot(flipped[head_dim:, :], weights.astype(bf16), preferred_element_type=f32)
-    chosen = jnp.where(place == wanted_ref[...], 1.0, 0.0).astype(bf16)
+    chosen = jnp.where(place == wanted, 1.0, 0.0).astype(bf16)
     picked = jnp.dot(flipped, chosen, preferred_element_type=f32)
+    if old is not None:
+        fade = jnp.exp2((old[0] - peak) * factor)
+        total = total + old[1] * fade
+        mixed = mixed + old[2] * fade
+        picked = picked + old[3]
+    return peak, total, mixed, picked
+
+
+def get_state(ref, pages_ref):
+    head_dim = ref.shape[0] - 8
+    peak = ref[head_dim : head_dim + 1, :]
+    total = ref[head_dim + 1 : head_dim + 2, :]
+    return peak, total, ref[:head_dim, :], pages_ref[...].astype(f32)
+
+
+def put_state(state, half, ref, pages_ref):
+    peak, total, mixed, picked = state
+    head_dim = mixed.shape[0]
+    tail = jnp.concatenate([peak, total, jnp.zeros((6, peak.shape[1]), f32)], axis=0)
+    count, wide = ref.shape[1], pages_ref.shape[1]
+    if half == 1:
+        mixed, tail = pltpu.roll(mixed, count, 1), pltpu.roll(tail, count, 1)
+        picked = picked[:, wide:]
+    ref[:head_dim, :] = mixed[:, :count]
+    ref[head_dim:, :] = tail[:, :count]
+    pages_ref[...] = picked[:, :wide].astype(bf16)
+
+
+def visit_kernel(seq_count, tokens, arrivals, first, last, *refs):
+    piece_count = sum(count for _, count in arrivals)
+    pieces = refs[:piece_count]
+    own_q, other_q, facts_ref, wanted_ref = refs[piece_count : piece_count + 4]
+    refs = refs[piece_count + 4 :]
+    old = None
     if not first:
-        total = total + old_ref[head_dim + 1 : head_dim + 2, :] * fade
-        mixed = mixed + old_ref[:head_dim, :] * fade
-        picked = picked + old_pages_ref[...].astype(f32)
-    picked = picked.astype(bf16)
-    count = mixed.shape[1]
-    tail = jnp.concatenate([new_peak, total, jnp.zeros((6, count), f32)], axis=0)
-    if not last:
-        new_ref, new_pages_ref = refs
-        new_ref[:head_dim, :] = mixed
-        new_ref[head_dim:, :] = tail
-        new_pages_ref[...] = picked
-    else:
-        mine_ref, my_pages_ref, theirs_ref, their_pages_ref = refs
-        half = count // 2
-        mine_ref[:head_dim, :] = mixed[:, :half]
-        mine_ref[head_dim:, :] = tail[:, :half]
-        theirs_ref[:head_dim, :] = pltpu.roll(mixed, half, 1)[:, :half]
-        theirs_ref[head_dim:, :] = pltpu.roll(tail, half, 1)[:, :half]
-        wide = picked.shape[1] // 2
-        my_pages_ref[...] = picked[:, :wide]
-        their_pages_ref[...] = picked[:, wide:]
-
-
-def join_kernel(mine_ref, my_pages_ref, got_ref, got_pages_ref, out_ref, pages_ref):
-    head_dim = mine_ref.shape[0] - 8
-    factor = float(head_dim**-0.5 * np.log2(np.e))
-    peaks = [ref[head_dim : head_dim + 1, :] for ref in (mine_ref, got_ref)]
-    top = jnp.maximum(peaks[0], peaks[1])
-    fades = [jnp.exp2((peak - top) * factor) for peak in peaks]
-    total = (
-        mine_ref[head_dim + 1 : head_dim + 2, :] * fades[0]
-        + got_ref[head_dim + 1 : head_dim + 2, :] * fades[1]
-    )
-    mixed = (mine_ref[:head_dim, :] * fades[0] + got_ref[:head_dim, :] * fades[1]) / total
-    flat = mixed.T
+        old = get_state(*refs[:2])
+        refs = refs[2:]
+    core = lax.axis_index("seq") % 2
+    blended, place, limit = read_chunks(
+        seq_count, tokens, arrivals, core, pieces, facts_ref, own_q.shape[0]
+    )
+    queries = jnp.concatenate([own_q[...], other_q[...]], axis=0)
+    state = attend(blended, place, queries, limit, wanted_ref[...], old)
+    put_state(state, 0, *refs[:2])
+    if last:
+        put_state(state, 1, *refs[2:])
+
+
+def merged(one, two, factor):
+    peak = jnp.maximum(one[0], two[0])
+    fades = [jnp.exp2((part[0] - peak) * factor) for part in (one, two)]
+    return [peak] + [one[i] * fades[0] + two[i] * fades[1] for i in (1, 2)] + [one[3] + two[3]]
+
+
+def close_kernel(seq_count, tokens, arrivals, *refs):
+    pieces = refs[: len(refs) - 7]
+    own_q, facts_ref, wanted_ref, mine, my_pages, new, new_pages = refs[-7:]
+    core = lax.axis_index("seq") % 2
+    query_rows = own_q.shape[0]
+    blended, place, limit = read_chunks(
+        seq_count, tokens, arrivals, core, pieces, facts_ref, query_rows
+    )
+    wanted = wanted_ref[:, :tokens]
+    old = get_state(mine, my_pages)
+    state = attend(blended, place, own_q[...], limit[:, :query_rows], wanted, old)
+    put_state(state, 0, new, new_pages)
+
+
+def finish_kernel(seq_count, tokens, arrivals, *refs):
+    pieces = refs[: len(refs) - 9]
+    own_q, facts_ref, wanted_ref, mine, my_pages, got, got_pages, out_ref, pages_ref = refs[-9:]
+    core = 1 - lax.axis_index("seq") % 2
+    query_rows, head_dim = own_q.shape
+    blended, place, limit = read_chunks(
+        seq_count, tokens, arrivals, core, pieces, facts_ref, query_rows
+    )
+    wanted = wanted_ref[:, :tokens]
+    old = merged(get_state(mine, my_pages), get_state(got, got_pages), score_factor(head_dim))
+    _, total, mixed, picked = attend(
+        blended, place, own_q[...], limit[:, :query_rows], wanted, old
+    )
+    flat = (mixed / total).T
     sel = out_ref.shape[0]
     for h in range(GROUP):
         out_ref[:, h * head_dim : (h + 1) * head_dim] = flat[h * sel : (h + 1) * sel, :].astype(
             bf16
         )
-    pages = (my_pages_ref[...].astype(f32) + got_pages_ref[...].astype(f32)).T
+    pages = picked.T
     count = pages_ref.shape[0]
     pair = 2 * head_dim
     for u in range(PAGE):
@@ -425,37 +462,45 @@
         jax.ShapeDtypeStruct((head_dim + 8, 2 * query_rows), f32),
         jax.ShapeDtypeStruct((2 * head_dim, 2 * tokens), bf16),
     )
-    last_shapes = (
+    half_shapes = (
         jax.ShapeDtypeStruct((head_dim + 8, query_rows), f32),
         jax.ShapeDtypeStruct((2 * head_dim, tokens), bf16),
-    ) * 2
-
-    def visit(state, arrivals, last=False):
-        steps = [step for step, _ in arrivals]
-        layout = [len(pieces) for _, pieces in arrivals]
-        pieces = [piece for _, group in arrivals for piece in group]
-        first = state is None
-        operands = [*pieces, queries, other_queries, facts, wanted]
-        aliases = {}
-        if not first:
-            if not last:
-                aliases = {len(operands): 0, len(operands) + 1: 1}
-            operands += list(state)
-        keys = PAGE * rows * len(steps)
+    )
+    out_shapes = (
+        jax.ShapeDtypeStruct((sel, GROUP * head_dim), bf16),
+        jax.ShapeDtypeStruct((pages, width), bf16),
+    )
+
+    def run(kernel, arrivals, operands, out_shape, name, aliases=(), weight=1):
+        layout = [(step, len(pieces)) for step, pieces in arrivals]
+        operands = [piece for _, pieces in arrivals for piece in pieces] + list(operands)
+        pairs = PAGE * rows * len(layout) * (query_rows + tokens)
         return pl.pallas_call(
-            partial(visit_kernel, seq_count, tokens, steps, layout, first, last),
-            out_shape=last_shapes if last else state_shapes,
+            partial(kernel, seq_count, tokens, layout),
+            out_shape=out_shape,
             in_specs=[vmem] * len(operands),
-            out_specs=(vmem,) * (4 if last else 2),
-            input_output_aliases=aliases,
+            out_specs=(vmem,) * len(out_shape),
+            input_output_aliases={len(operands) - 2 + i: i for i in aliases},
             compiler_params=params,
             cost_estimate=pl.CostEstimate(
-                flops=4 * keys * head_dim * (2 * query_rows + 2 * tokens),
-                bytes_accessed=4 * 2**20,
-                transcendentals=keys * 2 * query_rows,
+                flops=8 * pairs * head_dim * weight,
+                bytes_accessed=4 * 2**20 * weight,
+                transcendentals=2 * pairs * weight,
             ),
-            name="visit",
+            name=name,
         )(*operands)
+
+    def visit(state, arrivals, last=False):
+        operands = [queries, other_queries, facts, wanted]
+        first = state is None
+        kernel = lambda count, size, layout, *refs: visit_kernel(
+            count, size, layout, first, last, *refs
+        )
+        if not first:
+            operands += list(state)
+        out_shape = half_shapes * 2 if last else state_shapes
+        aliases = () if first or last else (0, 1)
+        return run(kernel, arrivals, operands, out_shape, "visit", aliases)
 
     state = None
     ahead = behind = chunk
@@ -469,21 +514,15 @@
     cut = round_up(rows // 2, TILE)
     upper = lax.ppermute(ahead[:cut], "seq", forward)
     lower = lax.ppermute(behind[cut:], "seq", backward)
-    state = visit(state, arrivals)
-    mine, my_pages, theirs, their_pages = visit(state, [(chips // 2, [upper, lower])], last=True)
+    mine, my_pages, theirs, their_pages = visit(state, arrivals, last=True)
     got = lax.ppermute(theirs, "seq", swap)
     got_pages = lax.ppermute(their_pages, "seq", swap)
-    return pl.pallas_call(
-        join_kernel,
-        out_shape=(
-            jax.ShapeDtypeStruct((sel, GROUP * head_dim), bf16),
-            jax.ShapeDtypeStruct((pages, width), bf16),
-        ),
-        in_specs=[vmem] * 4,
-        out_specs=(vmem, vmem),
-        compiler_params=params,
-        name="join",
-    )(mine, my_pages, got, got_pages)
+    farthest = [(chips // 2, [upper, lower])]
+    other_farthest = [(chips // 2, [lax.ppermute(piece, "seq", swap) for piece in (upper, lower)])]
+    operands = [queries, facts, wanted, mine, my_pages]
+    state = run(close_kernel, farthest, operands, half_shapes, "close", weight=10)
+    operands = [queries, facts, wanted, *state, got, got_pages]
+    return run(finish_kernel, other_farthest, operands, out_shapes, "finish")
 
 
 def solution(mesh):

time: 34.3 us -> 33.4 us (0.974)
  waiting for transfers between devices: 10.1 us -> 8.32 us
  starting transfers between devices: 9.9 us -> 10.4 us
  Pallas kernels: 12.8 us -> 13.2 us
    ppermute x1, waiting for transfers between devices: 1.33 us -> 0.01 us  [shards(): got_pages = lax.ppermute(their_pages, 'seq', swap)]
    ppermute x0 -> x2, starting transfers between devices: none -> 0.51 us  [shards(): lax.ppermute(piece, 'seq', swap)]
    ppermute x1, waiting for transfers between devices: 2.13 us -> 1.7 us  [shards(): lower = lax.ppermute(behind[cut:], 'seq', backward)]
    pallas_call x6, Pallas kernels: 10.4 us -> 10.8 us  [run(): pl.pallas_call(partial(kernel, seq_count, tokens, layout), out_shape=out_...]
  transfers between devices with their start and end apart: 11 -> 13, of which waited for: 6 -> 5; matrix products, arithmetic and copies ran while one was open for 2% -> 2% of each run, Pallas kernels for 27% -> 31%
where the time goes in v3:
time: 33.4 us; the launch traced here: 33.2 us
  Pallas kernels  13.2 us (40%)
  starting transfers between devices  10.4 us (31%)
  waiting for transfers between devices  8.32 us (25%)
  between operations  0.77 us (2%)
  other arithmetic  0.46 us (1%)
    pallas_call x6, Pallas kernels, run(): pl.pallas_call(partial(kernel, seq_count, tokens, layout), out_shape=out_...  10.8 us
    ppermute x3, starting transfers between devices, shards(): ahead = lax.ppermute(ahead, 'seq', forward)  6.41 us
    ppermute x3, waiting for transfers between devices, shards(): ahead = lax.ppermute(ahead, 'seq', forward)  5.85 us
    pallas_call x2, Pallas kernels, gathered(): pl.pallas_call(kernel, out_shape=out_shape, in_specs=[anywhere] * len(ope...  2.43 us
    ppermute x1, starting transfers between devices, shards(): upper = lax.ppermute(ahead[:cut], 'seq', forward)  1.88 us
    ppermute x1, waiting for transfers between devices, shards(): lower = lax.ppermute(behind[cut:], 'seq', backward)  1.7 us
    ppermute x1, waiting for transfers between devices, shards(): other_queries = lax.ppermute(queries, 'seq', swap)  0.75 us
    ppermute x3, starting transfers between devices, shards(): behind = lax.ppermute(behind, 'seq', backward)  0.72 us
  transfers between devices with their start and end apart: 13, of which 5 were waited for; matrix products, arithmetic and copies ran while one was open for 2% of the time, Pallas kernels for 31%

profile of v3, /device:TPU:0, one launch (start us, length us, event | category | flops | bytes accessed | tf_op | source)
XLA Modules:
  0.0 33.2 jit_solution(16345859958465814410)
XLA Ops:
  0.6 1.3 %prepare.1.refs_0_ = bf16[112,1024]{1,0:T(8,128)(2,1)S(1)} custom-call(s32[16]{0:T(128)} %refs_0_.3, s32[16]{0:T(128)} %refs_1_.3, s32[16]{0:T(128)} %refs_2_.3, f32[1,128]{1,0:T(1,128)} %constant.14.clone.refs_3_, s32[16,56]{1,0:T(8,128)} %refs_4_.3, bf16[56,256]{1,0:T(8,128)(2,1)} %refs_5_.2, bf16[96,1024]{1,0:T(8,128)(2,1)} %refs_6_.1), custom_call_target="tpu_custom_call" | custom-call | flops 100000000 | bytes 6291456 | tf_op jit(solution)/shard_map/prepare/pallas_call | solution.py:406
  1.9 3.1 %collective-permute-start = (bf16[112,1024]{1,0:T(8,128)(2,1)S(1)}, bf16[112,1024]{1,0:T(8,128)(2,1)S(1)}, u32[]{:S(2)}, u32[]{:S(2)}) collective-permute-start(bf16[112,1024]{1,0:T(8,128)(2,1)S(1)} %prepare.1.refs_0_), channel_id=1, source_target_pairs={{0,4},{1,5},{4,8},{5,9},{8,12},{9,13},{12,14},{13,15},{14,10},{15,... | collective-permute-start | bytes 688136 | tf_op jit(solution)/shard_map/ppermute | solution.py:509
  5.0 1.2 %plan.1 = (bf16[448,128]{1,0:T(8,128)(2,1)S(1)}, f32[24,128]{1,0:T(8,128)S(1)}) custom-call(s32[16]{0:T(128)} %refs_0_.3, s32[16]{0:T(128)} %refs_1_.3, s32[16]{0:T(128)} %refs_2_.3, f32[1,128]{1,0:T(1,128)} %constant.14.clone.refs_3_, s32[16,56]{1,0:T(8,128)} %refs_4_.3, bf16[56,1024]{1,0:T(8,128)(2,1)} %refs_5_.3), custom_call_target="tpu_custom_call" | custom-call | flops 100000000 | bytes 6291456 | tf_op jit(solution)/shard_map/plan/pallas_call | solution.py:406
  6.2 0.1 collective-permute-start.1
  6.2 0.1 add_multiply_fusion
  6.3 0.1 iota_add_fusion
  6.4 0.3 select_reduce_fusion
  6.7 0.1 convert_element_type.14.refs_4_.refs_5_
  6.8 0.8 %collective-permute-done.1.refs_2_.refs_3_ = bf16[448,128]{1,0:T(8,128)(2,1)S(1)} collective-permute-done((bf16[448,128]{1,0:T(8,128)(2,1)S(1)}, bf16[448,128]{1,0:T(8,128)(2,1)S(1)}, u32[]{:S(2)}, u32[]{:S(2)}) %collective-permute-start.1) | collective-permute-done | bytes 114720 | tf_op jit(solution)/shard_map/ppermute | solution.py:459
  7.6 1.3 %visit.4 = (f32[136,896]{1,0:T(8,128)S(1)}, bf16[256,768]{1,0:T(8,128)(2,1)S(1)}) custom-call(bf16[112,1024]{1,0:T(8,128)(2,1)S(1)} %prepare.1.refs_0_, bf16[448,128]{1,0:T(8,128)(2,1)S(1)} %get-tuple-element.25.refs_1_.refs_2_, bf16[448,128]{1,0:T(8,128)(2,1)S(1)} %collective-permute-done.1.refs_2_.refs_3_, ...), custom_call_target="tpu_custom_call" | custom-call | flops 381681664 | bytes 4194304 | tf_op jit(solution)/shard_map/visit/pallas_call | solution.py:478
  8.9 1.6 %collective-permute-done.refs_0_ = bf16[112,1024]{1,0:T(8,128)(2,1)S(1)} collective-permute-done((bf16[112,1024]{1,0:T(8,128)(2,1)S(1)}, bf16[112,1024]{1,0:T(8,128)(2,1)S(1)}, u32[]{:S(2)}, u32[]{:S(2)}) %collective-permute-start) | collective-permute-done | bytes 229408 | tf_op jit(solution)/shard_map/ppermute | solution.py:509
  10.5 1.8 %collective-permute-start.2 = (bf16[112,1024]{1,0:T(8,128)(2,1)S(1)}, bf16[112,1024]{1,0:T(8,128)(2,1)S(1)}, u32[]{:S(2)}, u32[]{:S(2)}) collective-permute-start(bf16[112,1024]{1,0:T(8,128)(2,1)S(1)} %collective-permute-done.refs_0_), channel_id=1, source_target_pairs={{0,4},{1,5},{4,8},{5,9},{8,12},{9,13},{12,14},{13,15},{14,10},{15,... | collective-permute-start | bytes 688136 | tf_op jit(solution)/shard_map/ppermute | solution.py:509
  12.3 0.0 collective-permute-done.3.refs_1_
  12.3 0.2 collective-permute-start.5
  12.5 2.3 %visit.5 = (f32[136,896]{1,0:T(8,128)S(1)}, bf16[256,768]{1,0:T(8,128)(2,1)S(1)}) custom-call(bf16[112,1024]{1,0:T(8,128)(2,1)S(1)} %collective-permute-done.refs_0_, bf16[112,1024]{1,0:T(8,128)(2,1)S(1)} %collective-permute-done.3.refs_1_, bf16[448,128]{1,0:T(8,128)(2,1)S(1)} %get-tuple-element.25.refs_1_.refs_2_, ...), custom_call_target="tpu_custom_call", output_to_operand_aliasing={{0}: (6, {}), {1}: (7, {})} | custom-call | flops 763363328 | bytes 4194304 | tf_op jit(solution)/shard_map/visit/pallas_call | solution.py:478
  14.8 2.5 %collective-permute-done.2.refs_0_ = bf16[112,1024]{1,0:T(8,128)(2,1)S(1)} collective-permute-done((bf16[112,1024]{1,0:T(8,128)(2,1)S(1)}, bf16[112,1024]{1,0:T(8,128)(2,1)S(1)}, u32[]{:S(2)}, u32[]{:S(2)}) %collective-permute-start.2) | collective-permute-done | bytes 229408 | tf_op jit(solution)/shard_map/ppermute | solution.py:509
  17.3 1.5 %collective-permute-start.4 = (bf16[112,1024]{1,0:T(8,128)(2,1)S(1)}, bf16[112,1024]{1,0:T(8,128)(2,1)S(1)}, u32[]{:S(2)}, u32[]{:S(2)}) collective-permute-start(bf16[112,1024]{1,0:T(8,128)(2,1)S(1)} %collective-permute-done.2.refs_0_), channel_id=1, source_target_pairs={{0,4},{1,5},{4,8},{5,9},{8,12},{9,13},{12,14},{13,15},{14,10},{15,... | collective-permute-start | bytes 688136 | tf_op jit(solution)/shard_map/ppermute | solution.py:509
  18.8 0.0 collective-permute-done.5.refs_1_
  18.8 0.5 %collective-permute-start.8 = (bf16[112,1024]{1,0:T(8,128)(2,1)S(1)}, bf16[112,1024]{1,0:T(8,128)(2,1)S(1)}, u32[]{:S(2)}, u32[]{:S(2)}) collective-permute-start(bf16[112,1024]{1,0:T(8,128)(2,1)S(1)} %collective-permute-done.5.refs_1_), channel_id=1, source_target_pairs={{0,2},{1,3},{4,0},{5,1},{8,4},{9,5},{12,8},{13,9},{14,12},{15,13},... | collective-permute-start | bytes 688136 | tf_op jit(solution)/shard_map/ppermute | solution.py:510
  19.3 2.3 %visit.6 = (f32[136,896]{1,0:T(8,128)S(1)}, bf16[256,768]{1,0:T(8,128)(2,1)S(1)}) custom-call(bf16[112,1024]{1,0:T(8,128)(2,1)S(1)} %collective-permute-done.2.refs_0_, bf16[112,1024]{1,0:T(8,128)(2,1)S(1)} %collective-permute-done.5.refs_1_, bf16[448,128]{1,0:T(8,128)(2,1)S(1)} %get-tuple-element.25.refs_1_.refs_2_, ...), custom_call_target="tpu_custom_call", output_to_operand_aliasing={{0}: (6, {}), {1}: (7, {})} | custom-call | flops 763363328 | bytes 4194304 | tf_op jit(solution)/shard_map/visit/pallas_call | solution.py:478
  21.6 1.8 %collective-permute-done.4.refs_0_ = bf16[112,1024]{1,0:T(8,128)(2,1)S(1)} collective-permute-done((bf16[112,1024]{1,0:T(8,128)(2,1)S(1)}, bf16[112,1024]{1,0:T(8,128)(2,1)S(1)}, u32[]{:S(2)}, u32[]{:S(2)}) %collective-permute-start.4) | collective-permute-done | bytes 229408 | tf_op jit(solution)/shard_map/ppermute | solution.py:509
  23.4 1.9 %collective-permute-start.6 = (bf16[64,1024]{1,0:T(8,128)(2,1)S(1)}, bf16[64,1024]{1,0:T(8,128)(2,1)S(1)}, u32[]{:S(2)}, u32[]{:S(2)}) collective-permute-start(bf16[64,1024]{1,0:T(8,128)(2,1)S(1)} %slice.6), channel_id=1, source_target_pairs={{0,4},{1,5},{4,8},{5,9},{8,12},{9,13},{12,14},{13,15},{14,10},{15,... | collective-permute-start | bytes 393224 | tf_op jit(solution)/shard_map/ppermute | solution.py:515
  25.3 0.0 collective-permute-done.8.refs_1_
  25.3 0.3 collective-permute-start.9
  25.5 2.1 %visit.7 = (f32[136,448]{1,0:T(8,128)S(1)}, bf16[256,384]{1,0:T(8,128)(2,1)S(1)}, f32[136,448]{1,0:T(8,128)S(1)}, bf16[256,384]{1,0:T(8,128)(2,1)S(1)}) custom-call(bf16[112,1024]{1,0:T(8,128)(2,1)S(1)} %collective-permute-done.4.refs_0_, bf16[112,1024]{1,0:T(8,128)(2,1)S(1)} %collective-permute-done.8.refs_1_, ...), custom_call_target="tpu_custom_call" | custom-call | flops 763363328 | bytes 4194304 | tf_op jit(solution)/shard_map/visit/pallas_call | solution.py:478
  27.7 0.1 collective-permute-start.11
  27.8 0.5 %collective-permute-start.12 = (bf16[256,384]{1,0:T(8,128)(2,1)S(1)}, bf16[256,384]{1,0:T(8,128)(2,1)S(1)}, u32[]{:S(2)}, u32[]{:S(2)}) collective-permute-start(bf16[256,384]{1,0:T(8,128)(2,1)S(1)} %get-tuple-element.47), channel_id=1, source_target_pairs={{0,1},{1,0},{2,3},{3,2},{4,5},{5,4},{6,7},{7,6},{8,9},{9,8},{10,11... | collective-permute-start | bytes 589832 | tf_op jit(solution)/shard_map/ppermute | solution.py:519
  28.3 1.7 %collective-permute-done.9.refs_1_ = bf16[48,1024]{1,0:T(8,128)(2,1)S(1)} collective-permute-done((bf16[48,1024]{1,0:T(8,128)(2,1)S(1)}, bf16[48,1024]{1,0:T(8,128)(2,1)S(1)}, u32[]{:S(2)}, u32[]{:S(2)}) %collective-permute-start.9) | collective-permute-done | bytes 98336 | tf_op jit(solution)/shard_map/ppermute | solution.py:516
  30.0 0.0 collective-permute-start.10
  30.0 0.5 %collective-permute-start.7 = (bf16[64,1024]{1,0:T(8,128)(2,1)S(1)}, bf16[64,1024]{1,0:T(8,128)(2,1)S(1)}, u32[]{:S(2)}, u32[]{:S(2)}) collective-permute-start(bf16[64,1024]{1,0:T(8,128)(2,1)S(1)} %collective-permute-done.6.refs_0_), channel_id=1, source_target_pairs={{0,1},{1,0},{2,3},{3,2},{4,5},{5,4},{6,7},{7,6},{8,9},{9,8},{10,11... | collective-permute-start | bytes 393224 | tf_op jit(solution)/shard_map/ppermute | solution.py:521
  30.5 1.0 %close.1 = (f32[136,448]{1,0:T(8,128)S(1)}, bf16[256,384]{1,0:T(8,128)(2,1)S(1)}) custom-call(bf16[64,1024]{1,0:T(8,128)(2,1)S(1)} %collective-permute-done.6.refs_0_, bf16[48,1024]{1,0:T(8,128)(2,1)S(1)} %collective-permute-done.9.refs_1_, bf16[448,128]{1,0:T(8,128)(2,1)S(1)} %get-tuple-element.25.refs_1_.refs_2_, ...), custom_call_target="tpu_custom_call" | custom-call | flops 3816816640 | bytes 41943040 | tf_op jit(solution)/shard_map/close/pallas_call | solution.py:478
  31.5 1.7 %finish.1 = (bf16[56,1024]{1,0:T(8,128)(2,1)}, bf16[96,1024]{1,0:T(8,128)(2,1)}) custom-call(bf16[64,1024]{1,0:T(8,128)(2,1)S(1)} %collective-permute-done.7.refs_0_, bf16[48,1024]{1,0:T(8,128)(2,1)S(1)} %collective-permute-done.10.refs_1_, bf16[448,128]{1,0:T(8,128)(2,1)S(1)} %get-tuple-element.25.refs_1_.refs_2_, ...), custom_call_target="tpu_custom_call" | custom-call | flops 381681664 | bytes 4194304 | tf_op jit(solution)/shard_map/finish/pallas_call | solution.py:478
  (12 shorter events, 0.0 us)
Async XLA Ops:
  0.6 5.8 %copy-start = (s32[1536]{0:T(1024)S(1)}, s32[1536]{0:T(1024)}, u32[]{:S(2)}) copy-start(s32[1536]{0:T(1024)} %param.14) | copy-start | bytes 18436
  1.9 8.6 %collective-permute-start = (bf16[112,1024]{1,0:T(8,128)(2,1)S(1)}, bf16[112,1024]{1,0:T(8,128)(2,1)S(1)}, u32[]{:S(2)}, u32[]{:S(2)}) collective-permute-start(bf16[112,1024]{1,0:T(8,128)(2,1)S(1)} %prepare.1.refs_0_), channel_id=1, source_target_pairs={{0,4},{1,5},{4,8},{5,9},{8,12},{9,13},{12,14},{13,15},{14,10},{15,... | collective-permute-start | bytes 688136 | tf_op jit(solution)/shard_map/ppermute | solution.py:509
  5.0 7.3 %collective-permute-start.3 = (bf16[112,1024]{1,0:T(8,128)(2,1)S(1)}, bf16[112,1024]{1,0:T(8,128)(2,1)S(1)}, u32[]{:S(2)}, u32[]{:S(2)}) collective-permute-start(bf16[112,1024]{1,0:T(8,128)(2,1)S(1)} %prepare.1.refs_0_), channel_id=1, source_target_pairs={{0,2},{1,3},{4,0},{5,1},{8,4},{9,5},{12,8},{13,9},{14,12},{15,13},... | collective-permute-start | bytes 688136 | tf_op jit(solution)/shard_map/ppermute | solution.py:510
  6.2 1.4 %collective-permute-start.1 = (bf16[448,128]{1,0:T(8,128)(2,1)S(1)}, bf16[448,128]{1,0:T(8,128)(2,1)S(1)}, u32[]{:S(2)}, u32[]{:S(2)}) collective-permute-start(bf16[448,128]{1,0:T(8,128)(2,1)S(1)} %get-tuple-element.25.refs_1_.refs_2_), channel_id=1, source_target_pairs={{0,1},{1,0},{2,3},{3,2},{4,5},{5,4},{6,7},{7,6},{8,9},{9,8},{10,11... | collective-permute-start | bytes 344072 | tf_op jit(solution)/shard_map/ppermute | solution.py:459
  10.5 6.8 %collective-permute-start.2 = (bf16[112,1024]{1,0:T(8,128)(2,1)S(1)}, bf16[112,1024]{1,0:T(8,128)(2,1)S(1)}, u32[]{:S(2)}, u32[]{:S(2)}) collective-permute-start(bf16[112,1024]{1,0:T(8,128)(2,1)S(1)} %collective-permute-done.refs_0_), channel_id=1, source_target_pairs={{0,4},{1,5},{4,8},{5,9},{8,12},{9,13},{12,14},{13,15},{14,10},{15,... | collective-permute-start | bytes 688136 | tf_op jit(solution)/shard_map/ppermute | solution.py:509
  12.3 6.5 %collective-permute-start.5 = (bf16[112,1024]{1,0:T(8,128)(2,1)S(1)}, bf16[112,1024]{1,0:T(8,128)(2,1)S(1)}, u32[]{:S(2)}, u32[]{:S(2)}) collective-permute-start(bf16[112,1024]{1,0:T(8,128)(2,1)S(1)} %collective-permute-done.3.refs_1_), channel_id=1, source_target_pairs={{0,2},{1,3},{4,0},{5,1},{8,4},{9,5},{12,8},{13,9},{14,12},{15,13},... | collective-permute-start | bytes 688136 | tf_op jit(solution)/shard_map/ppermute | solution.py:510
  17.3 6.1 %collective-permute-start.4 = (bf16[112,1024]{1,0:T(8,128)(2,1)S(1)}, bf16[112,1024]{1,0:T(8,128)(2,1)S(1)}, u32[]{:S(2)}, u32[]{:S(2)}) collective-permute-start(bf16[112,1024]{1,0:T(8,128)(2,1)S(1)} %collective-permute-done.2.refs_0_), channel_id=1, source_target_pairs={{0,4},{1,5},{4,8},{5,9},{8,12},{9,13},{12,14},{13,15},{14,10},{15,... | collective-permute-start | bytes 688136 | tf_op jit(solution)/shard_map/ppermute | solution.py:509
  18.8 6.5 %collective-permute-start.8 = (bf16[112,1024]{1,0:T(8,128)(2,1)S(1)}, bf16[112,1024]{1,0:T(8,128)(2,1)S(1)}, u32[]{:S(2)}, u32[]{:S(2)}) collective-permute-start(bf16[112,1024]{1,0:T(8,128)(2,1)S(1)} %collective-permute-done.5.refs_1_), channel_id=1, source_target_pairs={{0,2},{1,3},{4,0},{5,1},{8,4},{9,5},{12,8},{13,9},{14,12},{15,13},... | collective-permute-start | bytes 688136 | tf_op jit(solution)/shard_map/ppermute | solution.py:510
  23.4 6.6 %collective-permute-start.6 = (bf16[64,1024]{1,0:T(8,128)(2,1)S(1)}, bf16[64,1024]{1,0:T(8,128)(2,1)S(1)}, u32[]{:S(2)}, u32[]{:S(2)}) collective-permute-start(bf16[64,1024]{1,0:T(8,128)(2,1)S(1)} %slice.6), channel_id=1, source_target_pairs={{0,4},{1,5},{4,8},{5,9},{8,12},{9,13},{12,14},{13,15},{14,10},{15,... | collective-permute-start | bytes 393224 | tf_op jit(solution)/shard_map/ppermute | solution.py:515
  25.3 4.7 %collective-permute-start.9 = (bf16[48,1024]{1,0:T(8,128)(2,1)S(1)}, bf16[48,1024]{1,0:T(8,128)(2,1)S(1)}, u32[]{:S(2)}, u32[]{:S(2)}) collective-permute-start(bf16[48,1024]{1,0:T(8,128)(2,1)S(1)} %slice.8), channel_id=1, source_target_pairs={{0,2},{1,3},{4,0},{5,1},{8,4},{9,5},{12,8},{13,9},{14,12},{15,13},... | collective-permute-start | bytes 294920 | tf_op jit(solution)/shard_map/ppermute | solution.py:516
  27.7 3.8 %collective-permute-start.11 = (f32[136,448]{1,0:T(8,128)S(1)}, f32[136,448]{1,0:T(8,128)S(1)}, u32[]{:S(2)}, u32[]{:S(2)}) collective-permute-start(f32[136,448]{1,0:T(8,128)S(1)} %get-tuple-element.46), channel_id=1, source_target_pairs={{0,1},{1,0},{2,3},{3,2},{4,5},{5,4},{6,7},{7,6},{8,9},{9,8},{10,11... | collective-permute-start | bytes 731144 | tf_op jit(solution)/shard_map/ppermute | solution.py:518
  27.8 3.7 %collective-permute-start.12 = (bf16[256,384]{1,0:T(8,128)(2,1)S(1)}, bf16[256,384]{1,0:T(8,128)(2,1)S(1)}, u32[]{:S(2)}, u32[]{:S(2)}) collective-permute-start(bf16[256,384]{1,0:T(8,128)(2,1)S(1)} %get-tuple-element.47), channel_id=1, source_target_pairs={{0,1},{1,0},{2,3},{3,2},{4,5},{5,4},{6,7},{7,6},{8,9},{9,8},{10,11... | collective-permute-start | bytes 589832 | tf_op jit(solution)/shard_map/ppermute | solution.py:519
  30.0 1.5 %collective-permute-start.10 = (bf16[48,1024]{1,0:T(8,128)(2,1)S(1)}, bf16[48,1024]{1,0:T(8,128)(2,1)S(1)}, u32[]{:S(2)}, u32[]{:S(2)}) collective-permute-start(bf16[48,1024]{1,0:T(8,128)(2,1)S(1)} %collective-permute-done.9.refs_1_), channel_id=1, source_target_pairs={{0,1},{1,0},{2,3},{3,2},{4,5},{5,4},{6,7},{7,6},{8,9},{9,8},{10,11... | collective-permute-start | bytes 294920 | tf_op jit(solution)/shard_map/ppermute | solution.py:521
  30.0 1.5 %collective-permute-start.7 = (bf16[64,1024]{1,0:T(8,128)(2,1)S(1)}, bf16[64,1024]{1,0:T(8,128)(2,1)S(1)}, u32[]{:S(2)}, u32[]{:S(2)}) collective-permute-start(bf16[64,1024]{1,0:T(8,128)(2,1)S(1)} %collective-permute-done.6.refs_0_), channel_id=1, source_target_pairs={{0,1},{1,0},{2,3},{3,2},{4,5},{5,4},{6,7},{7,6},{8,9},{9,8},{10,11... | collective-permute-start | bytes 393224 | tf_op jit(solution)/shard_map/ppermute | solution.py:521

commit v4 on v3

--- a/solution.py
+++ b/solution.py
@@ -511,18 +511,15 @@
         state = visit(state, arrivals)
         ahead, state = lax.optimization_barrier((ahead, state))
         arrivals = [(step, [ahead]), (-step, [behind])]
-    cut = round_up(rows // 2, TILE)
-    upper = lax.ppermute(ahead[:cut], "seq", forward)
-    lower = lax.ppermute(behind[cut:], "seq", backward)
+    farthest = lax.ppermute(ahead, "seq", forward)
     mine, my_pages, theirs, their_pages = visit(state, arrivals, last=True)
     got = lax.ppermute(theirs, "seq", swap)
     got_pages = lax.ppermute(their_pages, "seq", swap)
-    farthest = [(chips // 2, [upper, lower])]
-    other_farthest = [(chips // 2, [lax.ppermute(piece, "seq", swap) for piece in (upper, lower)])]
+    other_farthest = lax.ppermute(farthest, "seq", swap)
     operands = [queries, facts, wanted, mine, my_pages]
-    state = run(close_kernel, farthest, operands, half_shapes, "close", weight=10)
+    state = run(close_kernel, [(chips // 2, [farthest])], operands, half_shapes, "close", weight=10)
     operands = [queries, facts, wanted, *state, got, got_pages]
-    return run(finish_kernel, other_farthest, operands, out_shapes, "finish")
+    return run(finish_kernel, [(chips // 2, [other_farthest])], operands, out_shapes, "finish")
 
 
 def solution(mesh):

time: 33.4 us -> 32.9 us (0.985)
  starting transfers between devices: 10.4 us -> 9.6 us
    ppermute x4 -> x2, starting transfers between devices: 2.64 us -> 1.83 us  [the longest x1 1.83 us: shards(): farthest = lax.ppermute(ahead, 'seq', forward)]
    ppermute x4 -> x2, waiting for transfers between devices: 1.71 us -> 1.94 us  [the longest x1 1.47 us: shards(): farthest = lax.ppermute(ahead, 'seq', forward)]
  transfers between devices with their start and end apart: 13 -> 11, of which waited for: 5 -> 6; matrix products, arithmetic and copies ran while one was open for 2% -> 2% of each run, Pallas kernels for 31% -> 31%
where the time goes in v4:
time: 32.9 us; the launch traced here: 32.7 us
  Pallas kernels  13.2 us (40%)
  starting transfers between devices  9.6 us (29%)
  waiting for transfers between devices  8.62 us (26%)
  between operations  0.75 us (2%)
  other arithmetic  0.46 us (1%)
    pallas_call x6, Pallas kernels, run(): pl.pallas_call(partial(kernel, seq_count, tokens, layout), out_shape=out_...  10.8 us
    ppermute x3, starting transfers between devices, shards(): ahead = lax.ppermute(ahead, 'seq', forward)  6.41 us
    ppermute x3, waiting for transfers between devices, shards(): ahead = lax.ppermute(ahead, 'seq', forward)  5.92 us
    pallas_call x2, Pallas kernels, gathered(): pl.pallas_call(kernel, out_shape=out_shape, in_specs=[anywhere] * len(ope...  2.43 us
    ppermute x1, starting transfers between devices, shards(): farthest = lax.ppermute(ahead, 'seq', forward)  1.83 us
    ppermute x1, waiting for transfers between devices, shards(): farthest = lax.ppermute(ahead, 'seq', forward)  1.47 us
    ppermute x1, waiting for transfers between devices, shards(): other_queries = lax.ppermute(queries, 'seq', swap)  0.75 us
    ppermute x3, starting transfers between devices, shards(): behind = lax.ppermute(behind, 'seq', backward)  0.72 us
  transfers between devices with their start and end apart: 11, of which 6 were waited for; matrix products, arithmetic and copies ran while one was open for 2% of the time, Pallas kernels for 31%

profile of v4, /device:TPU:0, one launch (start us, length us, event | category | flops | bytes accessed | tf_op | source)
XLA Modules:
  0.0 32.7 jit_solution(18003106386757504052)
XLA Ops:
  0.6 1.3 %prepare.1.refs_0_ = bf16[112,1024]{1,0:T(8,128)(2,1)S(1)} custom-call(s32[16]{0:T(128)} %refs_0_.3, s32[16]{0:T(128)} %refs_1_.3, s32[16]{0:T(128)} %refs_2_.3, f32[1,128]{1,0:T(1,128)} %constant.14.clone.refs_3_, s32[16,56]{1,0:T(8,128)} %refs_4_.3, bf16[56,256]{1,0:T(8,128)(2,1)} %refs_5_.2, bf16[96,1024]{1,0:T(8,128)(2,1)} %refs_6_.1), custom_call_target="tpu_custom_call" | custom-call | flops 100000000 | bytes 6291456 | tf_op jit(solution)/shard_map/prepare/pallas_call | solution.py:406
  1.9 3.1 %collective-permute-start = (bf16[112,1024]{1,0:T(8,128)(2,1)S(1)}, bf16[112,1024]{1,0:T(8,128)(2,1)S(1)}, u32[]{:S(2)}, u32[]{:S(2)}) collective-permute-start(bf16[112,1024]{1,0:T(8,128)(2,1)S(1)} %prepare.1.refs_0_), channel_id=1, source_target_pairs={{0,4},{1,5},{4,8},{5,9},{8,12},{9,13},{12,14},{13,15},{14,10},{15,... | collective-permute-start | bytes 688136 | tf_op jit(solution)/shard_map/ppermute | solution.py:509
  5.0 0.0 collective-permute-start.3
  5.0 1.2 %plan.1 = (bf16[448,128]{1,0:T(8,128)(2,1)S(1)}, f32[24,128]{1,0:T(8,128)S(1)}) custom-call(s32[16]{0:T(128)} %refs_0_.3, s32[16]{0:T(128)} %refs_1_.3, s32[16]{0:T(128)} %refs_2_.3, f32[1,128]{1,0:T(1,128)} %constant.14.clone.refs_3_, s32[16,56]{1,0:T(8,128)} %refs_4_.3, bf16[56,1024]{1,0:T(8,128)(2,1)} %refs_5_.3), custom_call_target="tpu_custom_call" | custom-call | flops 100000000 | bytes 6291456 | tf_op jit(solution)/shard_map/plan/pallas_call | solution.py:406
  6.2 0.1 collective-permute-start.1
  6.2 0.1 add_multiply_fusion
  6.3 0.1 iota_add_fusion
  6.4 0.3 select_reduce_fusion
  6.7 0.1 convert_element_type.14.refs_4_.refs_5_.refs_3_
  6.8 0.8 %collective-permute-done.1.refs_2_.refs_3_ = bf16[448,128]{1,0:T(8,128)(2,1)S(1)} collective-permute-done((bf16[448,128]{1,0:T(8,128)(2,1)S(1)}, bf16[448,128]{1,0:T(8,128)(2,1)S(1)}, u32[]{:S(2)}, u32[]{:S(2)}) %collective-permute-start.1) | collective-permute-done | bytes 114720 | tf_op jit(solution)/shard_map/ppermute | solution.py:459
  7.6 1.3 %visit.4 = (f32[136,896]{1,0:T(8,128)S(1)}, bf16[256,768]{1,0:T(8,128)(2,1)S(1)}) custom-call(bf16[112,1024]{1,0:T(8,128)(2,1)S(1)} %prepare.1.refs_0_, bf16[448,128]{1,0:T(8,128)(2,1)S(1)} %get-tuple-element.25.refs_1_.refs_2_, bf16[448,128]{1,0:T(8,128)(2,1)S(1)} %collective-permute-done.1.refs_2_.refs_3_, ...), custom_call_target="tpu_custom_call" | custom-call | flops 381681664 | bytes 4194304 | tf_op jit(solution)/shard_map/visit/pallas_call | solution.py:478
  8.9 1.6 %collective-permute-done.refs_0_ = bf16[112,1024]{1,0:T(8,128)(2,1)S(1)} collective-permute-done((bf16[112,1024]{1,0:T(8,128)(2,1)S(1)}, bf16[112,1024]{1,0:T(8,128)(2,1)S(1)}, u32[]{:S(2)}, u32[]{:S(2)}) %collective-permute-start) | collective-permute-done | bytes 229408 | tf_op jit(solution)/shard_map/ppermute | solution.py:509
  10.5 1.8 %collective-permute-start.2 = (bf16[112,1024]{1,0:T(8,128)(2,1)S(1)}, bf16[112,1024]{1,0:T(8,128)(2,1)S(1)}, u32[]{:S(2)}, u32[]{:S(2)}) collective-permute-start(bf16[112,1024]{1,0:T(8,128)(2,1)S(1)} %collective-permute-done.refs_0_), channel_id=1, source_target_pairs={{0,4},{1,5},{4,8},{5,9},{8,12},{9,13},{12,14},{13,15},{14,10},{15,... | collective-permute-start | bytes 688136 | tf_op jit(solution)/shard_map/ppermute | solution.py:509
  12.3 0.0 collective-permute-done.3.refs_1_
  12.3 0.2 collective-permute-start.5
  12.5 2.3 %visit.5 = (f32[136,896]{1,0:T(8,128)S(1)}, bf16[256,768]{1,0:T(8,128)(2,1)S(1)}) custom-call(bf16[112,1024]{1,0:T(8,128)(2,1)S(1)} %collective-permute-done.refs_0_, bf16[112,1024]{1,0:T(8,128)(2,1)S(1)} %collective-permute-done.3.refs_1_, bf16[448,128]{1,0:T(8,128)(2,1)S(1)} %get-tuple-element.25.refs_1_.refs_2_, ...), custom_call_target="tpu_custom_call", output_to_operand_aliasing={{0}: (6, {}), {1}: (7, {})} | custom-call | flops 763363328 | bytes 4194304 | tf_op jit(solution)/shard_map/visit/pallas_call | solution.py:478
  14.8 2.5 %collective-permute-done.2.refs_0_ = bf16[112,1024]{1,0:T(8,128)(2,1)S(1)} collective-permute-done((bf16[112,1024]{1,0:T(8,128)(2,1)S(1)}, bf16[112,1024]{1,0:T(8,128)(2,1)S(1)}, u32[]{:S(2)}, u32[]{:S(2)}) %collective-permute-start.2) | collective-permute-done | bytes 229408 | tf_op jit(solution)/shard_map/ppermute | solution.py:509
  17.3 1.5 %collective-permute-start.4 = (bf16[112,1024]{1,0:T(8,128)(2,1)S(1)}, bf16[112,1024]{1,0:T(8,128)(2,1)S(1)}, u32[]{:S(2)}, u32[]{:S(2)}) collective-permute-start(bf16[112,1024]{1,0:T(8,128)(2,1)S(1)} %collective-permute-done.2.refs_0_), channel_id=1, source_target_pairs={{0,4},{1,5},{4,8},{5,9},{8,12},{9,13},{12,14},{13,15},{14,10},{15,... | collective-permute-start | bytes 688136 | tf_op jit(solution)/shard_map/ppermute | solution.py:509
  18.8 0.0 collective-permute-done.5.refs_1_
  18.8 0.5 %collective-permute-start.8 = (bf16[112,1024]{1,0:T(8,128)(2,1)S(1)}, bf16[112,1024]{1,0:T(8,128)(2,1)S(1)}, u32[]{:S(2)}, u32[]{:S(2)}) collective-permute-start(bf16[112,1024]{1,0:T(8,128)(2,1)S(1)} %collective-permute-done.5.refs_1_), channel_id=1, source_target_pairs={{0,2},{1,3},{4,0},{5,1},{8,4},{9,5},{12,8},{13,9},{14,12},{15,13},... | collective-permute-start | bytes 688136 | tf_op jit(solution)/shard_map/ppermute | solution.py:510
  19.3 2.3 %visit.6 = (f32[136,896]{1,0:T(8,128)S(1)}, bf16[256,768]{1,0:T(8,128)(2,1)S(1)}) custom-call(bf16[112,1024]{1,0:T(8,128)(2,1)S(1)} %collective-permute-done.2.refs_0_, bf16[112,1024]{1,0:T(8,128)(2,1)S(1)} %collective-permute-done.5.refs_1_, bf16[448,128]{1,0:T(8,128)(2,1)S(1)} %get-tuple-element.25.refs_1_.refs_2_, ...), custom_call_target="tpu_custom_call", output_to_operand_aliasing={{0}: (6, {}), {1}: (7, {})} | custom-call | flops 763363328 | bytes 4194304 | tf_op jit(solution)/shard_map/visit/pallas_call | solution.py:478
  21.6 1.8 %collective-permute-done.4.refs_0_ = bf16[112,1024]{1,0:T(8,128)(2,1)S(1)} collective-permute-done((bf16[112,1024]{1,0:T(8,128)(2,1)S(1)}, bf16[112,1024]{1,0:T(8,128)(2,1)S(1)}, u32[]{:S(2)}, u32[]{:S(2)}) %collective-permute-start.4) | collective-permute-done | bytes 229408 | tf_op jit(solution)/shard_map/ppermute | solution.py:509
  23.5 1.8 %collective-permute-start.6 = (bf16[112,1024]{1,0:T(8,128)(2,1)S(1)}, bf16[112,1024]{1,0:T(8,128)(2,1)S(1)}, u32[]{:S(2)}, u32[]{:S(2)}) collective-permute-start(bf16[112,1024]{1,0:T(8,128)(2,1)S(1)} %collective-permute-done.4.refs_0_), channel_id=1, source_target_pairs={{0,4},{1,5},{4,8},{5,9},{8,12},{9,13},{12,14},{13,15},{14,10},{15,... | collective-permute-start | bytes 688136 | tf_op jit(solution)/shard_map/ppermute | solution.py:514
  25.3 2.1 %visit.7 = (f32[136,448]{1,0:T(8,128)S(1)}, bf16[256,384]{1,0:T(8,128)(2,1)S(1)}, f32[136,448]{1,0:T(8,128)S(1)}, bf16[256,384]{1,0:T(8,128)(2,1)S(1)}) custom-call(bf16[112,1024]{1,0:T(8,128)(2,1)S(1)} %collective-permute-done.4.refs_0_, bf16[112,1024]{1,0:T(8,128)(2,1)S(1)} %collective-permute-done.8.refs_1_, ...), custom_call_target="tpu_custom_call" | custom-call | flops 763363328 | bytes 4194304 | tf_op jit(solution)/shard_map/visit/pallas_call | solution.py:478
  27.4 0.1 collective-permute-start.9
  27.5 0.5 %collective-permute-start.10 = (bf16[256,384]{1,0:T(8,128)(2,1)S(1)}, bf16[256,384]{1,0:T(8,128)(2,1)S(1)}, u32[]{:S(2)}, u32[]{:S(2)}) collective-permute-start(bf16[256,384]{1,0:T(8,128)(2,1)S(1)} %get-tuple-element.47), channel_id=1, source_target_pairs={{0,1},{1,0},{2,3},{3,2},{4,5},{5,4},{6,7},{7,6},{8,9},{9,8},{10,11... | collective-permute-start | bytes 589832 | tf_op jit(solution)/shard_map/ppermute | solution.py:517
  28.0 1.5 %collective-permute-done.6.refs_0_ = bf16[112,1024]{1,0:T(8,128)(2,1)S(1)} collective-permute-done((bf16[112,1024]{1,0:T(8,128)(2,1)S(1)}, bf16[112,1024]{1,0:T(8,128)(2,1)S(1)}, u32[]{:S(2)}, u32[]{:S(2)}) %collective-permute-start.6) | collective-permute-done | bytes 229408 | tf_op jit(solution)/shard_map/ppermute | solution.py:514
  29.5 0.0 collective-permute-start.7
  29.5 1.0 %close.1 = (f32[136,448]{1,0:T(8,128)S(1)}, bf16[256,384]{1,0:T(8,128)(2,1)S(1)}) custom-call(bf16[112,1024]{1,0:T(8,128)(2,1)S(1)} %collective-permute-done.6.refs_0_, bf16[448,128]{1,0:T(8,128)(2,1)S(1)} %get-tuple-element.25.refs_1_.refs_2_, f32[24,128]{1,0:T(8,128)S(1)} %get-tuple-element.26.refs_3_.refs_4_.refs_2_, ...), custom_call_target="tpu_custom_call" | custom-call | flops 3816816640 | bytes 41943040 | tf_op jit(solution)/shard_map/close/pallas_call | solution.py:478
  30.5 0.0 collective-permute-done.10.refs_7_
  30.5 0.5 %collective-permute-done.7.refs_0_ = bf16[112,1024]{1,0:T(8,128)(2,1)S(1)} collective-permute-done((bf16[112,1024]{1,0:T(8,128)(2,1)S(1)}, bf16[112,1024]{1,0:T(8,128)(2,1)S(1)}, u32[]{:S(2)}, u32[]{:S(2)}) %collective-permute-start.7) | collective-permute-done | bytes 229408 | tf_op jit(solution)/shard_map/ppermute | solution.py:518
  31.0 1.7 %finish.1 = (bf16[56,1024]{1,0:T(8,128)(2,1)}, bf16[96,1024]{1,0:T(8,128)(2,1)}) custom-call(bf16[112,1024]{1,0:T(8,128)(2,1)S(1)} %collective-permute-done.7.refs_0_, bf16[448,128]{1,0:T(8,128)(2,1)S(1)} %get-tuple-element.25.refs_1_.refs_2_, f32[24,128]{1,0:T(8,128)S(1)} %get-tuple-element.26.refs_3_.refs_4_.refs_2_, ...), custom_call_target="tpu_custom_call" | custom-call | flops 381681664 | bytes 4194304 | tf_op jit(solution)/shard_map/finish/pallas_call | solution.py:478
  (6 shorter events, 0.0 us)
Async XLA Ops:
  0.6 5.8 %copy-start = (s32[1536]{0:T(1024)S(1)}, s32[1536]{0:T(1024)}, u32[]{:S(2)}) copy-start(s32[1536]{0:T(1024)} %param.14) | copy-start | bytes 18436
  1.9 8.6 %collective-permute-start = (bf16[112,1024]{1,0:T(8,128)(2,1)S(1)}, bf16[112,1024]{1,0:T(8,128)(2,1)S(1)}, u32[]{:S(2)}, u32[]{:S(2)}) collective-permute-start(bf16[112,1024]{1,0:T(8,128)(2,1)S(1)} %prepare.1.refs_0_), channel_id=1, source_target_pairs={{0,4},{1,5},{4,8},{5,9},{8,12},{9,13},{12,14},{13,15},{14,10},{15,... | collective-permute-start | bytes 688136 | tf_op jit(solution)/shard_map/ppermute | solution.py:509
  5.0 7.3 %collective-permute-start.3 = (bf16[112,1024]{1,0:T(8,128)(2,1)S(1)}, bf16[112,1024]{1,0:T(8,128)(2,1)S(1)}, u32[]{:S(2)}, u32[]{:S(2)}) collective-permute-start(bf16[112,1024]{1,0:T(8,128)(2,1)S(1)} %prepare.1.refs_0_), channel_id=1, source_target_pairs={{0,2},{1,3},{4,0},{5,1},{8,4},{9,5},{12,8},{13,9},{14,12},{15,13},... | collective-permute-start | bytes 688136 | tf_op jit(solution)/shard_map/ppermute | solution.py:510
  6.2 1.4 %collective-permute-start.1 = (bf16[448,128]{1,0:T(8,128)(2,1)S(1)}, bf16[448,128]{1,0:T(8,128)(2,1)S(1)}, u32[]{:S(2)}, u32[]{:S(2)}) collective-permute-start(bf16[448,128]{1,0:T(8,128)(2,1)S(1)} %get-tuple-element.25.refs_1_.refs_2_), channel_id=1, source_target_pairs={{0,1},{1,0},{2,3},{3,2},{4,5},{5,4},{6,7},{7,6},{8,9},{9,8},{10,11... | collective-permute-start | bytes 344072 | tf_op jit(solution)/shard_map/ppermute | solution.py:459
  10.5 6.8 %collective-permute-start.2 = (bf16[112,1024]{1,0:T(8,128)(2,1)S(1)}, bf16[112,1024]{1,0:T(8,128)(2,1)S(1)}, u32[]{:S(2)}, u32[]{:S(2)}) collective-permute-start(bf16[112,1024]{1,0:T(8,128)(2,1)S(1)} %collective-permute-done.refs_0_), channel_id=1, source_target_pairs={{0,4},{1,5},{4,8},{5,9},{8,12},{9,13},{12,14},{13,15},{14,10},{15,... | collective-permute-start | bytes 688136 | tf_op jit(solution)/shard_map/ppermute | solution.py:509
  12.3 6.5 %collective-permute-start.5 = (bf16[112,1024]{1,0:T(8,128)(2,1)S(1)}, bf16[112,1024]{1,0:T(8,128)(2,1)S(1)}, u32[]{:S(2)}, u32[]{:S(2)}) collective-permute-start(bf16[112,1024]{1,0:T(8,128)(2,1)S(1)} %collective-permute-done.3.refs_1_), channel_id=1, source_target_pairs={{0,2},{1,3},{4,0},{5,1},{8,4},{9,5},{12,8},{13,9},{14,12},{15,13},... | collective-permute-start | bytes 688136 | tf_op jit(solution)/shard_map/ppermute | solution.py:510
  17.3 6.1 %collective-permute-start.4 = (bf16[112,1024]{1,0:T(8,128)(2,1)S(1)}, bf16[112,1024]{1,0:T(8,128)(2,1)S(1)}, u32[]{:S(2)}, u32[]{:S(2)}) collective-permute-start(bf16[112,1024]{1,0:T(8,128)(2,1)S(1)} %collective-permute-done.2.refs_0_), channel_id=1, source_target_pairs={{0,4},{1,5},{4,8},{5,9},{8,12},{9,13},{12,14},{13,15},{14,10},{15,... | collective-permute-start | bytes 688136 | tf_op jit(solution)/shard_map/ppermute | solution.py:509
  18.8 6.5 %collective-permute-start.8 = (bf16[112,1024]{1,0:T(8,128)(2,1)S(1)}, bf16[112,1024]{1,0:T(8,128)(2,1)S(1)}, u32[]{:S(2)}, u32[]{:S(2)}) collective-permute-start(bf16[112,1024]{1,0:T(8,128)(2,1)S(1)} %collective-permute-done.5.refs_1_), channel_id=1, source_target_pairs={{0,2},{1,3},{4,0},{5,1},{8,4},{9,5},{12,8},{13,9},{14,12},{15,13},... | collective-permute-start | bytes 688136 | tf_op jit(solution)/shard_map/ppermute | solution.py:510
  23.5 6.0 %collective-permute-start.6 = (bf16[112,1024]{1,0:T(8,128)(2,1)S(1)}, bf16[112,1024]{1,0:T(8,128)(2,1)S(1)}, u32[]{:S(2)}, u32[]{:S(2)}) collective-permute-start(bf16[112,1024]{1,0:T(8,128)(2,1)S(1)} %collective-permute-done.4.refs_0_), channel_id=1, source_target_pairs={{0,4},{1,5},{4,8},{5,9},{8,12},{9,13},{12,14},{13,15},{14,10},{15,... | collective-permute-start | bytes 688136 | tf_op jit(solution)/shard_map/ppermute | solution.py:514
  27.4 3.1 %collective-permute-start.9 = (f32[136,448]{1,0:T(8,128)S(1)}, f32[136,448]{1,0:T(8,128)S(1)}, u32[]{:S(2)}, u32[]{:S(2)}) collective-permute-start(f32[136,448]{1,0:T(8,128)S(1)} %get-tuple-element.46), channel_id=1, source_target_pairs={{0,1},{1,0},{2,3},{3,2},{4,5},{5,4},{6,7},{7,6},{8,9},{9,8},{10,11... | collective-permute-start | bytes 731144 | tf_op jit(solution)/shard_map/ppermute | solution.py:516
  27.5 3.0 %collective-permute-start.10 = (bf16[256,384]{1,0:T(8,128)(2,1)S(1)}, bf16[256,384]{1,0:T(8,128)(2,1)S(1)}, u32[]{:S(2)}, u32[]{:S(2)}) collective-permute-start(bf16[256,384]{1,0:T(8,128)(2,1)S(1)} %get-tuple-element.47), channel_id=1, source_target_pairs={{0,1},{1,0},{2,3},{3,2},{4,5},{5,4},{6,7},{7,6},{8,9},{9,8},{10,11... | collective-permute-start | bytes 589832 | tf_op jit(solution)/shard_map/ppermute | solution.py:517
  29.5 1.5 %collective-permute-start.7 = (bf16[112,1024]{1,0:T(8,128)(2,1)S(1)}, bf16[112,1024]{1,0:T(8,128)(2,1)S(1)}, u32[]{:S(2)}, u32[]{:S(2)}) collective-permute-start(bf16[112,1024]{1,0:T(8,128)(2,1)S(1)} %collective-permute-done.6.refs_0_), channel_id=1, source_target_pairs={{0,1},{1,0},{2,3},{3,2},{4,5},{5,4},{6,7},{7,6},{8,9},{9,8},{10,11... | collective-permute-start | bytes 688136 | tf_op jit(solution)/shard_map/ppermute | solution.py:518

commit v5 on v4

--- a/solution.py
+++ b/solution.py
@@ -270,10 +270,9 @@
     return float(head_dim**-0.5 * np.log2(np.e))
 
 
-def attend(blended, place, queries, limit, wanted, old):
+def attend(blended, flipped, place, queries, limit, old):
     head_dim = queries.shape[1]
     factor = score_factor(head_dim)
-    flipped = blended.T
     scores = lax.dot_general(
         blended[:, :head_dim], queries, (((1,), (1,)), ((), ())), preferred_element_type=f32
     )
@@ -281,35 +280,44 @@
     peak = jnp.maximum(jnp.max(scores, axis=0, keepdims=True), LOWEST if old is None else old[0])
     weights = jnp.exp2((scores - peak) * factor)
     total = jnp.sum(weights, axis=0, keepdims=True)
-    mixed = jnp.dot(flipped[head_dim:, :], weights.astype(bf16), preferred_element_type=f32)
-    chosen = jnp.where(place == wanted, 1.0, 0.0).astype(bf16)
-    picked = jnp.dot(flipped, chosen, preferred_element_type=f32)
+    mixed = jnp.dot(flipped, weights.astype(bf16), preferred_element_type=f32)
     if old is not None:
         fade = jnp.exp2((old[0] - peak) * factor)
         total = total + old[1] * fade
         mixed = mixed + old[2] * fade
-        picked = picked + old[3]
-    return peak, total, mixed, picked
-
-
-def get_state(ref, pages_ref):
+    return peak, total, mixed
+
+
+def chosen(place, wanted):
+    return jnp.where(place == wanted, 1.0, 0.0).astype(bf16)
+
+
+def get_state(ref):
     head_dim = ref.shape[0] - 8
     peak = ref[head_dim : head_dim + 1, :]
     total = ref[head_dim + 1 : head_dim + 2, :]
-    return peak, total, ref[:head_dim, :], pages_ref[...].astype(f32)
-
-
-def put_state(state, half, ref, pages_ref):
-    peak, total, mixed, picked = state
+    return peak, total, ref[:head_dim, :]
+
+
+def put_state(state, half, ref):
+    peak, total, mixed = state
     head_dim = mixed.shape[0]
     tail = jnp.concatenate([peak, total, jnp.zeros((6, peak.shape[1]), f32)], axis=0)
-    count, wide = ref.shape[1], pages_ref.shape[1]
+    count = ref.shape[1]
     if half == 1:
         mixed, tail = pltpu.roll(mixed, count, 1), pltpu.roll(tail, count, 1)
-        picked = picked[:, wide:]
     ref[:head_dim, :] = mixed[:, :count]
     ref[head_dim:, :] = tail[:, :count]
-    pages_ref[...] = picked[:, :wide].astype(bf16)
+
+
+def put_pages(picked, ref, *others):
+    count = ref.shape[0]
+    pair = picked.shape[1]
+    for u in range(PAGE):
+        part = picked[u * count : (u + 1) * count, :]
+        for other in others:
+            part = part + other[:, u * pair : (u + 1) * pair].astype(f32)
+        ref[:, u * pair : (u + 1) * pair] = part.astype(bf16)
 
 
 def visit_kernel(seq_count, tokens, arrivals, first, last, *refs):
@@ -319,65 +327,79 @@
     refs = refs[piece_count + 4 :]
     old = None
     if not first:
-        old = get_state(*refs[:2])
+        old, old_pages = get_state(refs[0]), refs[1]
         refs = refs[2:]
     core = lax.axis_index("seq") % 2
     blended, place, limit = read_chunks(
         seq_count, tokens, arrivals, core, pieces, facts_ref, own_q.shape[0]
     )
     queries = jnp.concatenate([own_q[...], other_q[...]], axis=0)
-    state = attend(blended, place, queries, limit, wanted_ref[...], old)
-    put_state(state, 0, *refs[:2])
-    if last:
-        put_state(state, 1, *refs[2:])
-
-
-def merged(one, two, factor):
-    peak = jnp.maximum(one[0], two[0])
-    fades = [jnp.exp2((part[0] - peak) * factor) for part in (one, two)]
-    return [peak] + [one[i] * fades[0] + two[i] * fades[1] for i in (1, 2)] + [one[3] + two[3]]
+    flipped = blended.T
+    state = attend(blended, flipped[own_q.shape[1] :, :], place, queries, limit, old)
+    picked = jnp.dot(flipped, chosen(place, wanted_ref[...]), preferred_element_type=f32)
+    if not first:
+        picked = picked + old_pages[...].astype(f32)
+    if not last:
+        put_state(state, 0, refs[0])
+        refs[1][...] = picked.astype(bf16)
+    else:
+        turned_pages = picked.T
+        for half in (0, 1):
+            put_state(state, half, refs[2 * half])
+            put_pages(turned_pages[half * tokens : (half + 1) * tokens, :], refs[2 * half + 1])
 
 
 def close_kernel(seq_count, tokens, arrivals, *refs):
-    pieces = refs[: len(refs) - 7]
-    own_q, facts_ref, wanted_ref, mine, my_pages, new, new_pages = refs[-7:]
+    chunk, own_q, facts_ref, wanted_ref, mine, my_pages = refs[:6]
+    new, new_pages, next_place, next_chosen = refs[6:]
     core = lax.axis_index("seq") % 2
-    query_rows = own_q.shape[0]
-    blended, place, limit = read_chunks(
-        seq_count, tokens, arrivals, core, pieces, facts_ref, query_rows
-    )
-    wanted = wanted_ref[:, :tokens]
-    old = get_state(mine, my_pages)
-    state = attend(blended, place, own_q[...], limit[:, :query_rows], wanted, old)
-    put_state(state, 0, new, new_pages)
-
-
-def finish_kernel(seq_count, tokens, arrivals, *refs):
-    pieces = refs[: len(refs) - 9]
-    own_q, facts_ref, wanted_ref, mine, my_pages, got, got_pages, out_ref, pages_ref = refs[-9:]
-    core = 1 - lax.axis_index("seq") % 2
     query_rows, head_dim = own_q.shape
     blended, place, limit = read_chunks(
-        seq_count, tokens, arrivals, core, pieces, facts_ref, query_rows
+        seq_count, tokens, arrivals, core, [chunk], facts_ref, query_rows
     )
     wanted = wanted_ref[:, :tokens]
-    old = merged(get_state(mine, my_pages), get_state(got, got_pages), score_factor(head_dim))
-    _, total, mixed, picked = attend(
-        blended, place, own_q[...], limit[:, :query_rows], wanted, old
-    )
-    flat = (mixed / total).T
+    state = attend(
+        blended, blended[:, head_dim:].T, place, own_q[...], limit[:, :query_rows], get_state(mine)
+    )
+    put_state(state, 0, new)
+    picked = jnp.dot(chosen(place, wanted).T, blended, preferred_element_type=f32)
+    put_pages(picked, new_pages, my_pages)
+
+    _, place, _ = read_chunks(
+        seq_count, tokens, arrivals, 1 - core, [chunk], facts_ref, query_rows
+    )
+    next_place[...] = jnp.broadcast_to(place, next_place.shape)
+    next_chosen[...] = chosen(place, wanted).T
+
+
+def finish_kernel(seq_count, tokens, arrivals, *refs):
+    chunk, own_q, facts_ref, mine, my_pages, place_ref, chosen_ref, got, got_pages = refs[:9]
+    out_ref, pages_ref, out_scratch, pages_scratch, sems = refs[9:]
+    query_rows, head_dim = own_q.shape
+    table_rows, limit_rows, _ = fact_rows(seq_count, query_rows, facts_ref.shape[1])
+    limit = get_rows(facts_ref, table_rows, limit_rows)[:, :query_rows]
+    blended = chunk_rows([chunk])
+    picked = jnp.dot(chosen_ref[...], blended, preferred_element_type=f32)
+    put_pages(picked, pages_scratch, my_pages, got_pages)
+    pages_copy = pltpu.make_async_copy(pages_scratch, pages_ref, sems.at[0])
+    pages_copy.start()
+    one, two = get_state(mine), get_state(got)
+    peak = jnp.maximum(one[0], two[0])
+    fades = [jnp.exp2((part[0] - peak) * score_factor(head_dim)) for part in (one, two)]
+    old = [peak] + [one[i] * fades[0] + two[i] * fades[1] for i in (1, 2)]
+    _, total, mixed = attend(
+        blended, blended[:, head_dim:].T, place_ref[:, :1], own_q[...], limit, old
+    )
+    flat = (mixed * (1.0 / total)).T
     sel = out_ref.shape[0]
     for h in range(GROUP):
-        out_ref[:, h * head_dim : (h + 1) * head_dim] = flat[h * sel : (h + 1) * sel, :].astype(
-            bf16
-        )
-    pages = picked.T
-    count = pages_ref.shape[0]
-    pair = 2 * head_dim
-    for u in range(PAGE):
-        pages_ref[:, u * pair : (u + 1) * pair] = pages[u * count : (u + 1) * count, :].astype(
-            bf16
-        )
+        out_scratch[:, h * head_dim : (h + 1) * head_dim] = flat[
+            h * sel : (h + 1) * sel, :
+        ].astype(bf16)
+    out_copy = pltpu.make_async_copy(out_scratch, out_ref, sems.at[1])
+    out_copy.start()
+    pages_copy.wait()
+    out_copy.wait()
 
 
 def shards(
@@ -464,14 +486,18 @@
     )
     half_shapes = (
         jax.ShapeDtypeStruct((head_dim + 8, query_rows), f32),
-        jax.ShapeDtypeStruct((2 * head_dim, tokens), bf16),
+        jax.ShapeDtypeStruct((pages, width), bf16),
+    )
+    close_shapes = half_shapes + (
+        jax.ShapeDtypeStruct((PAGE * rows, LANES), f32),
+        jax.ShapeDtypeStruct((tokens, PAGE * rows), bf16),
     )
     out_shapes = (
         jax.ShapeDtypeStruct((sel, GROUP * head_dim), bf16),
         jax.ShapeDtypeStruct((pages, width), bf16),
     )
 
-    def run(kernel, arrivals, operands, out_shape, name, aliases=(), weight=1):
+    def run(kernel, arrivals, operands, out_shape, name, aliases=(), weight=1, scratch=()):
         layout = [(step, len(pieces)) for step, pieces in arrivals]
         operands = [piece for _, pieces in arrivals for piece in pieces] + list(operands)
         pairs = PAGE * rows * len(layout) * (query_rows + tokens)
@@ -479,7 +505,8 @@
             partial(kernel, seq_count, tokens, layout),
             out_shape=out_shape,
             in_specs=[vmem] * len(operands),
-            out_specs=(vmem,) * len(out_shape),
+            out_specs=(anywhere if scratch else vmem,) * len(out_shape),
+            scratch_shapes=scratch,
             input_output_aliases={len(operands) - 2 + i: i for i in aliases},
             compiler_params=params,
             cost_estimate=pl.CostEstimate(
@@ -517,9 +544,16 @@
     got_pages = lax.ppermute(their_pages, "seq", swap)
     other_farthest = lax.ppermute(farthest, "seq", swap)
     operands = [queries, facts, wanted, mine, my_pages]
-    state = run(close_kernel, [(chips // 2, [farthest])], operands, half_shapes, "close", weight=10)
-    operands = [queries, facts, wanted, *state, got, got_pages]
-    return run(finish_kernel, [(chips // 2, [other_farthest])], operands, out_shapes, "finish")
+    *state, place, choice = run(
+        close_kernel, [(chips // 2, [farthest])], operands, close_shapes, "close", weight=10
+    )
+    scratch = [pltpu.VMEM(x.shape, x.dtype) for x in out_shapes]
+    scratch.append(pltpu.SemaphoreType.DMA((2,)))
+    operands = [queries, facts, *state, place, choice, got, got_pages]
+    return run(
+        finish_kernel, [(chips // 2, [other_farthest])], operands, out_shapes, "finish",
+        scratch=scratch,
+    )
 
 
 def solution(mesh):

time: 32.9 us -> 32.6 us (level)
  waiting for transfers between devices: 8.62 us -> 8.29 us
    ppermute x1, waiting for transfers between devices: 0.47 us -> 0.14 us  [shards(): other_farthest = lax.ppermute(farthest, 'seq', swap)]
  transfers between devices with their start and end apart: 11 -> 11, of which waited for: 6 -> 6; matrix products, arithmetic and copies ran while one was open for 2% -> 2% of each run, Pallas kernels for 31% -> 32%
where the time goes in v5:
time: 32.6 us; the launch traced here: 32.4 us
  Pallas kernels  13.3 us (41%)
  starting transfers between devices  9.59 us (29%)
  waiting for transfers between devices  8.29 us (25%)
  between operations  0.74 us (2%)
  other arithmetic  0.46 us (1%)
    pallas_call x6, Pallas kernels, run(): pl.pallas_call(partial(kernel, seq_count, tokens, layout), out_shape=out_...  10.9 us
    ppermute x3, starting transfers between devices, shards(): ahead = lax.ppermute(ahead, 'seq', forward)  6.41 us
    ppermute x3, waiting for transfers between devices, shards(): ahead = lax.ppermute(ahead, 'seq', forward)  5.97 us
    pallas_call x2, Pallas kernels, gathered(): pl.pallas_call(kernel, out_shape=out_shape, in_specs=[anywhere] * len(ope...  2.43 us
    ppermute x1, starting transfers between devices, shards(): farthest = lax.ppermute(ahead, 'seq', forward)  1.83 us
    ppermute x1, waiting for transfers between devices, shards(): farthest = lax.ppermute(ahead, 'seq', forward)  1.42 us
    ppermute x1, waiting for transfers between devices, shards(): other_queries = lax.ppermute(queries, 'seq', swap)  0.75 us
    ppermute x3, starting transfers between devices, shards(): behind = lax.ppermute(behind, 'seq', backward)  0.72 us
  transfers between devices with their start and end apart: 11, of which 6 were waited for; matrix products, arithmetic and copies ran while one was open for 2% of the time, Pallas kernels for 32%

profile of v5, /device:TPU:0, one launch (start us, length us, event | category | flops | bytes accessed | tf_op | source)
XLA Modules:
  0.0 32.4 jit_solution(15473279312919176864)
XLA Ops:
  0.6 1.3 %prepare.1.refs_0_ = bf16[112,1024]{1,0:T(8,128)(2,1)S(1)} custom-call(s32[16]{0:T(128)} %refs_0_.3, s32[16]{0:T(128)} %refs_1_.3, s32[16]{0:T(128)} %refs_2_.3, f32[1,128]{1,0:T(1,128)} %constant.14.clone.refs_3_, s32[16,56]{1,0:T(8,128)} %refs_4_.3, bf16[56,256]{1,0:T(8,128)(2,1)} %refs_5_.2, bf16[96,1024]{1,0:T(8,128)(2,1)} %refs_6_.1), custom_call_target="tpu_custom_call" | custom-call | flops 100000000 | bytes 6291456 | tf_op jit(solution)/shard_map/prepare/pallas_call | solution.py:428
  1.9 3.1 %collective-permute-start = (bf16[112,1024]{1,0:T(8,128)(2,1)S(1)}, bf16[112,1024]{1,0:T(8,128)(2,1)S(1)}, u32[]{:S(2)}, u32[]{:S(2)}) collective-permute-start(bf16[112,1024]{1,0:T(8,128)(2,1)S(1)} %prepare.1.refs_0_), channel_id=1, source_target_pairs={{0,4},{1,5},{4,8},{5,9},{8,12},{9,13},{12,14},{13,15},{14,10},{15,... | collective-permute-start | bytes 688136 | tf_op jit(solution)/shard_map/ppermute | solution.py:536
  5.0 0.0 collective-permute-start.3
  5.0 1.2 %plan.1 = (bf16[448,128]{1,0:T(8,128)(2,1)S(1)}, f32[24,128]{1,0:T(8,128)S(1)}) custom-call(s32[16]{0:T(128)} %refs_0_.3, s32[16]{0:T(128)} %refs_1_.3, s32[16]{0:T(128)} %refs_2_.3, f32[1,128]{1,0:T(1,128)} %constant.14.clone.refs_3_, s32[16,56]{1,0:T(8,128)} %refs_4_.3, bf16[56,1024]{1,0:T(8,128)(2,1)} %refs_5_.3), custom_call_target="tpu_custom_call" | custom-call | flops 100000000 | bytes 6291456 | tf_op jit(solution)/shard_map/plan/pallas_call | solution.py:428
  6.2 0.1 collective-permute-start.1
  6.2 0.1 add_multiply_fusion
  6.3 0.1 iota_add_fusion
  6.4 0.3 select_reduce_fusion
  6.7 0.1 convert_element_type.14.refs_4_.refs_5_.refs_3_
  6.8 0.8 %collective-permute-done.1.refs_2_.refs_3_ = bf16[448,128]{1,0:T(8,128)(2,1)S(1)} collective-permute-done((bf16[448,128]{1,0:T(8,128)(2,1)S(1)}, bf16[448,128]{1,0:T(8,128)(2,1)S(1)}, u32[]{:S(2)}, u32[]{:S(2)}) %collective-permute-start.1) | collective-permute-done | bytes 114720 | tf_op jit(solution)/shard_map/ppermute | solution.py:481
  7.6 1.3 %visit.4 = (f32[136,896]{1,0:T(8,128)S(1)}, bf16[256,768]{1,0:T(8,128)(2,1)S(1)}) custom-call(bf16[112,1024]{1,0:T(8,128)(2,1)S(1)} %prepare.1.refs_0_, bf16[448,128]{1,0:T(8,128)(2,1)S(1)} %get-tuple-element.27.refs_1_.refs_2_, bf16[448,128]{1,0:T(8,128)(2,1)S(1)} %collective-permute-done.1.refs_2_.refs_3_, ...), custom_call_target="tpu_custom_call" | custom-call | flops 381681664 | bytes 4194304 | tf_op jit(solution)/shard_map/visit/pallas_call | solution.py:504
  8.9 1.6 %collective-permute-done.refs_0_ = bf16[112,1024]{1,0:T(8,128)(2,1)S(1)} collective-permute-done((bf16[112,1024]{1,0:T(8,128)(2,1)S(1)}, bf16[112,1024]{1,0:T(8,128)(2,1)S(1)}, u32[]{:S(2)}, u32[]{:S(2)}) %collective-permute-start) | collective-permute-done | bytes 229408 | tf_op jit(solution)/shard_map/ppermute | solution.py:536
  10.5 1.8 %collective-permute-start.2 = (bf16[112,1024]{1,0:T(8,128)(2,1)S(1)}, bf16[112,1024]{1,0:T(8,128)(2,1)S(1)}, u32[]{:S(2)}, u32[]{:S(2)}) collective-permute-start(bf16[112,1024]{1,0:T(8,128)(2,1)S(1)} %collective-permute-done.refs_0_), channel_id=1, source_target_pairs={{0,4},{1,5},{4,8},{5,9},{8,12},{9,13},{12,14},{13,15},{14,10},{15,... | collective-permute-start | bytes 688136 | tf_op jit(solution)/shard_map/ppermute | solution.py:536
  12.3 0.0 collective-permute-done.3.refs_1_
  12.3 0.2 collective-permute-start.5
  12.5 2.2 %visit.5 = (f32[136,896]{1,0:T(8,128)S(1)}, bf16[256,768]{1,0:T(8,128)(2,1)S(1)}) custom-call(bf16[112,1024]{1,0:T(8,128)(2,1)S(1)} %collective-permute-done.refs_0_, bf16[112,1024]{1,0:T(8,128)(2,1)S(1)} %collective-permute-done.3.refs_1_, bf16[448,128]{1,0:T(8,128)(2,1)S(1)} %get-tuple-element.27.refs_1_.refs_2_, ...), custom_call_target="tpu_custom_call", output_to_operand_aliasing={{0}: (6, {}), {1}: (7, {})} | custom-call | flops 763363328 | bytes 4194304 | tf_op jit(solution)/shard_map/visit/pallas_call | solution.py:504
  14.8 2.5 %collective-permute-done.2.refs_0_ = bf16[112,1024]{1,0:T(8,128)(2,1)S(1)} collective-permute-done((bf16[112,1024]{1,0:T(8,128)(2,1)S(1)}, bf16[112,1024]{1,0:T(8,128)(2,1)S(1)}, u32[]{:S(2)}, u32[]{:S(2)}) %collective-permute-start.2) | collective-permute-done | bytes 229408 | tf_op jit(solution)/shard_map/ppermute | solution.py:536
  17.3 1.5 %collective-permute-start.4 = (bf16[112,1024]{1,0:T(8,128)(2,1)S(1)}, bf16[112,1024]{1,0:T(8,128)(2,1)S(1)}, u32[]{:S(2)}, u32[]{:S(2)}) collective-permute-start(bf16[112,1024]{1,0:T(8,128)(2,1)S(1)} %collective-permute-done.2.refs_0_), channel_id=1, source_target_pairs={{0,4},{1,5},{4,8},{5,9},{8,12},{9,13},{12,14},{13,15},{14,10},{15,... | collective-permute-start | bytes 688136 | tf_op jit(solution)/shard_map/ppermute | solution.py:536
  18.8 0.5 %collective-permute-start.8 = (bf16[112,1024]{1,0:T(8,128)(2,1)S(1)}, bf16[112,1024]{1,0:T(8,128)(2,1)S(1)}, u32[]{:S(2)}, u32[]{:S(2)}) collective-permute-start(bf16[112,1024]{1,0:T(8,128)(2,1)S(1)} %collective-permute-done.5.refs_1_), channel_id=1, source_target_pairs={{0,2},{1,3},{4,0},{5,1},{8,4},{9,5},{12,8},{13,9},{14,12},{15,13},... | collective-permute-start | bytes 688136 | tf_op jit(solution)/shard_map/ppermute | solution.py:537
  19.3 2.3 %visit.6 = (f32[136,896]{1,0:T(8,128)S(1)}, bf16[256,768]{1,0:T(8,128)(2,1)S(1)}) custom-call(bf16[112,1024]{1,0:T(8,128)(2,1)S(1)} %collective-permute-done.2.refs_0_, bf16[112,1024]{1,0:T(8,128)(2,1)S(1)} %collective-permute-done.5.refs_1_, bf16[448,128]{1,0:T(8,128)(2,1)S(1)} %get-tuple-element.27.refs_1_.refs_2_, ...), custom_call_target="tpu_custom_call", output_to_operand_aliasing={{0}: (6, {}), {1}: (7, {})} | custom-call | flops 763363328 | bytes 4194304 | tf_op jit(solution)/shard_map/visit/pallas_call | solution.py:504
  21.6 1.8 %collective-permute-done.4.refs_0_ = bf16[112,1024]{1,0:T(8,128)(2,1)S(1)} collective-permute-done((bf16[112,1024]{1,0:T(8,128)(2,1)S(1)}, bf16[112,1024]{1,0:T(8,128)(2,1)S(1)}, u32[]{:S(2)}, u32[]{:S(2)}) %collective-permute-start.4) | collective-permute-done | bytes 229408 | tf_op jit(solution)/shard_map/ppermute | solution.py:536
  23.5 1.8 %collective-permute-start.6 = (bf16[112,1024]{1,0:T(8,128)(2,1)S(1)}, bf16[112,1024]{1,0:T(8,128)(2,1)S(1)}, u32[]{:S(2)}, u32[]{:S(2)}) collective-permute-start(bf16[112,1024]{1,0:T(8,128)(2,1)S(1)} %collective-permute-done.4.refs_0_), channel_id=1, source_target_pairs={{0,4},{1,5},{4,8},{5,9},{8,12},{9,13},{12,14},{13,15},{14,10},{15,... | collective-permute-start | bytes 688136 | tf_op jit(solution)/shard_map/ppermute | solution.py:541
  25.3 2.2 %visit.7 = (f32[136,448]{1,0:T(8,128)S(1)}, bf16[96,1024]{1,0:T(8,128)(2,1)S(1)}, f32[136,448]{1,0:T(8,128)S(1)}, bf16[96,1024]{1,0:T(8,128)(2,1)S(1)}) custom-call(bf16[112,1024]{1,0:T(8,128)(2,1)S(1)} %collective-permute-done.4.refs_0_, bf16[112,1024]{1,0:T(8,128)(2,1)S(1)} %collective-permute-done.8.refs_1_, ...), custom_call_target="tpu_custom_call" | custom-call | flops 763363328 | bytes 4194304 | tf_op jit(solution)/shard_map/visit/pallas_call | solution.py:504
  27.5 0.1 collective-permute-start.9
  27.6 0.5 %collective-permute-start.10 = (bf16[96,1024]{1,0:T(8,128)(2,1)S(1)}, bf16[96,1024]{1,0:T(8,128)(2,1)S(1)}, u32[]{:S(2)}, u32[]{:S(2)}) collective-permute-start(bf16[96,1024]{1,0:T(8,128)(2,1)S(1)} %get-tuple-element.51), channel_id=1, source_target_pairs={{0,1},{1,0},{2,3},{3,2},{4,5},{5,4},{6,7},{7,6},{8,9},{9,8},{10,11... | collective-permute-start | bytes 589832 | tf_op jit(solution)/shard_map/ppermute | solution.py:544
  28.1 1.4 %collective-permute-done.6.refs_0_ = bf16[112,1024]{1,0:T(8,128)(2,1)S(1)} collective-permute-done((bf16[112,1024]{1,0:T(8,128)(2,1)S(1)}, bf16[112,1024]{1,0:T(8,128)(2,1)S(1)}, u32[]{:S(2)}, u32[]{:S(2)}) %collective-permute-start.6) | collective-permute-done | bytes 229408 | tf_op jit(solution)/shard_map/ppermute | solution.py:541
  29.5 0.0 collective-permute-start.7
  29.5 1.3 %close.1 = (f32[136,448]{1,0:T(8,128)S(1)}, bf16[96,1024]{1,0:T(8,128)(2,1)S(1)}, f32[448,128]{1,0:T(8,128)S(1)}, bf16[384,448]{1,0:T(8,128)(2,1)S(1)}) custom-call(bf16[112,1024]{1,0:T(8,128)(2,1)S(1)} %collective-permute-done.6.refs_0_, bf16[448,128]{1,0:T(8,128)(2,1)S(1)} %get-tuple-element.27.refs_1_.refs_2_, ...), custom_call_target="tpu_custom_call" | custom-call | flops 3816816640 | bytes 41943040 | tf_op jit(solution)/shard_map/close/pallas_call | solution.py:504
  30.8 0.0 collective-permute-done.10.refs_8_
  30.8 0.0 collective-permute-done.9.refs_7_
  30.8 0.1 collective-permute-done.7.refs_0_
  31.0 1.5 %finish.1 = (bf16[56,1024]{1,0:T(8,128)(2,1)}, bf16[96,1024]{1,0:T(8,128)(2,1)}) custom-call(bf16[112,1024]{1,0:T(8,128)(2,1)S(1)} %collective-permute-done.7.refs_0_, bf16[448,128]{1,0:T(8,128)(2,1)S(1)} %get-tuple-element.27.refs_1_.refs_2_, f32[24,128]{1,0:T(8,128)S(1)} %get-tuple-element.28.refs_3_.refs_4_.refs_2_, ...), custom_call_target="tpu_custom_call" | custom-call | flops 381681664 | bytes 4194304 | tf_op jit(solution)/shard_map/finish/pallas_call | solution.py:504
  (6 shorter events, 0.0 us)
Async XLA Ops:
  0.6 5.8 %copy-start = (s32[1536]{0:T(1024)S(1)}, s32[1536]{0:T(1024)}, u32[]{:S(2)}) copy-start(s32[1536]{0:T(1024)} %param.14) | copy-start | bytes 18436
  1.9 8.6 %collective-permute-start = (bf16[112,1024]{1,0:T(8,128)(2,1)S(1)}, bf16[112,1024]{1,0:T(8,128)(2,1)S(1)}, u32[]{:S(2)}, u32[]{:S(2)}) collective-permute-start(bf16[112,1024]{1,0:T(8,128)(2,1)S(1)} %prepare.1.refs_0_), channel_id=1, source_target_pairs={{0,4},{1,5},{4,8},{5,9},{8,12},{9,13},{12,14},{13,15},{14,10},{15,... | collective-permute-start | bytes 688136 | tf_op jit(solution)/shard_map/ppermute | solution.py:536
  5.0 7.3 %collective-permute-start.3 = (bf16[112,1024]{1,0:T(8,128)(2,1)S(1)}, bf16[112,1024]{1,0:T(8,128)(2,1)S(1)}, u32[]{:S(2)}, u32[]{:S(2)}) collective-permute-start(bf16[112,1024]{1,0:T(8,128)(2,1)S(1)} %prepare.1.refs_0_), channel_id=1, source_target_pairs={{0,2},{1,3},{4,0},{5,1},{8,4},{9,5},{12,8},{13,9},{14,12},{15,13},... | collective-permute-start | bytes 688136 | tf_op jit(solution)/shard_map/ppermute | solution.py:537
  6.2 1.4 %collective-permute-start.1 = (bf16[448,128]{1,0:T(8,128)(2,1)S(1)}, bf16[448,128]{1,0:T(8,128)(2,1)S(1)}, u32[]{:S(2)}, u32[]{:S(2)}) collective-permute-start(bf16[448,128]{1,0:T(8,128)(2,1)S(1)} %get-tuple-element.27.refs_1_.refs_2_), channel_id=1, source_target_pairs={{0,1},{1,0},{2,3},{3,2},{4,5},{5,4},{6,7},{7,6},{8,9},{9,8},{10,11... | collective-permute-start | bytes 344072 | tf_op jit(solution)/shard_map/ppermute | solution.py:481
  10.5 6.8 %collective-permute-start.2 = (bf16[112,1024]{1,0:T(8,128)(2,1)S(1)}, bf16[112,1024]{1,0:T(8,128)(2,1)S(1)}, u32[]{:S(2)}, u32[]{:S(2)}) collective-permute-start(bf16[112,1024]{1,0:T(8,128)(2,1)S(1)} %collective-permute-done.refs_0_), channel_id=1, source_target_pairs={{0,4},{1,5},{4,8},{5,9},{8,12},{9,13},{12,14},{13,15},{14,10},{15,... | collective-permute-start | bytes 688136 | tf_op jit(solution)/shard_map/ppermute | solution.py:536
  12.3 6.5 %collective-permute-start.5 = (bf16[112,1024]{1,0:T(8,128)(2,1)S(1)}, bf16[112,1024]{1,0:T(8,128)(2,1)S(1)}, u32[]{:S(2)}, u32[]{:S(2)}) collective-permute-start(bf16[112,1024]{1,0:T(8,128)(2,1)S(1)} %collective-permute-done.3.refs_1_), channel_id=1, source_target_pairs={{0,2},{1,3},{4,0},{5,1},{8,4},{9,5},{12,8},{13,9},{14,12},{15,13},... | collective-permute-start | bytes 688136 | tf_op jit(solution)/shard_map/ppermute | solution.py:537
  17.3 6.1 %collective-permute-start.4 = (bf16[112,1024]{1,0:T(8,128)(2,1)S(1)}, bf16[112,1024]{1,0:T(8,128)(2,1)S(1)}, u32[]{:S(2)}, u32[]{:S(2)}) collective-permute-start(bf16[112,1024]{1,0:T(8,128)(2,1)S(1)} %collective-permute-done.2.refs_0_), channel_id=1, source_target_pairs={{0,4},{1,5},{4,8},{5,9},{8,12},{9,13},{12,14},{13,15},{14,10},{15,... | collective-permute-start | bytes 688136 | tf_op jit(solution)/shard_map/ppermute | solution.py:536
  18.8 6.5 %collective-permute-start.8 = (bf16[112,1024]{1,0:T(8,128)(2,1)S(1)}, bf16[112,1024]{1,0:T(8,128)(2,1)S(1)}, u32[]{:S(2)}, u32[]{:S(2)}) collective-permute-start(bf16[112,1024]{1,0:T(8,128)(2,1)S(1)} %collective-permute-done.5.refs_1_), channel_id=1, source_target_pairs={{0,2},{1,3},{4,0},{5,1},{8,4},{9,5},{12,8},{13,9},{14,12},{15,13},... | collective-permute-start | bytes 688136 | tf_op jit(solution)/shard_map/ppermute | solution.py:537
  23.5 6.0 %collective-permute-start.6 = (bf16[112,1024]{1,0:T(8,128)(2,1)S(1)}, bf16[112,1024]{1,0:T(8,128)(2,1)S(1)}, u32[]{:S(2)}, u32[]{:S(2)}) collective-permute-start(bf16[112,1024]{1,0:T(8,128)(2,1)S(1)} %collective-permute-done.4.refs_0_), channel_id=1, source_target_pairs={{0,4},{1,5},{4,8},{5,9},{8,12},{9,13},{12,14},{13,15},{14,10},{15,... | collective-permute-start | bytes 688136 | tf_op jit(solution)/shard_map/ppermute | solution.py:541
  27.5 3.3 %collective-permute-start.9 = (f32[136,448]{1,0:T(8,128)S(1)}, f32[136,448]{1,0:T(8,128)S(1)}, u32[]{:S(2)}, u32[]{:S(2)}) collective-permute-start(f32[136,448]{1,0:T(8,128)S(1)} %get-tuple-element.50), channel_id=1, source_target_pairs={{0,1},{1,0},{2,3},{3,2},{4,5},{5,4},{6,7},{7,6},{8,9},{9,8},{10,11... | collective-permute-start | bytes 731144 | tf_op jit(solution)/shard_map/ppermute | solution.py:543
  27.6 3.2 %collective-permute-start.10 = (bf16[96,1024]{1,0:T(8,128)(2,1)S(1)}, bf16[96,1024]{1,0:T(8,128)(2,1)S(1)}, u32[]{:S(2)}, u32[]{:S(2)}) collective-permute-start(bf16[96,1024]{1,0:T(8,128)(2,1)S(1)} %get-tuple-element.51), channel_id=1, source_target_pairs={{0,1},{1,0},{2,3},{3,2},{4,5},{5,4},{6,7},{7,6},{8,9},{9,8},{10,11... | collective-permute-start | bytes 589832 | tf_op jit(solution)/shard_map/ppermute | solution.py:544
  29.5 1.5 %collective-permute-start.7 = (bf16[112,1024]{1,0:T(8,128)(2,1)S(1)}, bf16[112,1024]{1,0:T(8,128)(2,1)S(1)}, u32[]{:S(2)}, u32[]{:S(2)}) collective-permute-start(bf16[112,1024]{1,0:T(8,128)(2,1)S(1)} %collective-permute-done.6.refs_0_), channel_id=1, source_target_pairs={{0,1},{1,0},{2,3},{3,2},{4,5},{5,4},{6,7},{7,6},{8,9},{9,8},{10,11... | collective-permute-start | bytes 688136 | tf_op jit(solution)/shard_map/ppermute | solution.py:545

commit v6 on v5

v6 whole, which is shorter than its diff:
```python
from functools import partial

import jax
import jax.numpy as jnp
import numpy as np
from jax import lax
from jax.experimental import pallas as pl
from jax.experimental.pallas import tpu as pltpu
from jax.sharding import PartitionSpec as P

GROUP = 8
PAGE = 4
ROPE_BASE = 500000.0
FAR = float(2**23)
MASKED = -1e30
LOWEST = -1e29
TILE = 16
LANES = 128

QUARTER = (1.5703125, 253 * 2.0**-19, 170 * 2.0**-27, float(np.pi / 2 - 1.5703125 - 253 * 2.0**-19 - 170 * 2.0**-27))

f32 = jnp.float32
bf16 = jnp.bfloat16


def round_up(value, step):
    return -(-value // step) * step


def frequencies(head_dim):
    half = head_dim // 2
    index = np.arange(half, dtype=np.float32) * np.float32(2.0 / head_dim)
    one = np.power(np.float32(ROPE_BASE), -index).astype(np.float32)
    return np.concatenate([one, one])[None, :]


def ring_place(chip, chips):
    return jnp.where(chip % 2 == 0, chip // 2, chips - 1 - chip // 2)


def ring_chip(place, chips):
    return jnp.where(place < chips // 2, 2 * place, 2 * (chips - 1 - place) + 1)


def ring_order(chips):
    return list(range(0, chips, 2)) + list(range(chips - 1, 0, -2))


def ring_pairs(chips, shift):
    order = ring_order(chips)
    return [
        (order[p] * 2 + core, order[(p + shift) % chips] * 2 + core)
        for p in range(chips)
        for core in range(2)
    ]


def turned(vector, cosine, signed_sine):
    half = vector.shape[1] // 2
    return vector * cosine + pltpu.roll(vector, half, 1) * signed_sine


def cos_sin(angle):
    turns = jnp.round(angle * float(2 / np.pi))
    rest = angle
    for part in QUARTER:
        rest = rest - turns * part
    square = rest * rest
    sine = rest + rest * square * (
        -1.6666654611e-1 + square * (8.3321608736e-3 - square * 1.9515295891e-4)
    )
    cosine = (
        1.0
        - 0.5 * square
        + square
        * square
        * (4.166664568298827e-2 + square * (-1.388731625493765e-3 + square * 2.443315711809948e-5))
    )
    quadrant = turns.astype(jnp.int32) & 3
    odd = (quadrant & 1) == 1
    cos_value = jnp.where(odd, sine, cosine)
    sin_value = jnp.where(odd, cosine, sine)
    cos_value = jnp.where((quadrant == 1) | (quadrant == 2), -cos_value, cos_value)
    sin_value = jnp.where(quadrant >= 2, -sin_value, sin_value)
    return cos_value, sin_value


def rotation(angle):
    head_dim = angle.shape[1]
    cosine, sine = cos_sin(angle)
    lower = lax.broadcasted_iota(jnp.int32, angle.shape, 1) < head_dim // 2
    return cosine, jnp.where(lower, -sine, sine)


def fresh_rotation(row, start, frequency):
    sel = row.shape[1]
    wide = jnp.broadcast_to(row.astype(f32), (sel, sel))
    same = lax.broadcasted_iota(jnp.int32, (sel, sel), 0) == lax.broadcasted_iota(
        jnp.int32, (sel, sel), 1
    )
    picked = jnp.sum(jnp.where(same, wide, 0.0), axis=1, keepdims=True)
    return rotation((picked + start.astype(f32)) * frequency)


def fetch(sources, targets, sems):
    copies = [
        pltpu.make_async_copy(source, target, sems.at[i])
        for i, (source, target) in enumerate(zip(sources, targets))
    ]
    for copy in copies:
        copy.start()
    return copies


def pack_pool(chunk_ref, pool_ref, angles):
    pages = pool_ref.shape[0]
    pair = pool_ref.shape[1] // PAGE
    half = pair // 2
    for u in range(PAGE):
        keys = slice(u * pair, u * pair + half)
        values = slice(u * pair + half, (u + 1) * pair)
        chunk_ref[:pages, keys] = turned(pool_ref[:, keys].astype(f32), *angles).astype(bf16)
        chunk_ref[:pages, values] = pool_ref[:, values]


def pack_fresh(chunk_ref, fresh_ref, kv_ref, angles):
    sel, pair = kv_ref.shape
    half = pair // 2
    extra = fresh_ref.shape[0] // PAGE
    pages = chunk_ref.shape[0] - extra
    fresh_ref[sel:, :] = jnp.zeros((fresh_ref.shape[0] - sel, pair), f32)
    fresh_ref[:sel, :half] = turned(kv_ref[:, :half].astype(f32), *angles)
    fresh_ref[:sel, half:] = kv_ref[:, half:].astype(f32)
    for u in range(PAGE):
        chunk_ref[pages:, u * pair : (u + 1) * pair] = fresh_ref[
            u * extra : (u + 1) * extra, :
        ].astype(bf16)


def holding(facts_ref, slots, source, pages):
    seq_count = slots.shape[1]
    spot = lax.broadcasted_iota(jnp.int32, (pages, seq_count), 0) * seq_count + source
    low = slots * pages
    held = jnp.where(jnp.logical_and(spot >= low, spot < low + pages), 1.0, 0.0)
    return jnp.dot(
        held,
        facts_ref[:seq_count, :],
        precision=lax.Precision.HIGHEST,
        preferred_element_type=f32,
    )


def pool_rotation(facts_ref, seq_count, query_rows, source, pages):
    table, limit, slot, _ = fact_rows(seq_count, query_rows, facts_ref.shape[1])
    slots = get_rows(facts_ref, table + limit, slot)[:, :seq_count].astype(jnp.int32)
    frequency = get_rows(facts_ref, table + limit + slot, 1)
    facts = holding(facts_ref, slots, source, pages)
    at = facts.shape[1] - 2
    return rotation((facts[:, at : at + 1] - pages * PAGE) * frequency)


def plan_kernel(seq_count, tokens, *refs):
    sources, outputs, targets = refs[:9], refs[9:14], refs[14:22]
    fresh_ref, heads_ref, sems = refs[22:]
    queries_ref, facts_ref, angles_ref, chunk_ref, page_table_ref = outputs
    for copy in fetch(sources, (*targets, page_table_ref), sems):
        copy.wait()
    slot_ref, order_ref, start_ref, freq_ref, picked_ref, kv_ref, q_ref, pool_ref = targets
    me = lax.axis_index("seq")
    sel = q_ref.shape[0]
    head_dim = freq_ref.shape[1]
    pages = pool_ref.shape[0]

    row = picked_ref[pl.ds(me, 1), :]
    fresh_angles = fresh_rotation(row, start_ref[me], freq_ref[...])
    for h in range(GROUP):
        head = q_ref[:, h * head_dim : (h + 1) * head_dim].astype(f32)
        heads_ref[h * sel : (h + 1) * sel, :] = turned(head, *fresh_angles)
    queries_ref[...] = heads_ref[...].astype(bf16)

    other = me + 1 - 2 * (me % 2)
    ours = (row + me * tokens).astype(f32)
    theirs = (picked_ref[pl.ds(other, 1), :] + other * tokens).astype(f32)
    both = jnp.concatenate([ours] * GROUP + [theirs] * GROUP, axis=1)
    at = put_rows(facts_ref, seq_count, both)

    shape = (seq_count, facts_ref.shape[1])
    lanes = lax.broadcasted_iota(jnp.int32, shape, 1)
    passages = lax.broadcasted_iota(jnp.int32, shape, 0)

    def start(k, rows):
        return jnp.where(passages == k, start_ref[k] + tokens, rows)

    starts = lax.fori_loop(0, seq_count, start, jnp.zeros(shape, jnp.int32), unroll=16)
    last = jnp.where(lanes == shape[1] - 1, (passages + 1) * tokens, starts).astype(f32)
    facts_ref[:seq_count, :] = jnp.where(lanes >= shape[1] - 2, last, FAR)
    facts_ref[:seq_count, :sel] = picked_ref[...].astype(f32)

    lanes = lax.broadcasted_iota(jnp.int32, (1, round_up(seq_count, shape[1])), 1)

    def slot(k, row):
        return jnp.where(lanes == k, slot_ref[order_ref[k]], row)

    slots = lax.fori_loop(0, seq_count, slot, jnp.zeros(lanes.shape, jnp.int32), unroll=16)
    at = put_rows(facts_ref, at, slots.astype(f32))
    put_rows(facts_ref, at, freq_ref[...])

    cosine, sine = pool_rotation(facts_ref, seq_count, queries_ref.shape[0], me, pages)
    angles_ref[:pages, :] = cosine
    angles_ref[pages:, :] = sine
    pack_pool(chunk_ref, pool_ref, (cosine, sine))
    pack_fresh(chunk_ref, fresh_ref, kv_ref, fresh_angles)


def merge_kernel(seq_count, query_rows, step, pool_ref, block_ref, facts_ref, angles_ref, chunk_ref):
    pages = pool_ref.shape[0]
    if pages % seq_count:
        me = lax.axis_index("seq")
        here = ring_place(me // 2, seq_count // 2)
        source = chunk_source(here, step, seq_count, me % 2)
        angles = pool_rotation(facts_ref, seq_count, query_rows, source, pages)
    else:
        angles = angles_ref[:pages, :], angles_ref[pages:, :]
    pack_pool(chunk_ref, pool_ref, angles)
    chunk_ref[pages:, :] = block_ref[...]


def chunk_source(here, step, seq_count, core):
    chips = seq_count // 2
    return ring_chip((here - step + chips) % chips, chips) * 2 + core


def put_rows(ref, at, row):
    width = ref.shape[1]
    for i in range(row.shape[1] // width):
        ref[at + i : at + i + 1, :] = row[:, i * width : (i + 1) * width]
    return at + row.shape[1] // width


def get_rows(ref, at, count):
    return jnp.concatenate([ref[at + i : at + i + 1, :] for i in range(count)], axis=1)


def fact_rows(seq_count, query_rows, width):
    return seq_count, 2 * query_rows // width, round_up(seq_count, width) // width, 1


def fresh_places(facts_ref, source, extra, tokens):
    row = jnp.broadcast_to(facts_ref[pl.ds(source, 1), :], (extra * PAGE, facts_ref.shape[1]))
    same = lax.broadcasted_iota(jnp.int32, row.shape, 0) == lax.broadcasted_iota(
        jnp.int32, row.shape, 1
    )
    fresh = jnp.sum(jnp.where(same, row, 0.0), axis=1, keepdims=True)
    return fresh + (source * tokens).astype(f32)


def cached_places(source, shared, seq_count, pages):
    spot = lax.broadcasted_iota(jnp.int32, (pages, 1), 0) * seq_count + source
    spot = spot.astype(f32)
    page = spot - pages * jnp.floor((spot + 0.5) * (1.0 / pages))
    begin = shared[:, shared.shape[1] - 1 :] - pages * PAGE + page * PAGE
    holder = jnp.floor(shared * (1.0 / PAGE))
    bits = jnp.where(holder == page, jnp.exp2(shared - PAGE * holder), 0.0)
    bits = jnp.sum(bits, axis=1, keepdims=True).astype(jnp.int32)
    return [jnp.where(((bits >> u) & 1) == 1, FAR, begin + u) for u in range(PAGE)]


def read_places(seq_count, tokens, arrivals, core, extra, facts_ref, query_rows):
    pages = tokens // PAGE
    here = ring_place(lax.axis_index("seq") // 2, seq_count // 2)
    table_rows, limit_rows, slot_rows, _ = fact_rows(seq_count, query_rows, facts_ref.shape[1])
    slots = get_rows(facts_ref, table_rows + limit_rows, slot_rows)[:, :seq_count].astype(jnp.int32)
    parts, shared = [], None
    for pool_step, fresh_steps in arrivals:
        groups = []
        if pool_step is not None:
            source = chunk_source(here, pool_step, seq_count, core)
            if shared is None or pages % seq_count:
                shared = holding(facts_ref, slots, source, pages)
            groups.append(cached_places(source, shared, seq_count, pages))
        for step in fresh_steps:
            if step is None:
                groups.append([jnp.full((extra, 1), FAR, f32)] * PAGE)
            else:
                source = chunk_source(here, step, seq_count, core)
                fresh = fresh_places(facts_ref, source, extra, tokens)
                groups.append([fresh[u * extra : (u + 1) * extra, :] for u in range(PAGE)])
        for u in range(PAGE):
            parts += [group[u] for group in groups]
    return jnp.concatenate(parts, axis=0)


def read_rows(pieces):
    parts = []
    for piece in pieces:
        width = piece.shape[1] // PAGE
        parts += [piece[:, u * width : (u + 1) * width] for u in range(PAGE)]
    return jnp.concatenate(parts, axis=0)


def read_limit(facts_ref, seq_count, query_rows):
    table_rows, limit_rows, _, _ = fact_rows(seq_count, query_rows, facts_ref.shape[1])
    return get_rows(facts_ref, table_rows, limit_rows)


def score_factor(head_dim):
    return float(head_dim**-0.5 * np.log2(np.e))


def attend(blended, flipped, place, queries, limit, old):
    head_dim = queries.shape[1]
    factor = score_factor(head_dim)
    scores = lax.dot_general(
        blended[:, :head_dim], queries, (((1,), (1,)), ((), ())), preferred_element_type=f32
    )
    scores = jnp.where(place <= limit, scores, MASKED)
    peak = jnp.maximum(jnp.max(scores, axis=0, keepdims=True), LOWEST if old is None else old[0])
    weights = jnp.exp2((scores - peak) * factor)
    total = jnp.sum(weights, axis=0, keepdims=True)
    mixed = jnp.dot(flipped, weights.astype(bf16), preferred_element_type=f32)
    if old is not None:
        fade = jnp.exp2((old[0] - peak) * factor)
        total = total + old[1] * fade
        mixed = mixed + old[2] * fade
    return peak, total, mixed


def chosen(place, wanted):
    return jnp.where(place == wanted, 1.0, 0.0).astype(bf16)


def get_state(ref):
    head_dim = ref.shape[0] - 8
    peak = ref[head_dim : head_dim + 1, :]
    total = ref[head_dim + 1 : head_dim + 2, :]
    return peak, total, ref[:head_dim, :]


def put_state(state, half, ref):
    peak, total, mixed = state
    head_dim = mixed.shape[0]
    tail = jnp.concatenate([peak, total, jnp.zeros((6, peak.shape[1]), f32)], axis=0)
    count = ref.shape[1]
    if half == 1:
        mixed, tail = pltpu.roll(mixed, count, 1), pltpu.roll(tail, count, 1)
    ref[:head_dim, :] = mixed[:, :count]
    ref[head_dim:, :] = tail[:, :count]


def put_pages(picked, ref, *others):
    count = ref.shape[0]
    pair = picked.shape[1]
    for u in range(PAGE):
        part = picked[u * count : (u + 1) * count, :]
        for other in others:
            part = part + other[:, u * pair : (u + 1) * pair].astype(f32)
        ref[:, u * pair : (u + 1) * pair] = part.astype(bf16)


def visit_kernel(seq_count, tokens, extra, arrivals, first, last, *refs):
    pieces, refs = refs[: len(arrivals)], refs[len(arrivals) :]
    own_q, other_q, facts_ref, wanted_ref = refs[:4]
    refs = refs[4:]
    old = None
    if not first:
        old, old_pages = get_state(refs[0]), refs[1]
        refs = refs[2:]
    core = lax.axis_index("seq") % 2
    query_rows = own_q.shape[0]
    place = read_places(seq_count, tokens, arrivals, core, extra, facts_ref, query_rows)
    blended = read_rows(pieces)
    limit = read_limit(facts_ref, seq_count, query_rows)
    queries = jnp.concatenate([own_q[...], other_q[...]], axis=0)
    flipped = blended.T
    state = attend(blended, flipped[own_q.shape[1] :, :], place, queries, limit, old)
    picked = jnp.dot(flipped, chosen(place, wanted_ref[...]), preferred_element_type=f32)
    if not first:
        picked = picked + old_pages[...].astype(f32)
    if not last:
        put_state(state, 0, refs[0])
        refs[1][...] = picked.astype(bf16)
    else:
        turned_pages = picked.T
        for half in (0, 1):
            put_state(state, half, refs[2 * half])
            put_pages(turned_pages[half * tokens : (half + 1) * tokens, :], refs[2 * half + 1])


def close_kernel(seq_count, tokens, extra, arrivals, *refs):
    pieces, refs = refs[: len(arrivals)], refs[len(arrivals) :]
    own_q, facts_ref, wanted_ref, mine, my_pages = refs[:5]
    new, new_pages, next_place, next_chosen = refs[5:]
    core = lax.axis_index("seq") % 2
    query_rows, head_dim = own_q.shape
    place = read_places(seq_count, tokens, arrivals, core, extra, facts_ref, query_rows)
    blended = read_rows(pieces)
    limit = read_limit(facts_ref, seq_count, query_rows)[:, :query_rows]
    wanted = wanted_ref[:, :tokens]
    state = attend(
        blended, blended[:, head_dim:].T, place, own_q[...], limit, get_state(mine)
    )
    put_state(state, 0, new)
    picked = jnp.dot(chosen(place, wanted).T, blended, preferred_element_type=f32)
    put_pages(picked, new_pages, my_pages)

    place = read_places(seq_count, tokens, arrivals, 1 - core, extra, facts_ref, query_rows)
    next_place[...] = jnp.broadcast_to(place, next_place.shape)
    next_chosen[...] = chosen(place, wanted).T


def finish_kernel(seq_count, tokens, extra, arrivals, *refs):
    pieces, refs = refs[: len(arrivals)], refs[len(arrivals) :]
    own_q, facts_ref, mine, my_pages, place_ref, chosen_ref, got, got_pages = refs[:8]
    out_ref, pages_ref, out_scratch, pages_scratch, sems = refs[8:]
    query_rows, head_dim = own_q.shape
    limit = read_limit(facts_ref, seq_count, query_rows)[:, :query_rows]
    blended = read_rows(pieces)
    picked = jnp.dot(chosen_ref[...], blended, preferred_element_type=f32)
    put_pages(picked, pages_scratch, my_pages, got_pages)
    pages_copy = pltpu.make_async_copy(pages_scratch, pages_ref, sems.at[0])
    pages_copy.start()
    one, two = get_state(mine), get_state(got)
    peak = jnp.maximum(one[0], two[0])
    fades = [jnp.exp2((part[0] - peak) * score_factor(head_dim)) for part in (one, two)]
    old = [peak] + [one[i] * fades[0] + two[i] * fades[1] for i in (1, 2)]
    _, total, mixed = attend(
        blended, blended[:, head_dim:].T, place_ref[:, :1], own_q[...], limit, old
    )
    flat = (mixed * (1.0 / total)).T
    sel = out_ref.shape[0]
    for h in range(GROUP):
        out_scratch[:, h * head_dim : (h + 1) * head_dim] = flat[
            h * sel : (h + 1) * sel, :
        ].astype(bf16)
    out_copy = pltpu.make_async_copy(out_scratch, out_ref, sems.at[1])
    out_copy.start()
    pages_copy.wait()
    out_copy.wait()


def shards(
    pool_kv, pool_slot, passage_order, passage_start, recompute_pos, page_table, fresh_q, fresh_kv
):
    seq_count = lax.axis_size("seq")
    chips = seq_count // 2
    me = lax.axis_index("seq")
    pages, width = pool_kv.shape
    sel = fresh_q.shape[0]
    head_dim = fresh_kv.shape[1] // 2
    tokens = pages * PAGE
    extra = round_up(-(-sel // PAGE), TILE)
    rows = pages + extra
    query_rows = sel * GROUP
    vmem = pl.BlockSpec(memory_space=pltpu.VMEM)
    params = pltpu.CompilerParams(vmem_limit_bytes=40 * 2**20)

    anywhere = pl.BlockSpec(memory_space=pltpu.HBM)
    frequency = jnp.asarray(frequencies(head_dim))

    swap = [(i, i ^ 1) for i in range(seq_count)]
    forward, backward = ring_pairs(chips, 1), ring_pairs(chips, -1)
    ahead = lax.ppermute(pool_kv, "seq", forward)
    behind = lax.ppermute(pool_kv, "seq", backward)

    fact_width = round_up(sel + 2, LANES)
    fact_count = round_up(sum(fact_rows(seq_count, query_rows, fact_width)), 8)
    chunk_shape = jax.ShapeDtypeStruct((rows, width), bf16)
    in_smem = [pool_slot, passage_order, passage_start]
    in_vmem = [frequency, recompute_pos, fresh_kv, fresh_q, pool_kv]
    in_all = [*in_smem, *in_vmem, page_table]
    queries, facts, angles, chunk, page_table = pl.pallas_call(
        partial(plan_kernel, seq_count, tokens),
        out_shape=(
            jax.ShapeDtypeStruct((query_rows, head_dim), bf16),
            jax.ShapeDtypeStruct((fact_count, fact_width), f32),
            jax.ShapeDtypeStruct((2 * pages, head_dim), f32),
            chunk_shape,
            jax.ShapeDtypeStruct(page_table.shape, page_table.dtype),
        ),
        in_specs=[anywhere] * 9,
        out_specs=(vmem,) * 5,
        scratch_shapes=[
            *[pltpu.SMEM(x.shape, x.dtype) for x in in_smem],
            *[pltpu.VMEM(x.shape, x.dtype) for x in in_vmem],
            pltpu.VMEM((extra * PAGE, 2 * head_dim), f32),
            pltpu.VMEM((query_rows, head_dim), f32),
            pltpu.SemaphoreType.DMA((9,)),
        ],
        compiler_params=params,
        cost_estimate=pl.CostEstimate(flops=10**8, bytes_accessed=6 * 2**20, transcendentals=0),
        name="plan",
    )(*[pltpu.with_memory_space_constraint(x, pltpu.HBM) for x in in_all])

    def merge(step, pool_part, block):
        return pl.pallas_call(
            partial(merge_kernel, seq_count, query_rows, step),
            out_shape=chunk_shape,
            in_specs=[vmem] * 4,
            out_specs=vmem,
            compiler_params=params,
            cost_estimate=pl.CostEstimate(flops=10**7, bytes_accessed=2**20, transcendentals=0),
            name="merge",
        )(pool_part, block, facts, angles)

    pair = jnp.stack([me, me ^ 1])
    page_ids = jnp.arange(pages, dtype=jnp.int32)
    request_pages = jnp.arange(page_table.shape[0], dtype=jnp.int32)
    owned = pair[:, None] * pages + page_ids[None, :]
    wanted = jnp.sum(
        jnp.where(page_table[None, None, :] == owned[:, :, None], request_pages[None, None, :], 0),
        axis=2,
    )
    wanted = wanted[:, None, :] * PAGE + jnp.arange(PAGE, dtype=jnp.int32)[None, :, None]
    wanted = wanted.astype(f32).reshape(1, 2 * tokens)

    other_queries = lax.ppermute(queries, "seq", swap)

    state_shapes = (
        jax.ShapeDtypeStruct((head_dim + 8, 2 * query_rows), f32),
        jax.ShapeDtypeStruct((2 * head_dim, 2 * tokens), bf16),
    )
    half_shapes = (
        jax.ShapeDtypeStruct((head_dim + 8, query_rows), f32),
        jax.ShapeDtypeStruct((pages, width), bf16),
    )
    close_shapes = half_shapes + (
        jax.ShapeDtypeStruct((PAGE * (rows + extra), LANES), f32),
        jax.ShapeDtypeStruct((tokens, PAGE * (rows + extra)), bf16),
    )
    out_shapes = (
        jax.ShapeDtypeStruct((sel, GROUP * head_dim), bf16),
        jax.ShapeDtypeStruct((pages, width), bf16),
    )

    def run(kernel, arrivals, operands, out_shape, name, aliases=(), weight=1, scratch=()):
        layout = [(pool_step, fresh_steps) for pool_step, fresh_steps, _ in arrivals]
        pieces = [piece for _, _, piece in arrivals]
        operands = pieces + list(operands)
        keys = PAGE * sum(piece.shape[0] for piece in pieces)
        pairs = keys * (query_rows + tokens)
        return pl.pallas_call(
            partial(kernel, seq_count, tokens, extra, layout),
            out_shape=out_shape,
            in_specs=[vmem] * len(operands),
            out_specs=(anywhere if scratch else vmem,) * len(out_shape),
            scratch_shapes=scratch,
            input_output_aliases={len(operands) - 2 + i: i for i in aliases},
            compiler_params=params,
            cost_estimate=pl.CostEstimate(
                flops=8 * pairs * head_dim * weight,
                bytes_accessed=4 * 2**20 * weight,
                transcendentals=2 * pairs * weight,
            ),
            name=name,
        )(*operands)

    def visit(state, arrivals, last=False):
        operands = [queries, other_queries, facts, wanted]
        first = state is None
        kernel = lambda count, size, more, layout, *refs: visit_kernel(
            count, size, more, layout, first, last, *refs
        )
        if not first:
            operands += list(state)
        out_shape = half_shapes * 2 if last else state_shapes
        aliases = () if first or last else (0, 1)
        return run(kernel, arrivals, operands, out_shape, "visit", aliases)

    half = chips // 2
    own_block = chunk[pages:]
    block = lax.ppermute(own_block, "seq", backward)
    ahead, behind = merge(1, ahead, own_block), merge(-1, behind, block)
    behind, other_queries = lax.optimization_barrier((behind, other_queries))
    state = visit(None, [(0, (0,), chunk)])
    arrivals = [(1, (None,), ahead), (-1, (-1,), behind)]
    for step in range(2, half):
        ahead = lax.ppermute(ahead, "seq", forward)
        behind = lax.ppermute(behind, "seq", backward)
        state = visit(state, arrivals)
        behind, state = lax.optimization_barrier((behind, state))
        arrivals = [(step, (step - 1,), ahead), (-step, (-step,), behind)]
    farthest = lax.ppermute(behind, "seq", backward)
    fresh_left = lax.ppermute(ahead[pages:], "seq", forward)
    mine, my_pages, theirs, their_pages = visit(state, arrivals, last=True)
    got = lax.ppermute(theirs, "seq", swap)
    got_pages = lax.ppermute(their_pages, "seq", swap)
    other_farthest = lax.ppermute(farthest, "seq", swap)
    other_fresh = lax.ppermute(fresh_left, "seq", swap)
    operands = [queries, facts, wanted, mine, my_pages]
    *state, place, choice = run(
        close_kernel, [(half, (half,), farthest), (None, (half - 1,), fresh_left)], operands, close_shapes, "close", weight=10
    )
    scratch = [pltpu.VMEM(x.shape, x.dtype) for x in out_shapes]
    scratch.append(pltpu.SemaphoreType.DMA((2,)))
    operands = [queries, facts, *state, place, choice, got, got_pages]
    return run(
        finish_kernel, [(half, (half,), other_farthest), (None, (half - 1,), other_fresh)], operands, out_shapes, "finish",
        scratch=scratch,
    )


def solution(mesh):
    placed = (
        P(("groups", "seq"), None),
        P("groups"),
        P("groups"),
        P("groups"),
        P("groups", None),
        P("groups"),
        P(("groups", "seq"), None),
        P(("groups", "seq"), None),
    )
    return jax.shard_map(
        shards,
        mesh=mesh,
        in_specs=placed,
        out_specs=(P(("groups", "seq"), None), P(("groups", "seq"), None)),
        check_vma=False,
    )
```

time: 32.6 us -> 31.9 us (0.979)
  waiting for transfers between devices: 8.29 us -> 5.83 us
  starting transfers between devices: 9.59 us -> 11.9 us
  Pallas kernels: 13.3 us -> 12.7 us
    ppermute x3 -> x2, waiting for transfers between devices: 5.97 us -> 0.01 us  [shards(): ahead = lax.ppermute(ahead, 'seq', forward)]
    ppermute x3 -> x2, starting transfers between devices: 6.41 us -> 1.11 us  [shards(): ahead = lax.ppermute(ahead, 'seq', forward)]
    ppermute x1 -> x6, starting transfers between devices: 1.83 us -> 7.1 us  [the longest x1 2.99 us: shards(): behind = lax.ppermute(pool_kv, 'seq', backward)]
    ppermute x3 -> x2, waiting for transfers between devices: 0.01 us -> 2.74 us  [shards(): behind = lax.ppermute(behind, 'seq', backward)]
    ppermute x3 -> x2, starting transfers between devices: 0.72 us -> 3.04 us  [shards(): behind = lax.ppermute(behind, 'seq', backward)]
    ppermute x1 -> x6, waiting for transfers between devices: 1.42 us -> 3.05 us  [the longest x1 1.82 us: shards(): block = lax.ppermute(own_block, 'seq', backward)]
    ppermute x1, waiting for transfers between devices: 0.75 us -> 0.01 us  [shards(): other_queries = lax.ppermute(queries, 'seq', swap)]
    pallas_call x8 -> x9, Pallas kernels: 13.3 us -> 12.7 us  [the longest x6 11 us: run(): pl.pallas_call(partial(kernel, seq_count, tokens, extra, layout), out_sha...]
  transfers between devices with their start and end apart: 11 -> 14, of which waited for: 6 -> 5; matrix products, arithmetic and copies ran while one was open for 2% -> 2% of each run, Pallas kernels for 32% -> 35%
where the time goes in v6:
time: 31.9 us; the launch traced here: 31.7 us
  Pallas kernels  12.7 us (40%)
  starting transfers between devices  11.9 us (37%)
  waiting for transfers between devices  5.83 us (18%)
  between operations  0.76 us (2%)
  other arithmetic  0.46 us (1%)
    pallas_call x6, Pallas kernels, run(): pl.pallas_call(partial(kernel, seq_count, tokens, extra, layout), out_sha...  11 us
    ppermute x2, starting transfers between devices, shards(): behind = lax.ppermute(behind, 'seq', backward)  3.04 us
    ppermute x1, starting transfers between devices, shards(): behind = lax.ppermute(pool_kv, 'seq', backward)  2.99 us
    ppermute x2, waiting for transfers between devices, shards(): behind = lax.ppermute(behind, 'seq', backward)  2.74 us
    ppermute x1, starting transfers between devices, shards(): block = lax.ppermute(own_block, 'seq', backward)  1.93 us
    ppermute x1, waiting for transfers between devices, shards(): block = lax.ppermute(own_block, 'seq', backward)  1.82 us
    ppermute x1, starting transfers between devices, shards(): farthest = lax.ppermute(behind, 'seq', backward)  1.66 us
    pallas_call x1, Pallas kernels, shards(): pl.pallas_call(partial(plan_kernel, seq_count, tokens), out_shape=(jax.Sh...  1.51 us
  transfers between devices with their start and end apart: 14, of which 5 were waited for; matrix products, arithmetic and copies ran while one was open for 2% of the time, Pallas kernels for 35%

profile of v6, /device:TPU:0, one launch (start us, length us, event | category | flops | bytes accessed | tf_op | source)
XLA Modules:
  0.0 31.7 jit_solution(10158723067115285095)
XLA Ops:
  0.6 3.0 %collective-permute-start = (bf16[96,1024]{1,0:T(8,128)(2,1)}, bf16[96,1024]{1,0:T(8,128)(2,1)S(1)}, u32[]{:S(2)}, u32[]{:S(2)}) collective-permute-start(bf16[96,1024]{1,0:T(8,128)(2,1)} %refs_7_.1), channel_id=1, source_target_pairs={{0,2},{1,3},{4,0},{5,1},{8,4},{9,5},{12,8},{13,9},{14,12},{15,13},... | collective-permute-start | bytes 589832 | tf_op jit(solution)/shard_map/ppermute | solution.py:463
  3.6 0.1 collective-permute-start.4
  3.8 1.5 %plan.1 = (bf16[448,128]{1,0:T(8,128)(2,1)S(1)}, f32[32,128]{1,0:T(8,128)S(1)}, f32[192,128]{1,0:T(8,128)S(1)}, bf16[112,1024]{1,0:T(8,128)(2,1)S(1)}, s32[1536]{0:T(1024)S(1)}) custom-call(s32[16]{0:T(128)} %refs_0_.1, s32[16]{0:T(128)} %refs_1_.1, s32[16]{0:T(128)} %refs_2_.1, f32[1,128]{1,0:T(1,128)} %constant.14.clone.refs_3_, s32[16,56]{1,0:T(8,128)} %refs_4_.1, ...), custom_call_target="tpu_custom_call" | custom-call | flops 100000000 | bytes 6291456 | tf_op jit(solution)/shard_map/plan/pallas_call | solution.py:471
  5.3 1.9 %collective-permute-start.1 = (bf16[16,1024]{1,0:T(8,128)(2,1)S(1)}, bf16[16,1024]{1,0:T(8,128)(2,1)S(1)}, u32[]{:S(2)}, u32[]{:S(2)}) collective-permute-start(bf16[16,1024]{1,0:T(8,128)(2,1)S(1)} %slice.6.block_ref), channel_id=1, source_target_pairs={{0,2},{1,3},{4,0},{5,1},{8,4},{9,5},{12,8},{13,9},{14,12},{15,13},... | collective-permute-start | bytes 98312 | tf_op jit(solution)/shard_map/ppermute | solution.py:571
  7.2 0.0 collective-permute-start.2
  7.2 0.1 add_multiply_fusion
  7.3 0.1 iota_add_fusion
  7.4 0.3 select_reduce_fusion
  7.7 1.8 %collective-permute-done.1.block_ref = bf16[16,1024]{1,0:T(8,128)(2,1)S(1)} collective-permute-done((bf16[16,1024]{1,0:T(8,128)(2,1)S(1)}, bf16[16,1024]{1,0:T(8,128)(2,1)S(1)}, u32[]{:S(2)}, u32[]{:S(2)}) %collective-permute-start.1) | collective-permute-done | bytes 32800 | tf_op jit(solution)/shard_map/ppermute | solution.py:571
  9.5 0.1 merge.2.refs_1_
  9.6 1.7 %collective-permute-start.3 = (bf16[112,1024]{1,0:T(8,128)(2,1)S(1)}, bf16[112,1024]{1,0:T(8,128)(2,1)S(1)}, u32[]{:S(2)}, u32[]{:S(2)}) collective-permute-start(bf16[112,1024]{1,0:T(8,128)(2,1)S(1)} %merge.2.refs_1_), channel_id=1, source_target_pairs={{0,2},{1,3},{4,0},{5,1},{8,4},{9,5},{12,8},{13,9},{14,12},{15,13},... | collective-permute-start | bytes 688136 | tf_op jit(solution)/shard_map/ppermute | solution.py:578
  11.4 0.1 convert_element_type.14.refs_4_.refs_5_
  11.4 0.1 merge.3.refs_0_
  11.6 0.4 %collective-permute-start.6 = (bf16[112,1024]{1,0:T(8,128)(2,1)S(1)}, bf16[112,1024]{1,0:T(8,128)(2,1)S(1)}, u32[]{:S(2)}, u32[]{:S(2)}) collective-permute-start(bf16[112,1024]{1,0:T(8,128)(2,1)S(1)} %merge.3.refs_0_), channel_id=1, source_target_pairs={{0,4},{1,5},{4,8},{5,9},{8,12},{9,13},{12,14},{13,15},{14,10},{15,... | collective-permute-start | bytes 688136 | tf_op jit(solution)/shard_map/ppermute | solution.py:577
  12.0 1.3 %visit.4 = (f32[136,896]{1,0:T(8,128)S(1)}, bf16[256,768]{1,0:T(8,128)(2,1)S(1)}) custom-call(bf16[112,1024]{1,0:T(8,128)(2,1)S(1)} %get-tuple-element.29.refs_0_, bf16[448,128]{1,0:T(8,128)(2,1)S(1)} %get-tuple-element.32.refs_1_.refs_2_, bf16[448,128]{1,0:T(8,128)(2,1)S(1)} %collective-permute-done.2.refs_2_.refs_3_, ...), custom_call_target="tpu_custom_call" | custom-call | flops 381681664 | bytes 4194304 | tf_op jit(solution)/shard_map/visit/pallas_call | solution.py:541
  13.3 2.3 %visit.5 = (f32[136,896]{1,0:T(8,128)S(1)}, bf16[256,768]{1,0:T(8,128)(2,1)S(1)}) custom-call(bf16[112,1024]{1,0:T(8,128)(2,1)S(1)} %merge.3.refs_0_, bf16[112,1024]{1,0:T(8,128)(2,1)S(1)} %merge.2.refs_1_, bf16[448,128]{1,0:T(8,128)(2,1)S(1)} %get-tuple-element.32.refs_1_.refs_2_, ...), custom_call_target="tpu_custom_call", output_to_operand_aliasing={{0}: (6, {}), {1}: (7, {})} | custom-call | flops 763363328 | bytes 4194304 | tf_op jit(solution)/shard_map/visit/pallas_call | solution.py:541
  15.6 0.9 %collective-permute-done.3.refs_1_ = bf16[112,1024]{1,0:T(8,128)(2,1)S(1)} collective-permute-done((bf16[112,1024]{1,0:T(8,128)(2,1)S(1)}, bf16[112,1024]{1,0:T(8,128)(2,1)S(1)}, u32[]{:S(2)}, u32[]{:S(2)}) %collective-permute-start.3) | collective-permute-done | bytes 229408 | tf_op jit(solution)/shard_map/ppermute | solution.py:578
  16.5 1.3 %collective-permute-start.5 = (bf16[112,1024]{1,0:T(8,128)(2,1)S(1)}, bf16[112,1024]{1,0:T(8,128)(2,1)S(1)}, u32[]{:S(2)}, u32[]{:S(2)}) collective-permute-start(bf16[112,1024]{1,0:T(8,128)(2,1)S(1)} %collective-permute-done.3.refs_1_), channel_id=1, source_target_pairs={{0,2},{1,3},{4,0},{5,1},{8,4},{9,5},{12,8},{13,9},{14,12},{15,13},... | collective-permute-start | bytes 688136 | tf_op jit(solution)/shard_map/ppermute | solution.py:578
  17.8 0.7 %collective-permute-start.9 = (bf16[112,1024]{1,0:T(8,128)(2,1)S(1)}, bf16[112,1024]{1,0:T(8,128)(2,1)S(1)}, u32[]{:S(2)}, u32[]{:S(2)}) collective-permute-start(bf16[112,1024]{1,0:T(8,128)(2,1)S(1)} %collective-permute-done.6.refs_0_), channel_id=1, source_target_pairs={{0,4},{1,5},{4,8},{5,9},{8,12},{9,13},{12,14},{13,15},{14,10},{15,... | collective-permute-start | bytes 688136 | tf_op jit(solution)/shard_map/ppermute | solution.py:577
  18.5 2.3 %visit.6 = (f32[136,896]{1,0:T(8,128)S(1)}, bf16[256,768]{1,0:T(8,128)(2,1)S(1)}) custom-call(bf16[112,1024]{1,0:T(8,128)(2,1)S(1)} %collective-permute-done.6.refs_0_, bf16[112,1024]{1,0:T(8,128)(2,1)S(1)} %collective-permute-done.3.refs_1_, bf16[448,128]{1,0:T(8,128)(2,1)S(1)} %get-tuple-element.32.refs_1_.refs_2_, ...), custom_call_target="tpu_custom_call", output_to_operand_aliasing={{0}: (6, {}), {1}: (7, {})} | custom-call | flops 763363328 | bytes 4194304 | tf_op jit(solution)/shard_map/visit/pallas_call | solution.py:541
  20.8 1.8 %collective-permute-done.5.refs_1_ = bf16[112,1024]{1,0:T(8,128)(2,1)S(1)} collective-permute-done((bf16[112,1024]{1,0:T(8,128)(2,1)S(1)}, bf16[112,1024]{1,0:T(8,128)(2,1)S(1)}, u32[]{:S(2)}, u32[]{:S(2)}) %collective-permute-start.5) | collective-permute-done | bytes 229408 | tf_op jit(solution)/shard_map/ppermute | solution.py:578
  22.6 1.7 %collective-permute-start.7 = (bf16[112,1024]{1,0:T(8,128)(2,1)S(1)}, bf16[112,1024]{1,0:T(8,128)(2,1)S(1)}, u32[]{:S(2)}, u32[]{:S(2)}) collective-permute-start(bf16[112,1024]{1,0:T(8,128)(2,1)S(1)} %collective-permute-done.5.refs_1_), channel_id=1, source_target_pairs={{0,2},{1,3},{4,0},{5,1},{8,4},{9,5},{12,8},{13,9},{14,12},{15,13},... | collective-permute-start | bytes 688136 | tf_op jit(solution)/shard_map/ppermute | solution.py:582
  24.3 0.4 %collective-permute-start.10 = (bf16[16,1024]{1,0:T(8,128)(2,1)S(1)}, bf16[16,1024]{1,0:T(8,128)(2,1)S(1)}, u32[]{:S(2)}, u32[]{:S(2)}) collective-permute-start(bf16[16,1024]{1,0:T(8,128)(2,1)S(1)} %slice.8), channel_id=1, source_target_pairs={{0,4},{1,5},{4,8},{5,9},{8,12},{9,13},{12,14},{13,15},{14,10},{15,... | collective-permute-start | bytes 98312 | tf_op jit(solution)/shard_map/ppermute | solution.py:583
  24.7 2.2 %visit.7 = (f32[136,448]{1,0:T(8,128)S(1)}, bf16[96,1024]{1,0:T(8,128)(2,1)S(1)}, f32[136,448]{1,0:T(8,128)S(1)}, bf16[96,1024]{1,0:T(8,128)(2,1)S(1)}) custom-call(bf16[112,1024]{1,0:T(8,128)(2,1)S(1)} %collective-permute-done.9.refs_0_, bf16[112,1024]{1,0:T(8,128)(2,1)S(1)} %collective-permute-done.5.refs_1_, ...), custom_call_target="tpu_custom_call" | custom-call | flops 763363328 | bytes 4194304 | tf_op jit(solution)/shard_map/visit/pallas_call | solution.py:541
  26.9 0.1 collective-permute-start.12
  26.9 0.5 %collective-permute-start.13 = (bf16[96,1024]{1,0:T(8,128)(2,1)S(1)}, bf16[96,1024]{1,0:T(8,128)(2,1)S(1)}, u32[]{:S(2)}, u32[]{:S(2)}) collective-permute-start(bf16[96,1024]{1,0:T(8,128)(2,1)S(1)} %get-tuple-element.55), channel_id=1, source_target_pairs={{0,1},{1,0},{2,3},{3,2},{4,5},{5,4},{6,7},{7,6},{8,9},{9,8},{10,11... | collective-permute-start | bytes 589832 | tf_op jit(solution)/shard_map/ppermute | solution.py:586
  27.4 0.8 %collective-permute-done.10.refs_1_ = bf16[16,1024]{1,0:T(8,128)(2,1)S(1)} collective-permute-done((bf16[16,1024]{1,0:T(8,128)(2,1)S(1)}, bf16[16,1024]{1,0:T(8,128)(2,1)S(1)}, u32[]{:S(2)}, u32[]{:S(2)}) %collective-permute-start.10) | collective-permute-done | bytes 32800 | tf_op jit(solution)/shard_map/ppermute | solution.py:583
  28.2 0.4 %collective-permute-done.7.refs_0_ = bf16[112,1024]{1,0:T(8,128)(2,1)S(1)} collective-permute-done((bf16[112,1024]{1,0:T(8,128)(2,1)S(1)}, bf16[112,1024]{1,0:T(8,128)(2,1)S(1)}, u32[]{:S(2)}, u32[]{:S(2)}) %collective-permute-start.7) | collective-permute-done | bytes 229408 | tf_op jit(solution)/shard_map/ppermute | solution.py:582
  28.7 0.1 collective-permute-start.8
  28.7 1.4 %close.1 = (f32[136,448]{1,0:T(8,128)S(1)}, bf16[96,1024]{1,0:T(8,128)(2,1)S(1)}, f32[512,128]{1,0:T(8,128)S(1)}, bf16[384,512]{1,0:T(8,128)(2,1)S(1)}) custom-call(bf16[112,1024]{1,0:T(8,128)(2,1)S(1)} %collective-permute-done.7.refs_0_, bf16[16,1024]{1,0:T(8,128)(2,1)S(1)} %collective-permute-done.10.refs_1_, ...), custom_call_target="tpu_custom_call" | custom-call | flops 4362076160 | bytes 41943040 | tf_op jit(solution)/shard_map/close/pallas_call | solution.py:541
  30.1 0.0 collective-permute-done.8.refs_0_
  30.1 1.6 %finish.1 = (bf16[56,1024]{1,0:T(8,128)(2,1)}, bf16[96,1024]{1,0:T(8,128)(2,1)}) custom-call(bf16[112,1024]{1,0:T(8,128)(2,1)S(1)} %collective-permute-done.8.refs_0_, bf16[16,1024]{1,0:T(8,128)(2,1)S(1)} %collective-permute-done.11.refs_1_, bf16[448,128]{1,0:T(8,128)(2,1)S(1)} %get-tuple-element.32.refs_1_.refs_2_, ...), custom_call_target="tpu_custom_call" | custom-call | flops 436207616 | bytes 4194304 | tf_op jit(solution)/shard_map/finish/pallas_call | solution.py:541
  (13 shorter events, 0.0 us)
Async XLA Ops:
  0.6 8.9 %collective-permute-start = (bf16[96,1024]{1,0:T(8,128)(2,1)}, bf16[96,1024]{1,0:T(8,128)(2,1)S(1)}, u32[]{:S(2)}, u32[]{:S(2)}) collective-permute-start(bf16[96,1024]{1,0:T(8,128)(2,1)} %refs_7_.1), channel_id=1, source_target_pairs={{0,2},{1,3},{4,0},{5,1},{8,4},{9,5},{12,8},{13,9},{14,12},{15,13},... | collective-permute-start | bytes 589832 | tf_op jit(solution)/shard_map/ppermute | solution.py:463
  3.6 7.8 %collective-permute-start.4 = (bf16[96,1024]{1,0:T(8,128)(2,1)}, bf16[96,1024]{1,0:T(8,128)(2,1)S(1)}, u32[]{:S(2)}, u32[]{:S(2)}) collective-permute-start(bf16[96,1024]{1,0:T(8,128)(2,1)} %refs_7_.1), channel_id=1, source_target_pairs={{0,4},{1,5},{4,8},{5,9},{8,12},{9,13},{12,14},{13,15},{14,10},{15,... | collective-permute-start | bytes 589832 | tf_op jit(solution)/shard_map/ppermute | solution.py:462
  5.3 4.2 %collective-permute-start.1 = (bf16[16,1024]{1,0:T(8,128)(2,1)S(1)}, bf16[16,1024]{1,0:T(8,128)(2,1)S(1)}, u32[]{:S(2)}, u32[]{:S(2)}) collective-permute-start(bf16[16,1024]{1,0:T(8,128)(2,1)S(1)} %slice.6.block_ref), channel_id=1, source_target_pairs={{0,2},{1,3},{4,0},{5,1},{8,4},{9,5},{12,8},{13,9},{14,12},{15,13},... | collective-permute-start | bytes 98312 | tf_op jit(solution)/shard_map/ppermute | solution.py:571
  7.2 2.4 %collective-permute-start.2 = (bf16[448,128]{1,0:T(8,128)(2,1)S(1)}, bf16[448,128]{1,0:T(8,128)(2,1)S(1)}, u32[]{:S(2)}, u32[]{:S(2)}) collective-permute-start(bf16[448,128]{1,0:T(8,128)(2,1)S(1)} %get-tuple-element.32.refs_1_.refs_2_), channel_id=1, source_target_pairs={{0,1},{1,0},{2,3},{3,2},{4,5},{5,4},{6,7},{7,6},{8,9},{9,8},{10,11... | collective-permute-start | bytes 344072 | tf_op jit(solution)/shard_map/ppermute | solution.py:516
  9.6 6.8 %collective-permute-start.3 = (bf16[112,1024]{1,0:T(8,128)(2,1)S(1)}, bf16[112,1024]{1,0:T(8,128)(2,1)S(1)}, u32[]{:S(2)}, u32[]{:S(2)}) collective-permute-start(bf16[112,1024]{1,0:T(8,128)(2,1)S(1)} %merge.2.refs_1_), channel_id=1, source_target_pairs={{0,2},{1,3},{4,0},{5,1},{8,4},{9,5},{12,8},{13,9},{14,12},{15,13},... | collective-permute-start | bytes 688136 | tf_op jit(solution)/shard_map/ppermute | solution.py:578
  11.6 6.3 %collective-permute-start.6 = (bf16[112,1024]{1,0:T(8,128)(2,1)S(1)}, bf16[112,1024]{1,0:T(8,128)(2,1)S(1)}, u32[]{:S(2)}, u32[]{:S(2)}) collective-permute-start(bf16[112,1024]{1,0:T(8,128)(2,1)S(1)} %merge.3.refs_0_), channel_id=1, source_target_pairs={{0,4},{1,5},{4,8},{5,9},{8,12},{9,13},{12,14},{13,15},{14,10},{15,... | collective-permute-start | bytes 688136 | tf_op jit(solution)/shard_map/ppermute | solution.py:577
  16.5 6.1 %collective-permute-start.5 = (bf16[112,1024]{1,0:T(8,128)(2,1)S(1)}, bf16[112,1024]{1,0:T(8,128)(2,1)S(1)}, u32[]{:S(2)}, u32[]{:S(2)}) collective-permute-start(bf16[112,1024]{1,0:T(8,128)(2,1)S(1)} %collective-permute-done.3.refs_1_), channel_id=1, source_target_pairs={{0,2},{1,3},{4,0},{5,1},{8,4},{9,5},{12,8},{13,9},{14,12},{15,13},... | collective-permute-start | bytes 688136 | tf_op jit(solution)/shard_map/ppermute | solution.py:578
  17.8 6.5 %collective-permute-start.9 = (bf16[112,1024]{1,0:T(8,128)(2,1)S(1)}, bf16[112,1024]{1,0:T(8,128)(2,1)S(1)}, u32[]{:S(2)}, u32[]{:S(2)}) collective-permute-start(bf16[112,1024]{1,0:T(8,128)(2,1)S(1)} %collective-permute-done.6.refs_0_), channel_id=1, source_target_pairs={{0,4},{1,5},{4,8},{5,9},{8,12},{9,13},{12,14},{13,15},{14,10},{15,... | collective-permute-start | bytes 688136 | tf_op jit(solution)/shard_map/ppermute | solution.py:577
  22.6 6.0 %collective-permute-start.7 = (bf16[112,1024]{1,0:T(8,128)(2,1)S(1)}, bf16[112,1024]{1,0:T(8,128)(2,1)S(1)}, u32[]{:S(2)}, u32[]{:S(2)}) collective-permute-start(bf16[112,1024]{1,0:T(8,128)(2,1)S(1)} %collective-permute-done.5.refs_1_), channel_id=1, source_target_pairs={{0,2},{1,3},{4,0},{5,1},{8,4},{9,5},{12,8},{13,9},{14,12},{15,13},... | collective-permute-start | bytes 688136 | tf_op jit(solution)/shard_map/ppermute | solution.py:582
  24.3 3.9 %collective-permute-start.10 = (bf16[16,1024]{1,0:T(8,128)(2,1)S(1)}, bf16[16,1024]{1,0:T(8,128)(2,1)S(1)}, u32[]{:S(2)}, u32[]{:S(2)}) collective-permute-start(bf16[16,1024]{1,0:T(8,128)(2,1)S(1)} %slice.8), channel_id=1, source_target_pairs={{0,4},{1,5},{4,8},{5,9},{8,12},{9,13},{12,14},{13,15},{14,10},{15,... | collective-permute-start | bytes 98312 | tf_op jit(solution)/shard_map/ppermute | solution.py:583
  26.9 3.3 %collective-permute-start.12 = (f32[136,448]{1,0:T(8,128)S(1)}, f32[136,448]{1,0:T(8,128)S(1)}, u32[]{:S(2)}, u32[]{:S(2)}) collective-permute-start(f32[136,448]{1,0:T(8,128)S(1)} %get-tuple-element.54), channel_id=1, source_target_pairs={{0,1},{1,0},{2,3},{3,2},{4,5},{5,4},{6,7},{7,6},{8,9},{9,8},{10,11... | collective-permute-start | bytes 731144 | tf_op jit(solution)/shard_map/ppermute | solution.py:585
  26.9 3.2 %collective-permute-start.13 = (bf16[96,1024]{1,0:T(8,128)(2,1)S(1)}, bf16[96,1024]{1,0:T(8,128)(2,1)S(1)}, u32[]{:S(2)}, u32[]{:S(2)}) collective-permute-start(bf16[96,1024]{1,0:T(8,128)(2,1)S(1)} %get-tuple-element.55), channel_id=1, source_target_pairs={{0,1},{1,0},{2,3},{3,2},{4,5},{5,4},{6,7},{7,6},{8,9},{9,8},{10,11... | collective-permute-start | bytes 589832 | tf_op jit(solution)/shard_map/ppermute | solution.py:586
  28.2 1.9 %collective-permute-start.11 = (bf16[16,1024]{1,0:T(8,128)(2,1)S(1)}, bf16[16,1024]{1,0:T(8,128)(2,1)S(1)}, u32[]{:S(2)}, u32[]{:S(2)}) collective-permute-start(bf16[16,1024]{1,0:T(8,128)(2,1)S(1)} %collective-permute-done.10.refs_1_), channel_id=1, source_target_pairs={{0,1},{1,0},{2,3},{3,2},{4,5},{5,4},{6,7},{7,6},{8,9},{9,8},{10,11... | collective-permute-start | bytes 98312 | tf_op jit(solution)/shard_map/ppermute | solution.py:588
  28.7 1.5 %collective-permute-start.8 = (bf16[112,1024]{1,0:T(8,128)(2,1)S(1)}, bf16[112,1024]{1,0:T(8,128)(2,1)S(1)}, u32[]{:S(2)}, u32[]{:S(2)}) collective-permute-start(bf16[112,1024]{1,0:T(8,128)(2,1)S(1)} %collective-permute-done.7.refs_0_), channel_id=1, source_target_pairs={{0,1},{1,0},{2,3},{3,2},{4,5},{5,4},{6,7},{7,6},{8,9},{9,8},{10,11... | collective-permute-start | bytes 688136 | tf_op jit(solution)/shard_map/ppermute | solution.py:587

commit v7 on v6

--- a/solution.py
+++ b/solution.py
@@ -570,6 +570,7 @@
     own_block = chunk[pages:]
     block = lax.ppermute(own_block, "seq", backward)
     ahead, behind = merge(1, ahead, own_block), merge(-1, behind, block)
+    ahead, other_queries = lax.optimization_barrier((ahead, other_queries))
     behind, other_queries = lax.optimization_barrier((behind, other_queries))
     state = visit(None, [(0, (0,), chunk)])
     arrivals = [(1, (None,), ahead), (-1, (-1,), behind)]
@@ -577,24 +578,24 @@
         ahead = lax.ppermute(ahead, "seq", forward)
         behind = lax.ppermute(behind, "seq", backward)
         state = visit(state, arrivals)
-        behind, state = lax.optimization_barrier((behind, state))
+        ahead, state = lax.optimization_barrier((ahead, state))
         arrivals = [(step, (step - 1,), ahead), (-step, (-step,), behind)]
-    farthest = lax.ppermute(behind, "seq", backward)
-    fresh_left = lax.ppermute(ahead[pages:], "seq", forward)
+    farthest = lax.ppermute(ahead, "seq", forward)
+    fresh_farthest = lax.ppermute(behind[pages:], "seq", backward)
     mine, my_pages, theirs, their_pages = visit(state, arrivals, last=True)
     got = lax.ppermute(theirs, "seq", swap)
     got_pages = lax.ppermute(their_pages, "seq", swap)
     other_farthest = lax.ppermute(farthest, "seq", swap)
-    other_fresh = lax.ppermute(fresh_left, "seq", swap)
+    other_fresh = lax.ppermute(fresh_farthest, "seq", swap)
     operands = [queries, facts, wanted, mine, my_pages]
     *state, place, choice = run(
-        close_kernel, [(half, (half,), farthest), (None, (half - 1,), fresh_left)], operands, close_shapes, "close", weight=10
+        close_kernel, [(half, (half - 1,), farthest), (None, (half,), fresh_farthest)], operands, close_shapes, "close", weight=10
     )
     scratch = [pltpu.VMEM(x.shape, x.dtype) for x in out_shapes]
     scratch.append(pltpu.SemaphoreType.DMA((2,)))
     operands = [queries, facts, *state, place, choice, got, got_pages]
     return run(
-        finish_kernel, [(half, (half,), other_farthest), (None, (half - 1,), other_fresh)], operands, out_shapes, "finish",
+        finish_kernel, [(half, (half - 1,), other_farthest), (None, (half,), other_fresh)], operands, out_shapes, "finish",
         scratch=scratch,
     )
 

time: 31.9 us -> 31.7 us (level)
  waiting for transfers between devices: 5.83 us -> 3.16 us
  starting transfers between devices: 11.9 us -> 14.4 us
    ppermute x1, starting transfers between devices: 2.99 us -> 0.01 us  [shards(): behind = lax.ppermute(pool_kv, 'seq', backward)]
    ppermute x1, starting transfers between devices: 0.15 us -> 3.08 us  [shards(): ahead = lax.ppermute(pool_kv, 'seq', forward)]
    ppermute x2, waiting for transfers between devices: 2.74 us -> 0.18 us  [shards(): behind = lax.ppermute(behind, 'seq', backward)]
    ppermute x2, starting transfers between devices: 1.11 us -> 3.39 us  [shards(): ahead = lax.ppermute(ahead, 'seq', forward)]
    ppermute x2, waiting for transfers between devices: 0.01 us -> 1.74 us  [shards(): ahead = lax.ppermute(ahead, 'seq', forward)]
    ppermute x1, waiting for transfers between devices: 1.82 us -> 0.16 us  [shards(): block = lax.ppermute(own_block, 'seq', backward)]
    ppermute x2, starting transfers between devices: 3.04 us -> 1.87 us  [shards(): behind = lax.ppermute(behind, 'seq', backward)]
    ppermute x3, waiting for transfers between devices: 1.23 us -> 0.1 us  [the longest x1 0.1 us: shards(): farthest = lax.ppermute(ahead, 'seq', forward)]
  transfers between devices with their start and end apart: 14 -> 14, of which waited for: 5 -> 7; matrix products, arithmetic and copies ran while one was open for 2% -> 2% of each run, Pallas kernels for 35% -> 35%
where the time goes in v7:
time: 31.7 us; the launch traced here: 31.5 us
  starting transfers between devices  14.4 us (45%)
  Pallas kernels  12.7 us (40%)
  waiting for transfers between devices  3.16 us (10%)
  between operations  0.77 us (2%)
  other arithmetic  0.46 us (1%)
    pallas_call x6, Pallas kernels, run(): pl.pallas_call(partial(kernel, seq_count, tokens, extra, layout), out_sha...  11 us
    ppermute x2, starting transfers between devices, shards(): ahead = lax.ppermute(ahead, 'seq', forward)  3.39 us
    ppermute x1, starting transfers between devices, shards(): ahead = lax.ppermute(pool_kv, 'seq', forward)  3.08 us
    ppermute x1, starting transfers between devices, shards(): block = lax.ppermute(own_block, 'seq', backward)  1.99 us
    ppermute x1, starting transfers between devices, shards(): fresh_farthest = lax.ppermute(behind[pages:], 'seq', backward)  1.95 us
    ppermute x2, starting transfers between devices, shards(): behind = lax.ppermute(behind, 'seq', backward)  1.87 us
    ppermute x2, waiting for transfers between devices, shards(): ahead = lax.ppermute(ahead, 'seq', forward)  1.74 us
    pallas_call x1, Pallas kernels, shards(): pl.pallas_call(partial(plan_kernel, seq_count, tokens), out_shape=(jax.Sh...  1.52 us
  transfers between devices with their start and end apart: 14, of which 7 were waited for; matrix products, arithmetic and copies ran while one was open for 2% of the time, Pallas kernels for 35%

profile of v7, /device:TPU:0, one launch (start us, length us, event | category | flops | bytes accessed | tf_op | source)
XLA Modules:
  0.0 31.5 jit_solution(7081689891855600236)
XLA Ops:
  0.6 3.1 %collective-permute-start = (bf16[96,1024]{1,0:T(8,128)(2,1)}, bf16[96,1024]{1,0:T(8,128)(2,1)S(1)}, u32[]{:S(2)}, u32[]{:S(2)}) collective-permute-start(bf16[96,1024]{1,0:T(8,128)(2,1)} %refs_7_.1), channel_id=1, source_target_pairs={{0,4},{1,5},{4,8},{5,9},{8,12},{9,13},{12,14},{13,15},{14,10},{15,... | collective-permute-start | bytes 589832 | tf_op jit(solution)/shard_map/ppermute | solution.py:462
  3.7 1.5 %plan.1 = (bf16[448,128]{1,0:T(8,128)(2,1)S(1)}, f32[32,128]{1,0:T(8,128)S(1)}, f32[192,128]{1,0:T(8,128)S(1)}, bf16[112,1024]{1,0:T(8,128)(2,1)S(1)}, s32[1536]{0:T(1024)S(1)}) custom-call(s32[16]{0:T(128)} %refs_0_.1, s32[16]{0:T(128)} %refs_1_.1, s32[16]{0:T(128)} %refs_2_.1, f32[1,128]{1,0:T(1,128)} %constant.14.clone.refs_3_, s32[16,56]{1,0:T(8,128)} %refs_4_.1, ...), custom_call_target="tpu_custom_call" | custom-call | flops 100000000 | bytes 6291456 | tf_op jit(solution)/shard_map/plan/pallas_call | solution.py:471
  5.2 0.1 collective-permute-start.1
  5.3 2.0 %collective-permute-start.4 = (bf16[16,1024]{1,0:T(8,128)(2,1)S(1)}, bf16[16,1024]{1,0:T(8,128)(2,1)S(1)}, u32[]{:S(2)}, u32[]{:S(2)}) collective-permute-start(bf16[16,1024]{1,0:T(8,128)(2,1)S(1)} %slice.6.block_ref), channel_id=1, source_target_pairs={{0,2},{1,3},{4,0},{5,1},{8,4},{9,5},{12,8},{13,9},{14,12},{15,13},... | collective-permute-start | bytes 98312 | tf_op jit(solution)/shard_map/ppermute | solution.py:571
  7.3 0.1 add_multiply_fusion
  7.4 0.1 iota_add_fusion
  7.5 0.3 select_reduce_fusion
  7.8 1.0 %collective-permute-done.pool_ref = bf16[96,1024]{1,0:T(8,128)(2,1)S(1)} collective-permute-done((bf16[96,1024]{1,0:T(8,128)(2,1)}, bf16[96,1024]{1,0:T(8,128)(2,1)S(1)}, u32[]{:S(2)}, u32[]{:S(2)}) %collective-permute-start) | collective-permute-done | bytes 196640 | tf_op jit(solution)/shard_map/ppermute | solution.py:462
  8.7 0.1 merge.2.refs_0_
  8.9 1.9 %collective-permute-start.2 = (bf16[112,1024]{1,0:T(8,128)(2,1)S(1)}, bf16[112,1024]{1,0:T(8,128)(2,1)S(1)}, u32[]{:S(2)}, u32[]{:S(2)}) collective-permute-start(bf16[112,1024]{1,0:T(8,128)(2,1)S(1)} %merge.2.refs_0_), channel_id=1, source_target_pairs={{0,4},{1,5},{4,8},{5,9},{8,12},{9,13},{12,14},{13,15},{14,10},{15,... | collective-permute-start | bytes 688136 | tf_op jit(solution)/shard_map/ppermute | solution.py:578
  10.7 0.1 convert_element_type.14.refs_4_.refs_5_
  10.8 0.2 collective-permute-done.4.block_ref
  11.0 0.1 merge.3.refs_1_
  11.1 0.4 %collective-permute-start.6 = (bf16[112,1024]{1,0:T(8,128)(2,1)S(1)}, bf16[112,1024]{1,0:T(8,128)(2,1)S(1)}, u32[]{:S(2)}, u32[]{:S(2)}) collective-permute-start(bf16[112,1024]{1,0:T(8,128)(2,1)S(1)} %merge.3.refs_1_), channel_id=1, source_target_pairs={{0,2},{1,3},{4,0},{5,1},{8,4},{9,5},{12,8},{13,9},{14,12},{15,13},... | collective-permute-start | bytes 688136 | tf_op jit(solution)/shard_map/ppermute | solution.py:579
  11.5 1.3 %visit.4 = (f32[136,896]{1,0:T(8,128)S(1)}, bf16[256,768]{1,0:T(8,128)(2,1)S(1)}) custom-call(bf16[112,1024]{1,0:T(8,128)(2,1)S(1)} %get-tuple-element.31.refs_0_, bf16[448,128]{1,0:T(8,128)(2,1)S(1)} %get-tuple-element.34.refs_1_.refs_2_, bf16[448,128]{1,0:T(8,128)(2,1)S(1)} %collective-permute-done.1.refs_2_.refs_3_, ...), custom_call_target="tpu_custom_call" | custom-call | flops 381681664 | bytes 4194304 | tf_op jit(solution)/shard_map/visit/pallas_call | solution.py:541
  12.8 2.3 %visit.5 = (f32[136,896]{1,0:T(8,128)S(1)}, bf16[256,768]{1,0:T(8,128)(2,1)S(1)}) custom-call(bf16[112,1024]{1,0:T(8,128)(2,1)S(1)} %merge.2.refs_0_, bf16[112,1024]{1,0:T(8,128)(2,1)S(1)} %merge.3.refs_1_, bf16[448,128]{1,0:T(8,128)(2,1)S(1)} %get-tuple-element.34.refs_1_.refs_2_, ...), custom_call_target="tpu_custom_call", output_to_operand_aliasing={{0}: (6, {}), {1}: (7, {})} | custom-call | flops 763363328 | bytes 4194304 | tf_op jit(solution)/shard_map/visit/pallas_call | solution.py:541
  15.1 0.6 %collective-permute-done.2.refs_0_ = bf16[112,1024]{1,0:T(8,128)(2,1)S(1)} collective-permute-done((bf16[112,1024]{1,0:T(8,128)(2,1)S(1)}, bf16[112,1024]{1,0:T(8,128)(2,1)S(1)}, u32[]{:S(2)}, u32[]{:S(2)}) %collective-permute-start.2) | collective-permute-done | bytes 229408 | tf_op jit(solution)/shard_map/ppermute | solution.py:578
  15.7 1.5 %collective-permute-start.5 = (bf16[112,1024]{1,0:T(8,128)(2,1)S(1)}, bf16[112,1024]{1,0:T(8,128)(2,1)S(1)}, u32[]{:S(2)}, u32[]{:S(2)}) collective-permute-start(bf16[112,1024]{1,0:T(8,128)(2,1)S(1)} %collective-permute-done.2.refs_0_), channel_id=1, source_target_pairs={{0,4},{1,5},{4,8},{5,9},{8,12},{9,13},{12,14},{13,15},{14,10},{15,... | collective-permute-start | bytes 688136 | tf_op jit(solution)/shard_map/ppermute | solution.py:578
  17.2 0.1 collective-permute-done.6.refs_1_
  17.3 1.5 %collective-permute-start.9 = (bf16[112,1024]{1,0:T(8,128)(2,1)S(1)}, bf16[112,1024]{1,0:T(8,128)(2,1)S(1)}, u32[]{:S(2)}, u32[]{:S(2)}) collective-permute-start(bf16[112,1024]{1,0:T(8,128)(2,1)S(1)} %collective-permute-done.6.refs_1_), channel_id=1, source_target_pairs={{0,2},{1,3},{4,0},{5,1},{8,4},{9,5},{12,8},{13,9},{14,12},{15,13},... | collective-permute-start | bytes 688136 | tf_op jit(solution)/shard_map/ppermute | solution.py:579
  18.8 2.3 %visit.6 = (f32[136,896]{1,0:T(8,128)S(1)}, bf16[256,768]{1,0:T(8,128)(2,1)S(1)}) custom-call(bf16[112,1024]{1,0:T(8,128)(2,1)S(1)} %collective-permute-done.2.refs_0_, bf16[112,1024]{1,0:T(8,128)(2,1)S(1)} %collective-permute-done.6.refs_1_, bf16[448,128]{1,0:T(8,128)(2,1)S(1)} %get-tuple-element.34.refs_1_.refs_2_, ...), custom_call_target="tpu_custom_call", output_to_operand_aliasing={{0}: (6, {}), {1}: (7, {})} | custom-call | flops 763363328 | bytes 4194304 | tf_op jit(solution)/shard_map/visit/pallas_call | solution.py:541
  21.1 1.1 %collective-permute-done.5.refs_0_ = bf16[112,1024]{1,0:T(8,128)(2,1)S(1)} collective-permute-done((bf16[112,1024]{1,0:T(8,128)(2,1)S(1)}, bf16[112,1024]{1,0:T(8,128)(2,1)S(1)}, u32[]{:S(2)}, u32[]{:S(2)}) %collective-permute-start.5) | collective-permute-done | bytes 229408 | tf_op jit(solution)/shard_map/ppermute | solution.py:578
  22.2 1.0 %collective-permute-start.7 = (bf16[112,1024]{1,0:T(8,128)(2,1)S(1)}, bf16[112,1024]{1,0:T(8,128)(2,1)S(1)}, u32[]{:S(2)}, u32[]{:S(2)}) collective-permute-start(bf16[112,1024]{1,0:T(8,128)(2,1)S(1)} %collective-permute-done.5.refs_0_), channel_id=1, source_target_pairs={{0,4},{1,5},{4,8},{5,9},{8,12},{9,13},{12,14},{13,15},{14,10},{15,... | collective-permute-start | bytes 688136 | tf_op jit(solution)/shard_map/ppermute | solution.py:583
  23.2 0.1 collective-permute-done.9.refs_1_
  23.3 1.9 %collective-permute-start.10 = (bf16[16,1024]{1,0:T(8,128)(2,1)S(1)}, bf16[16,1024]{1,0:T(8,128)(2,1)S(1)}, u32[]{:S(2)}, u32[]{:S(2)}) collective-permute-start(bf16[16,1024]{1,0:T(8,128)(2,1)S(1)} %slice.8), channel_id=1, source_target_pairs={{0,2},{1,3},{4,0},{5,1},{8,4},{9,5},{12,8},{13,9},{14,12},{15,13},... | collective-permute-start | bytes 98312 | tf_op jit(solution)/shard_map/ppermute | solution.py:584
  25.3 2.2 %visit.7 = (f32[136,448]{1,0:T(8,128)S(1)}, bf16[96,1024]{1,0:T(8,128)(2,1)S(1)}, f32[136,448]{1,0:T(8,128)S(1)}, bf16[96,1024]{1,0:T(8,128)(2,1)S(1)}) custom-call(bf16[112,1024]{1,0:T(8,128)(2,1)S(1)} %collective-permute-done.5.refs_0_, bf16[112,1024]{1,0:T(8,128)(2,1)S(1)} %collective-permute-done.9.refs_1_, ...), custom_call_target="tpu_custom_call" | custom-call | flops 763363328 | bytes 4194304 | tf_op jit(solution)/shard_map/visit/pallas_call | solution.py:541
  27.5 0.5 %collective-permute-start.13 = (bf16[96,1024]{1,0:T(8,128)(2,1)S(1)}, bf16[96,1024]{1,0:T(8,128)(2,1)S(1)}, u32[]{:S(2)}, u32[]{:S(2)}) collective-permute-start(bf16[96,1024]{1,0:T(8,128)(2,1)S(1)} %get-tuple-element.59), channel_id=1, source_target_pairs={{0,1},{1,0},{2,3},{3,2},{4,5},{5,4},{6,7},{7,6},{8,9},{9,8},{10,11... | collective-permute-start | bytes 589832 | tf_op jit(solution)/shard_map/ppermute | solution.py:587
  28.0 0.1 collective-permute-start.11
  28.1 0.1 collective-permute-done.7.refs_0_
  28.2 0.3 %collective-permute-start.8 = (bf16[112,1024]{1,0:T(8,128)(2,1)S(1)}, bf16[112,1024]{1,0:T(8,128)(2,1)S(1)}, u32[]{:S(2)}, u32[]{:S(2)}) collective-permute-start(bf16[112,1024]{1,0:T(8,128)(2,1)S(1)} %collective-permute-done.7.refs_0_), channel_id=1, source_target_pairs={{0,1},{1,0},{2,3},{3,2},{4,5},{5,4},{6,7},{7,6},{8,9},{9,8},{10,11... | collective-permute-start | bytes 688136 | tf_op jit(solution)/shard_map/ppermute | solution.py:588
  28.6 1.4 %close.1 = (f32[136,448]{1,0:T(8,128)S(1)}, bf16[96,1024]{1,0:T(8,128)(2,1)S(1)}, f32[512,128]{1,0:T(8,128)S(1)}, bf16[384,512]{1,0:T(8,128)(2,1)S(1)}) custom-call(bf16[112,1024]{1,0:T(8,128)(2,1)S(1)} %collective-permute-done.7.refs_0_, bf16[16,1024]{1,0:T(8,128)(2,1)S(1)} %collective-permute-done.10.refs_1_, ...), custom_call_target="tpu_custom_call" | custom-call | flops 4362076160 | bytes 41943040 | tf_op jit(solution)/shard_map/close/pallas_call | solution.py:541
  30.0 1.6 %finish.1 = (bf16[56,1024]{1,0:T(8,128)(2,1)}, bf16[96,1024]{1,0:T(8,128)(2,1)}) custom-call(bf16[112,1024]{1,0:T(8,128)(2,1)S(1)} %collective-permute-done.8.refs_0_, bf16[16,1024]{1,0:T(8,128)(2,1)S(1)} %collective-permute-done.11.refs_1_, bf16[448,128]{1,0:T(8,128)(2,1)S(1)} %get-tuple-element.34.refs_1_.refs_2_, ...), custom_call_target="tpu_custom_call" | custom-call | flops 436207616 | bytes 4194304 | tf_op jit(solution)/shard_map/finish/pallas_call | solution.py:541
  (13 shorter events, 0.1 us)
Async XLA Ops:
  0.6 8.1 %collective-permute-start = (bf16[96,1024]{1,0:T(8,128)(2,1)}, bf16[96,1024]{1,0:T(8,128)(2,1)S(1)}, u32[]{:S(2)}, u32[]{:S(2)}) collective-permute-start(bf16[96,1024]{1,0:T(8,128)(2,1)} %refs_7_.1), channel_id=1, source_target_pairs={{0,4},{1,5},{4,8},{5,9},{8,12},{9,13},{12,14},{13,15},{14,10},{15,... | collective-permute-start | bytes 589832 | tf_op jit(solution)/shard_map/ppermute | solution.py:462
  3.7 7.3 %collective-permute-start.3 = (bf16[96,1024]{1,0:T(8,128)(2,1)}, bf16[96,1024]{1,0:T(8,128)(2,1)S(1)}, u32[]{:S(2)}, u32[]{:S(2)}) collective-permute-start(bf16[96,1024]{1,0:T(8,128)(2,1)} %refs_7_.1), channel_id=1, source_target_pairs={{0,2},{1,3},{4,0},{5,1},{8,4},{9,5},{12,8},{13,9},{14,12},{15,13},... | collective-permute-start | bytes 589832 | tf_op jit(solution)/shard_map/ppermute | solution.py:463
  5.2 3.6 %collective-permute-start.1 = (bf16[448,128]{1,0:T(8,128)(2,1)S(1)}, bf16[448,128]{1,0:T(8,128)(2,1)S(1)}, u32[]{:S(2)}, u32[]{:S(2)}) collective-permute-start(bf16[448,128]{1,0:T(8,128)(2,1)S(1)} %get-tuple-element.34.refs_1_.refs_2_), channel_id=1, source_target_pairs={{0,1},{1,0},{2,3},{3,2},{4,5},{5,4},{6,7},{7,6},{8,9},{9,8},{10,11... | collective-permute-start | bytes 344072 | tf_op jit(solution)/shard_map/ppermute | solution.py:516
  5.3 5.7 %collective-permute-start.4 = (bf16[16,1024]{1,0:T(8,128)(2,1)S(1)}, bf16[16,1024]{1,0:T(8,128)(2,1)S(1)}, u32[]{:S(2)}, u32[]{:S(2)}) collective-permute-start(bf16[16,1024]{1,0:T(8,128)(2,1)S(1)} %slice.6.block_ref), channel_id=1, source_target_pairs={{0,2},{1,3},{4,0},{5,1},{8,4},{9,5},{12,8},{13,9},{14,12},{15,13},... | collective-permute-start | bytes 98312 | tf_op jit(solution)/shard_map/ppermute | solution.py:571
  8.9 6.8 %collective-permute-start.2 = (bf16[112,1024]{1,0:T(8,128)(2,1)S(1)}, bf16[112,1024]{1,0:T(8,128)(2,1)S(1)}, u32[]{:S(2)}, u32[]{:S(2)}) collective-permute-start(bf16[112,1024]{1,0:T(8,128)(2,1)S(1)} %merge.2.refs_0_), channel_id=1, source_target_pairs={{0,4},{1,5},{4,8},{5,9},{8,12},{9,13},{12,14},{13,15},{14,10},{15,... | collective-permute-start | bytes 688136 | tf_op jit(solution)/shard_map/ppermute | solution.py:578
  11.1 6.2 %collective-permute-start.6 = (bf16[112,1024]{1,0:T(8,128)(2,1)S(1)}, bf16[112,1024]{1,0:T(8,128)(2,1)S(1)}, u32[]{:S(2)}, u32[]{:S(2)}) collective-permute-start(bf16[112,1024]{1,0:T(8,128)(2,1)S(1)} %merge.3.refs_1_), channel_id=1, source_target_pairs={{0,2},{1,3},{4,0},{5,1},{8,4},{9,5},{12,8},{13,9},{14,12},{15,13},... | collective-permute-start | bytes 688136 | tf_op jit(solution)/shard_map/ppermute | solution.py:579
  15.7 6.5 %collective-permute-start.5 = (bf16[112,1024]{1,0:T(8,128)(2,1)S(1)}, bf16[112,1024]{1,0:T(8,128)(2,1)S(1)}, u32[]{:S(2)}, u32[]{:S(2)}) collective-permute-start(bf16[112,1024]{1,0:T(8,128)(2,1)S(1)} %collective-permute-done.2.refs_0_), channel_id=1, source_target_pairs={{0,4},{1,5},{4,8},{5,9},{8,12},{9,13},{12,14},{13,15},{14,10},{15,... | collective-permute-start | bytes 688136 | tf_op jit(solution)/shard_map/ppermute | solution.py:578
  17.3 6.0 %collective-permute-start.9 = (bf16[112,1024]{1,0:T(8,128)(2,1)S(1)}, bf16[112,1024]{1,0:T(8,128)(2,1)S(1)}, u32[]{:S(2)}, u32[]{:S(2)}) collective-permute-start(bf16[112,1024]{1,0:T(8,128)(2,1)S(1)} %collective-permute-done.6.refs_1_), channel_id=1, source_target_pairs={{0,2},{1,3},{4,0},{5,1},{8,4},{9,5},{12,8},{13,9},{14,12},{15,13},... | collective-permute-start | bytes 688136 | tf_op jit(solution)/shard_map/ppermute | solution.py:579
  22.2 6.0 %collective-permute-start.7 = (bf16[112,1024]{1,0:T(8,128)(2,1)S(1)}, bf16[112,1024]{1,0:T(8,128)(2,1)S(1)}, u32[]{:S(2)}, u32[]{:S(2)}) collective-permute-start(bf16[112,1024]{1,0:T(8,128)(2,1)S(1)} %collective-permute-done.5.refs_0_), channel_id=1, source_target_pairs={{0,4},{1,5},{4,8},{5,9},{8,12},{9,13},{12,14},{13,15},{14,10},{15,... | collective-permute-start | bytes 688136 | tf_op jit(solution)/shard_map/ppermute | solution.py:583
  23.3 4.7 %collective-permute-start.10 = (bf16[16,1024]{1,0:T(8,128)(2,1)S(1)}, bf16[16,1024]{1,0:T(8,128)(2,1)S(1)}, u32[]{:S(2)}, u32[]{:S(2)}) collective-permute-start(bf16[16,1024]{1,0:T(8,128)(2,1)S(1)} %slice.8), channel_id=1, source_target_pairs={{0,2},{1,3},{4,0},{5,1},{8,4},{9,5},{12,8},{13,9},{14,12},{15,13},... | collective-permute-start | bytes 98312 | tf_op jit(solution)/shard_map/ppermute | solution.py:584
  27.5 2.5 %collective-permute-start.12 = (f32[136,448]{1,0:T(8,128)S(1)}, f32[136,448]{1,0:T(8,128)S(1)}, u32[]{:S(2)}, u32[]{:S(2)}) collective-permute-start(f32[136,448]{1,0:T(8,128)S(1)} %get-tuple-element.58), channel_id=1, source_target_pairs={{0,1},{1,0},{2,3},{3,2},{4,5},{5,4},{6,7},{7,6},{8,9},{9,8},{10,11... | collective-permute-start | bytes 731144 | tf_op jit(solution)/shard_map/ppermute | solution.py:586
  27.5 2.4 %collective-permute-start.13 = (bf16[96,1024]{1,0:T(8,128)(2,1)S(1)}, bf16[96,1024]{1,0:T(8,128)(2,1)S(1)}, u32[]{:S(2)}, u32[]{:S(2)}) collective-permute-start(bf16[96,1024]{1,0:T(8,128)(2,1)S(1)} %get-tuple-element.59), channel_id=1, source_target_pairs={{0,1},{1,0},{2,3},{3,2},{4,5},{5,4},{6,7},{7,6},{8,9},{9,8},{10,11... | collective-permute-start | bytes 589832 | tf_op jit(solution)/shard_map/ppermute | solution.py:587
  28.0 1.9 %collective-permute-start.11 = (bf16[16,1024]{1,0:T(8,128)(2,1)S(1)}, bf16[16,1024]{1,0:T(8,128)(2,1)S(1)}, u32[]{:S(2)}, u32[]{:S(2)}) collective-permute-start(bf16[16,1024]{1,0:T(8,128)(2,1)S(1)} %collective-permute-done.10.refs_1_), channel_id=1, source_target_pairs={{0,1},{1,0},{2,3},{3,2},{4,5},{5,4},{6,7},{7,6},{8,9},{9,8},{10,11... | collective-permute-start | bytes 98312 | tf_op jit(solution)/shard_map/ppermute | solution.py:589
  28.2 1.7 %collective-permute-start.8 = (bf16[112,1024]{1,0:T(8,128)(2,1)S(1)}, bf16[112,1024]{1,0:T(8,128)(2,1)S(1)}, u32[]{:S(2)}, u32[]{:S(2)}) collective-permute-start(bf16[112,1024]{1,0:T(8,128)(2,1)S(1)} %collective-permute-done.7.refs_0_), channel_id=1, source_target_pairs={{0,1},{1,0},{2,3},{3,2},{4,5},{5,4},{6,7},{7,6},{8,9},{9,8},{10,11... | collective-permute-start | bytes 688136 | tf_op jit(solution)/shard_map/ppermute | solution.py:588

commit v8 on v7

--- a/solution.py
+++ b/solution.py
@@ -386,26 +386,29 @@
             put_pages(turned_pages[half * tokens : (half + 1) * tokens, :], refs[2 * half + 1])
 
 
+def places_kernel(seq_count, tokens, extra, arrivals, query_rows, facts_ref, wanted_ref, *outputs):
+    core = lax.axis_index("seq") % 2
+    wanted = wanted_ref[:, :tokens]
+    for side in range(2):
+        at = core + side * (1 - 2 * core)
+        place = read_places(seq_count, tokens, arrivals, at, extra, facts_ref, query_rows)
+        place_ref, chosen_ref = outputs[2 * side : 2 * side + 2]
+        place_ref[...] = jnp.broadcast_to(place, place_ref.shape)
+        chosen_ref[...] = chosen(place, wanted).T
+
+
 def close_kernel(seq_count, tokens, extra, arrivals, *refs):
     pieces, refs = refs[: len(arrivals)], refs[len(arrivals) :]
-    own_q, facts_ref, wanted_ref, mine, my_pages = refs[:5]
-    new, new_pages, next_place, next_chosen = refs[5:]
-    core = lax.axis_index("seq") % 2
+    own_q, facts_ref, place_ref, chosen_ref, mine, my_pages, new, new_pages = refs
     query_rows, head_dim = own_q.shape
-    place = read_places(seq_count, tokens, arrivals, core, extra, facts_ref, query_rows)
     blended = read_rows(pieces)
     limit = read_limit(facts_ref, seq_count, query_rows)[:, :query_rows]
-    wanted = wanted_ref[:, :tokens]
     state = attend(
-        blended, blended[:, head_dim:].T, place, own_q[...], limit, get_state(mine)
+        blended, blended[:, head_dim:].T, place_ref[:, :1], own_q[...], limit, get_state(mine)
     )
     put_state(state, 0, new)
-    picked = jnp.dot(chosen(place, wanted).T, blended, preferred_element_type=f32)
+    picked = jnp.dot(chosen_ref[...], blended, preferred_element_type=f32)
     put_pages(picked, new_pages, my_pages)
-
-    place = read_places(seq_count, tokens, arrivals, 1 - core, extra, facts_ref, query_rows)
-    next_place[...] = jnp.broadcast_to(place, next_place.shape)
-    next_chosen[...] = chosen(place, wanted).T
 
 
 def finish_kernel(seq_count, tokens, extra, arrivals, *refs):
@@ -423,10 +426,15 @@
     peak = jnp.maximum(one[0], two[0])
     fades = [jnp.exp2((part[0] - peak) * score_factor(head_dim)) for part in (one, two)]
     old = [peak] + [one[i] * fades[0] + two[i] * fades[1] for i in (1, 2)]
-    _, total, mixed = attend(
-        blended, blended[:, head_dim:].T, place_ref[:, :1], own_q[...], limit, old
-    )
-    flat = (mixed * (1.0 / total)).T
+    flat = []
+    cut = round_up(query_rows // 2, LANES)
+    for columns in (slice(0, cut), slice(cut, query_rows)):
+        _, total, mixed = attend(
+            blended, blended[:, head_dim:].T, place_ref[:, :1], own_q[columns, :],
+            limit[:, columns], [part[:, columns] for part in old],
+        )
+        flat.append((mixed * (1.0 / total)).T)
+    flat = jnp.concatenate(flat, axis=0)
     sel = out_ref.shape[0]
     for h in range(GROUP):
         out_scratch[:, h * head_dim : (h + 1) * head_dim] = flat[
@@ -523,10 +531,10 @@
         jax.ShapeDtypeStruct((head_dim + 8, query_rows), f32),
         jax.ShapeDtypeStruct((pages, width), bf16),
     )
-    close_shapes = half_shapes + (
+    place_shapes = (
         jax.ShapeDtypeStruct((PAGE * (rows + extra), LANES), f32),
         jax.ShapeDtypeStruct((tokens, PAGE * (rows + extra)), bf16),
-    )
+    ) * 2
     out_shapes = (
         jax.ShapeDtypeStruct((sel, GROUP * head_dim), bf16),
         jax.ShapeDtypeStruct((pages, width), bf16),
@@ -567,6 +575,7 @@
         return run(kernel, arrivals, operands, out_shape, "visit", aliases)
 
     half = chips // 2
+    last_steps = [(half, (half - 1,)), (None, (half,))]
     own_block = chunk[pages:]
     block = lax.ppermute(own_block, "seq", backward)
     ahead, behind = merge(1, ahead, own_block), merge(-1, behind, block)
@@ -578,7 +587,21 @@
         ahead = lax.ppermute(ahead, "seq", forward)
         behind = lax.ppermute(behind, "seq", backward)
         state = visit(state, arrivals)
-        ahead, state = lax.optimization_barrier((ahead, state))
+        if step == half - 1:
+            found = pl.pallas_call(
+                partial(places_kernel, seq_count, tokens, extra, last_steps, query_rows),
+                out_shape=place_shapes,
+                in_specs=[vmem] * 2,
+                out_specs=(vmem,) * 4,
+                compiler_params=params,
+                cost_estimate=pl.CostEstimate(
+                    flops=10**8, bytes_accessed=2**21, transcendentals=0
+                ),
+                name="places",
+            )(facts, wanted)
+            ahead, state, found = lax.optimization_barrier((ahead, state, found))
+        else:
+            ahead, state = lax.optimization_barrier((ahead, state))
         arrivals = [(step, (step - 1,), ahead), (-step, (-step,), behind)]
     farthest = lax.ppermute(ahead, "seq", forward)
     fresh_farthest = lax.ppermute(behind[pages:], "seq", backward)
@@ -587,13 +610,13 @@
     got_pages = lax.ppermute(their_pages, "seq", swap)
     other_farthest = lax.ppermute(farthest, "seq", swap)
     other_fresh = lax.ppermute(fresh_farthest, "seq", swap)
-    operands = [queries, facts, wanted, mine, my_pages]
-    *state, place, choice = run(
-        close_kernel, [(half, (half - 1,), farthest), (None, (half,), fresh_farthest)], operands, close_shapes, "close", weight=10
+    state = run(
+        close_kernel, [(half, (half - 1,), farthest), (None, (half,), fresh_farthest)],
+        [queries, facts, *found[:2], mine, my_pages], half_shapes, "close", weight=10,
     )
     scratch = [pltpu.VMEM(x.shape, x.dtype) for x in out_shapes]
     scratch.append(pltpu.SemaphoreType.DMA((2,)))
-    operands = [queries, facts, *state, place, choice, got, got_pages]
+    operands = [queries, facts, *state, *found[2:], got, got_pages]
     return run(
         finish_kernel, [(half, (half - 1,), other_farthest), (None, (half,), other_fresh)], operands, out_shapes, "finish",
         scratch=scratch,

time: 31.7 us -> 31.7 us (level)
  starting transfers between devices: 14.4 us -> 12.6 us
  waiting for transfers between devices: 3.16 us -> 4.68 us
    ppermute x1, starting transfers between devices: 1.95 us -> 0.83 us  [shards(): fresh_farthest = lax.ppermute(behind[pages:], 'seq', backward)]
    ppermute x2, waiting for transfers between devices: 0.18 us -> 1.2 us  [shards(): behind = lax.ppermute(behind, 'seq', backward)]
    pallas_call x0 -> x1, Pallas kernels: none -> 0.79 us  [shards(): pl.pallas_call(partial(places_kernel, seq_count, tokens, extra, last_step...]
    ppermute x2, starting transfers between devices: 1.87 us -> 1.16 us  [shards(): behind = lax.ppermute(behind, 'seq', backward)]
    pallas_call x6, Pallas kernels: 11 us -> 10.4 us  [run(): pl.pallas_call(partial(kernel, seq_count, tokens, extra, layout), out_sha...]
  transfers between devices with their start and end apart: 14 -> 14, of which waited for: 7 -> 7; matrix products, arithmetic and copies ran while one was open for 2% -> 2% of each run, Pallas kernels for 35% -> 36%
where the time goes in v8:
time: 31.7 us; the launch traced here: 31.5 us
  Pallas kernels  12.9 us (41%)
  starting transfers between devices  12.6 us (40%)
  waiting for transfers between devices  4.68 us (15%)
  between operations  0.77 us (2%)
  other arithmetic  0.46 us (1%)
    pallas_call x6, Pallas kernels, run(): pl.pallas_call(partial(kernel, seq_count, tokens, extra, layout), out_sha...  10.4 us
    ppermute x2, starting transfers between devices, shards(): ahead = lax.ppermute(ahead, 'seq', forward)  3.39 us
    ppermute x1, starting transfers between devices, shards(): ahead = lax.ppermute(pool_kv, 'seq', forward)  3.08 us
    ppermute x1, starting transfers between devices, shards(): block = lax.ppermute(own_block, 'seq', backward)  1.99 us
    ppermute x2, waiting for transfers between devices, shards(): ahead = lax.ppermute(ahead, 'seq', forward)  1.74 us
    pallas_call x1, Pallas kernels, shards(): pl.pallas_call(partial(plan_kernel, seq_count, tokens), out_shape=(jax.Sh...  1.52 us
    ppermute x2, waiting for transfers between devices, shards(): behind = lax.ppermute(behind, 'seq', backward)  1.2 us
    ppermute x2, starting transfers between devices, shards(): behind = lax.ppermute(behind, 'seq', backward)  1.16 us
  transfers between devices with their start and end apart: 14, of which 7 were waited for; matrix products, arithmetic and copies ran while one was open for 2% of the time, Pallas kernels for 36%

profile of v8, /device:TPU:0, one launch (start us, length us, event | category | flops | bytes accessed | tf_op | source)
XLA Modules:
  0.0 31.5 jit_solution(15516251658702347618)
XLA Ops:
  0.6 3.1 %collective-permute-start = (bf16[96,1024]{1,0:T(8,128)(2,1)}, bf16[96,1024]{1,0:T(8,128)(2,1)S(1)}, u32[]{:S(2)}, u32[]{:S(2)}) collective-permute-start(bf16[96,1024]{1,0:T(8,128)(2,1)} %refs_7_.1), channel_id=1, source_target_pairs={{0,4},{1,5},{4,8},{5,9},{8,12},{9,13},{12,14},{13,15},{14,10},{15,... | collective-permute-start | bytes 589832 | tf_op jit(solution)/shard_map/ppermute | solution.py:470
  3.7 1.5 %plan.1 = (bf16[448,128]{1,0:T(8,128)(2,1)S(1)}, f32[32,128]{1,0:T(8,128)S(1)}, f32[192,128]{1,0:T(8,128)S(1)}, bf16[112,1024]{1,0:T(8,128)(2,1)S(1)}, s32[1536]{0:T(1024)S(1)}) custom-call(s32[16]{0:T(128)} %refs_0_.1, s32[16]{0:T(128)} %refs_1_.1, s32[16]{0:T(128)} %refs_2_.1, f32[1,128]{1,0:T(1,128)} %constant.14.clone.refs_3_, s32[16,56]{1,0:T(8,128)} %refs_4_.1, ...), custom_call_target="tpu_custom_call" | custom-call | flops 100000000 | bytes 6291456 | tf_op jit(solution)/shard_map/plan/pallas_call | solution.py:479
  5.2 0.1 collective-permute-start.1
  5.3 2.0 %collective-permute-start.4 = (bf16[16,1024]{1,0:T(8,128)(2,1)S(1)}, bf16[16,1024]{1,0:T(8,128)(2,1)S(1)}, u32[]{:S(2)}, u32[]{:S(2)}) collective-permute-start(bf16[16,1024]{1,0:T(8,128)(2,1)S(1)} %slice.6.block_ref), channel_id=1, source_target_pairs={{0,2},{1,3},{4,0},{5,1},{8,4},{9,5},{12,8},{13,9},{14,12},{15,13},... | collective-permute-start | bytes 98312 | tf_op jit(solution)/shard_map/ppermute | solution.py:580
  7.3 0.1 add_multiply_fusion
  7.4 0.1 iota_add_fusion
  7.5 0.3 select_reduce_fusion
  7.8 1.0 %collective-permute-done.pool_ref = bf16[96,1024]{1,0:T(8,128)(2,1)S(1)} collective-permute-done((bf16[96,1024]{1,0:T(8,128)(2,1)}, bf16[96,1024]{1,0:T(8,128)(2,1)S(1)}, u32[]{:S(2)}, u32[]{:S(2)}) %collective-permute-start) | collective-permute-done | bytes 196640 | tf_op jit(solution)/shard_map/ppermute | solution.py:470
  8.7 0.1 merge.2.refs_0_
  8.9 1.9 %collective-permute-start.2 = (bf16[112,1024]{1,0:T(8,128)(2,1)S(1)}, bf16[112,1024]{1,0:T(8,128)(2,1)S(1)}, u32[]{:S(2)}, u32[]{:S(2)}) collective-permute-start(bf16[112,1024]{1,0:T(8,128)(2,1)S(1)} %merge.2.refs_0_), channel_id=1, source_target_pairs={{0,4},{1,5},{4,8},{5,9},{8,12},{9,13},{12,14},{13,15},{14,10},{15,... | collective-permute-start | bytes 688136 | tf_op jit(solution)/shard_map/ppermute | solution.py:587
  10.7 0.1 convert_element_type.14.refs_4_.refs_5_.wanted_ref
  10.8 0.2 collective-permute-done.4.block_ref
  11.0 0.1 merge.3.refs_1_
  11.1 0.4 %collective-permute-start.6 = (bf16[112,1024]{1,0:T(8,128)(2,1)S(1)}, bf16[112,1024]{1,0:T(8,128)(2,1)S(1)}, u32[]{:S(2)}, u32[]{:S(2)}) collective-permute-start(bf16[112,1024]{1,0:T(8,128)(2,1)S(1)} %merge.3.refs_1_), channel_id=1, source_target_pairs={{0,2},{1,3},{4,0},{5,1},{8,4},{9,5},{12,8},{13,9},{14,12},{15,13},... | collective-permute-start | bytes 688136 | tf_op jit(solution)/shard_map/ppermute | solution.py:588
  11.5 1.3 %visit.4 = (f32[136,896]{1,0:T(8,128)S(1)}, bf16[256,768]{1,0:T(8,128)(2,1)S(1)}) custom-call(bf16[112,1024]{1,0:T(8,128)(2,1)S(1)} %get-tuple-element.37.refs_0_, bf16[448,128]{1,0:T(8,128)(2,1)S(1)} %get-tuple-element.40.refs_1_.refs_2_, bf16[448,128]{1,0:T(8,128)(2,1)S(1)} %collective-permute-done.1.refs_2_.refs_3_, ...), custom_call_target="tpu_custom_call" | custom-call | flops 381681664 | bytes 4194304 | tf_op jit(solution)/shard_map/visit/pallas_call | solution.py:549
  12.8 2.3 %visit.5 = (f32[136,896]{1,0:T(8,128)S(1)}, bf16[256,768]{1,0:T(8,128)(2,1)S(1)}) custom-call(bf16[112,1024]{1,0:T(8,128)(2,1)S(1)} %merge.2.refs_0_, bf16[112,1024]{1,0:T(8,128)(2,1)S(1)} %merge.3.refs_1_, bf16[448,128]{1,0:T(8,128)(2,1)S(1)} %get-tuple-element.40.refs_1_.refs_2_, ...), custom_call_target="tpu_custom_call", output_to_operand_aliasing={{0}: (6, {}), {1}: (7, {})} | custom-call | flops 763363328 | bytes 4194304 | tf_op jit(solution)/shard_map/visit/pallas_call | solution.py:549
  15.1 0.6 %collective-permute-done.2.refs_0_ = bf16[112,1024]{1,0:T(8,128)(2,1)S(1)} collective-permute-done((bf16[112,1024]{1,0:T(8,128)(2,1)S(1)}, bf16[112,1024]{1,0:T(8,128)(2,1)S(1)}, u32[]{:S(2)}, u32[]{:S(2)}) %collective-permute-start.2) | collective-permute-done | bytes 229408 | tf_op jit(solution)/shard_map/ppermute | solution.py:587
  15.7 1.5 %collective-permute-start.5 = (bf16[112,1024]{1,0:T(8,128)(2,1)S(1)}, bf16[112,1024]{1,0:T(8,128)(2,1)S(1)}, u32[]{:S(2)}, u32[]{:S(2)}) collective-permute-start(bf16[112,1024]{1,0:T(8,128)(2,1)S(1)} %collective-permute-done.2.refs_0_), channel_id=1, source_target_pairs={{0,4},{1,5},{4,8},{5,9},{8,12},{9,13},{12,14},{13,15},{14,10},{15,... | collective-permute-start | bytes 688136 | tf_op jit(solution)/shard_map/ppermute | solution.py:587
  17.2 0.8 %places.1 = (f32[512,128]{1,0:T(8,128)S(1)}, bf16[384,512]{1,0:T(8,128)(2,1)S(1)}, f32[512,128]{1,0:T(8,128)S(1)}, bf16[384,512]{1,0:T(8,128)(2,1)S(1)}) custom-call(f32[32,128]{1,0:T(8,128)S(1)} %get-tuple-element.38.facts_ref.refs_3_.refs_4_, f32[1,768]{1,0:T(1,128)S(1)} %convert_element_type.14.refs_4_.refs_5_.wanted_ref), custom_call_target="tpu_custom_call" | custom-call | flops 100000000 | bytes 2097152 | tf_op jit(solution)/shard_map/places/pallas_call | solution.py:591
  18.0 0.8 %collective-permute-start.9 = (bf16[112,1024]{1,0:T(8,128)(2,1)S(1)}, bf16[112,1024]{1,0:T(8,128)(2,1)S(1)}, u32[]{:S(2)}, u32[]{:S(2)}) collective-permute-start(bf16[112,1024]{1,0:T(8,128)(2,1)S(1)} %collective-permute-done.6.refs_1_), channel_id=1, source_target_pairs={{0,2},{1,3},{4,0},{5,1},{8,4},{9,5},{12,8},{13,9},{14,12},{15,13},... | collective-permute-start | bytes 688136 | tf_op jit(solution)/shard_map/ppermute | solution.py:588
  18.8 2.3 %visit.6 = (f32[136,896]{1,0:T(8,128)S(1)}, bf16[256,768]{1,0:T(8,128)(2,1)S(1)}) custom-call(bf16[112,1024]{1,0:T(8,128)(2,1)S(1)} %collective-permute-done.2.refs_0_, bf16[112,1024]{1,0:T(8,128)(2,1)S(1)} %collective-permute-done.6.refs_1_, bf16[448,128]{1,0:T(8,128)(2,1)S(1)} %get-tuple-element.40.refs_1_.refs_2_, ...), custom_call_target="tpu_custom_call", output_to_operand_aliasing={{0}: (6, {}), {1}: (7, {})} | custom-call | flops 763363328 | bytes 4194304 | tf_op jit(solution)/shard_map/visit/pallas_call | solution.py:549
  21.1 1.1 %collective-permute-done.5.refs_0_ = bf16[112,1024]{1,0:T(8,128)(2,1)S(1)} collective-permute-done((bf16[112,1024]{1,0:T(8,128)(2,1)S(1)}, bf16[112,1024]{1,0:T(8,128)(2,1)S(1)}, u32[]{:S(2)}, u32[]{:S(2)}) %collective-permute-start.5) | collective-permute-done | bytes 229408 | tf_op jit(solution)/shard_map/ppermute | solution.py:587
  22.2 1.0 %collective-permute-start.7 = (bf16[112,1024]{1,0:T(8,128)(2,1)S(1)}, bf16[112,1024]{1,0:T(8,128)(2,1)S(1)}, u32[]{:S(2)}, u32[]{:S(2)}) collective-permute-start(bf16[112,1024]{1,0:T(8,128)(2,1)S(1)} %collective-permute-done.5.refs_0_), channel_id=1, source_target_pairs={{0,4},{1,5},{4,8},{5,9},{8,12},{9,13},{12,14},{13,15},{14,10},{15,... | collective-permute-start | bytes 688136 | tf_op jit(solution)/shard_map/ppermute | solution.py:606
  23.2 1.2 %collective-permute-done.9.refs_1_ = bf16[112,1024]{1,0:T(8,128)(2,1)S(1)} collective-permute-done((bf16[112,1024]{1,0:T(8,128)(2,1)S(1)}, bf16[112,1024]{1,0:T(8,128)(2,1)S(1)}, u32[]{:S(2)}, u32[]{:S(2)}) %collective-permute-start.9) | collective-permute-done | bytes 229408 | tf_op jit(solution)/shard_map/ppermute | solution.py:588
  24.4 0.8 %collective-permute-start.10 = (bf16[16,1024]{1,0:T(8,128)(2,1)S(1)}, bf16[16,1024]{1,0:T(8,128)(2,1)S(1)}, u32[]{:S(2)}, u32[]{:S(2)}) collective-permute-start(bf16[16,1024]{1,0:T(8,128)(2,1)S(1)} %slice.8), channel_id=1, source_target_pairs={{0,2},{1,3},{4,0},{5,1},{8,4},{9,5},{12,8},{13,9},{14,12},{15,13},... | collective-permute-start | bytes 98312 | tf_op jit(solution)/shard_map/ppermute | solution.py:607
  25.3 2.2 %visit.7 = (f32[136,448]{1,0:T(8,128)S(1)}, bf16[96,1024]{1,0:T(8,128)(2,1)S(1)}, f32[136,448]{1,0:T(8,128)S(1)}, bf16[96,1024]{1,0:T(8,128)(2,1)S(1)}) custom-call(bf16[112,1024]{1,0:T(8,128)(2,1)S(1)} %collective-permute-done.5.refs_0_, bf16[112,1024]{1,0:T(8,128)(2,1)S(1)} %collective-permute-done.9.refs_1_, ...), custom_call_target="tpu_custom_call" | custom-call | flops 763363328 | bytes 4194304 | tf_op jit(solution)/shard_map/visit/pallas_call | solution.py:549
  27.5 0.5 %collective-permute-start.13 = (bf16[96,1024]{1,0:T(8,128)(2,1)S(1)}, bf16[96,1024]{1,0:T(8,128)(2,1)S(1)}, u32[]{:S(2)}, u32[]{:S(2)}) collective-permute-start(bf16[96,1024]{1,0:T(8,128)(2,1)S(1)} %get-tuple-element.71), channel_id=1, source_target_pairs={{0,1},{1,0},{2,3},{3,2},{4,5},{5,4},{6,7},{7,6},{8,9},{9,8},{10,11... | collective-permute-start | bytes 589832 | tf_op jit(solution)/shard_map/ppermute | solution.py:610
  28.0 0.3 %collective-permute-done.10.refs_1_ = bf16[16,1024]{1,0:T(8,128)(2,1)S(1)} collective-permute-done((bf16[16,1024]{1,0:T(8,128)(2,1)S(1)}, bf16[16,1024]{1,0:T(8,128)(2,1)S(1)}, u32[]{:S(2)}, u32[]{:S(2)}) %collective-permute-start.10) | collective-permute-done | bytes 32800 | tf_op jit(solution)/shard_map/ppermute | solution.py:607
  28.4 0.5 %collective-permute-start.8 = (bf16[112,1024]{1,0:T(8,128)(2,1)S(1)}, bf16[112,1024]{1,0:T(8,128)(2,1)S(1)}, u32[]{:S(2)}, u32[]{:S(2)}) collective-permute-start(bf16[112,1024]{1,0:T(8,128)(2,1)S(1)} %collective-permute-done.7.refs_0_), channel_id=1, source_target_pairs={{0,1},{1,0},{2,3},{3,2},{4,5},{5,4},{6,7},{7,6},{8,9},{9,8},{10,11... | collective-permute-start | bytes 688136 | tf_op jit(solution)/shard_map/ppermute | solution.py:611
  28.9 0.8 %close.1 = (f32[136,448]{1,0:T(8,128)S(1)}, bf16[96,1024]{1,0:T(8,128)(2,1)S(1)}) custom-call(bf16[112,1024]{1,0:T(8,128)(2,1)S(1)} %collective-permute-done.7.refs_0_, bf16[16,1024]{1,0:T(8,128)(2,1)S(1)} %collective-permute-done.10.refs_1_, bf16[448,128]{1,0:T(8,128)(2,1)S(1)} %get-tuple-element.40.refs_1_.refs_2_, ...), custom_call_target="tpu_custom_call" | custom-call | flops 4362076160 | bytes 41943040 | tf_op jit(solution)/shard_map/close/pallas_call | solution.py:549
  29.7 0.3 collective-permute-done.8.refs_0_
  30.0 1.5 %finish.1 = (bf16[56,1024]{1,0:T(8,128)(2,1)}, bf16[96,1024]{1,0:T(8,128)(2,1)}) custom-call(bf16[112,1024]{1,0:T(8,128)(2,1)S(1)} %collective-permute-done.8.refs_0_, bf16[16,1024]{1,0:T(8,128)(2,1)S(1)} %collective-permute-done.11.refs_1_, bf16[448,128]{1,0:T(8,128)(2,1)S(1)} %get-tuple-element.40.refs_1_.refs_2_, ...), custom_call_target="tpu_custom_call" | custom-call | flops 436207616 | bytes 4194304 | tf_op jit(solution)/shard_map/finish/pallas_call | solution.py:549
  (14 shorter events, 0.1 us)
Async XLA Ops:
  0.6 8.1 %collective-permute-start = (bf16[96,1024]{1,0:T(8,128)(2,1)}, bf16[96,1024]{1,0:T(8,128)(2,1)S(1)}, u32[]{:S(2)}, u32[]{:S(2)}) collective-permute-start(bf16[96,1024]{1,0:T(8,128)(2,1)} %refs_7_.1), channel_id=1, source_target_pairs={{0,4},{1,5},{4,8},{5,9},{8,12},{9,13},{12,14},{13,15},{14,10},{15,... | collective-permute-start | bytes 589832 | tf_op jit(solution)/shard_map/ppermute | solution.py:470
  3.7 7.3 %collective-permute-start.3 = (bf16[96,1024]{1,0:T(8,128)(2,1)}, bf16[96,1024]{1,0:T(8,128)(2,1)S(1)}, u32[]{:S(2)}, u32[]{:S(2)}) collective-permute-start(bf16[96,1024]{1,0:T(8,128)(2,1)} %refs_7_.1), channel_id=1, source_target_pairs={{0,2},{1,3},{4,0},{5,1},{8,4},{9,5},{12,8},{13,9},{14,12},{15,13},... | collective-permute-start | bytes 589832 | tf_op jit(solution)/shard_map/ppermute | solution.py:471
  5.2 3.6 %collective-permute-start.1 = (bf16[448,128]{1,0:T(8,128)(2,1)S(1)}, bf16[448,128]{1,0:T(8,128)(2,1)S(1)}, u32[]{:S(2)}, u32[]{:S(2)}) collective-permute-start(bf16[448,128]{1,0:T(8,128)(2,1)S(1)} %get-tuple-element.40.refs_1_.refs_2_), channel_id=1, source_target_pairs={{0,1},{1,0},{2,3},{3,2},{4,5},{5,4},{6,7},{7,6},{8,9},{9,8},{10,11... | collective-permute-start | bytes 344072 | tf_op jit(solution)/shard_map/ppermute | solution.py:524
  5.3 5.7 %collective-permute-start.4 = (bf16[16,1024]{1,0:T(8,128)(2,1)S(1)}, bf16[16,1024]{1,0:T(8,128)(2,1)S(1)}, u32[]{:S(2)}, u32[]{:S(2)}) collective-permute-start(bf16[16,1024]{1,0:T(8,128)(2,1)S(1)} %slice.6.block_ref), channel_id=1, source_target_pairs={{0,2},{1,3},{4,0},{5,1},{8,4},{9,5},{12,8},{13,9},{14,12},{15,13},... | collective-permute-start | bytes 98312 | tf_op jit(solution)/shard_map/ppermute | solution.py:580
  8.9 6.8 %collective-permute-start.2 = (bf16[112,1024]{1,0:T(8,128)(2,1)S(1)}, bf16[112,1024]{1,0:T(8,128)(2,1)S(1)}, u32[]{:S(2)}, u32[]{:S(2)}) collective-permute-start(bf16[112,1024]{1,0:T(8,128)(2,1)S(1)} %merge.2.refs_0_), channel_id=1, source_target_pairs={{0,4},{1,5},{4,8},{5,9},{8,12},{9,13},{12,14},{13,15},{14,10},{15,... | collective-permute-start | bytes 688136 | tf_op jit(solution)/shard_map/ppermute | solution.py:587
  11.1 6.9 %collective-permute-start.6 = (bf16[112,1024]{1,0:T(8,128)(2,1)S(1)}, bf16[112,1024]{1,0:T(8,128)(2,1)S(1)}, u32[]{:S(2)}, u32[]{:S(2)}) collective-permute-start(bf16[112,1024]{1,0:T(8,128)(2,1)S(1)} %merge.3.refs_1_), channel_id=1, source_target_pairs={{0,2},{1,3},{4,0},{5,1},{8,4},{9,5},{12,8},{13,9},{14,12},{15,13},... | collective-permute-start | bytes 688136 | tf_op jit(solution)/shard_map/ppermute | solution.py:588
  15.7 6.5 %collective-permute-start.5 = (bf16[112,1024]{1,0:T(8,128)(2,1)S(1)}, bf16[112,1024]{1,0:T(8,128)(2,1)S(1)}, u32[]{:S(2)}, u32[]{:S(2)}) collective-permute-start(bf16[112,1024]{1,0:T(8,128)(2,1)S(1)} %collective-permute-done.2.refs_0_), channel_id=1, source_target_pairs={{0,4},{1,5},{4,8},{5,9},{8,12},{9,13},{12,14},{13,15},{14,10},{15,... | collective-permute-start | bytes 688136 | tf_op jit(solution)/shard_map/ppermute | solution.py:587
  18.0 6.4 %collective-permute-start.9 = (bf16[112,1024]{1,0:T(8,128)(2,1)S(1)}, bf16[112,1024]{1,0:T(8,128)(2,1)S(1)}, u32[]{:S(2)}, u32[]{:S(2)}) collective-permute-start(bf16[112,1024]{1,0:T(8,128)(2,1)S(1)} %collective-permute-done.6.refs_1_), channel_id=1, source_target_pairs={{0,2},{1,3},{4,0},{5,1},{8,4},{9,5},{12,8},{13,9},{14,12},{15,13},... | collective-permute-start | bytes 688136 | tf_op jit(solution)/shard_map/ppermute | solution.py:588
  22.2 6.2 %collective-permute-start.7 = (bf16[112,1024]{1,0:T(8,128)(2,1)S(1)}, bf16[112,1024]{1,0:T(8,128)(2,1)S(1)}, u32[]{:S(2)}, u32[]{:S(2)}) collective-permute-start(bf16[112,1024]{1,0:T(8,128)(2,1)S(1)} %collective-permute-done.5.refs_0_), channel_id=1, source_target_pairs={{0,4},{1,5},{4,8},{5,9},{8,12},{9,13},{12,14},{13,15},{14,10},{15,... | collective-permute-start | bytes 688136 | tf_op jit(solution)/shard_map/ppermute | solution.py:606
  24.4 3.9 %collective-permute-start.10 = (bf16[16,1024]{1,0:T(8,128)(2,1)S(1)}, bf16[16,1024]{1,0:T(8,128)(2,1)S(1)}, u32[]{:S(2)}, u32[]{:S(2)}) collective-permute-start(bf16[16,1024]{1,0:T(8,128)(2,1)S(1)} %slice.8), channel_id=1, source_target_pairs={{0,2},{1,3},{4,0},{5,1},{8,4},{9,5},{12,8},{13,9},{14,12},{15,13},... | collective-permute-start | bytes 98312 | tf_op jit(solution)/shard_map/ppermute | solution.py:607
  27.5 2.2 %collective-permute-start.12 = (f32[136,448]{1,0:T(8,128)S(1)}, f32[136,448]{1,0:T(8,128)S(1)}, u32[]{:S(2)}, u32[]{:S(2)}) collective-permute-start(f32[136,448]{1,0:T(8,128)S(1)} %get-tuple-element.70), channel_id=1, source_target_pairs={{0,1},{1,0},{2,3},{3,2},{4,5},{5,4},{6,7},{7,6},{8,9},{9,8},{10,11... | collective-permute-start | bytes 731144 | tf_op jit(solution)/shard_map/ppermute | solution.py:609
  27.5 2.1 %collective-permute-start.13 = (bf16[96,1024]{1,0:T(8,128)(2,1)S(1)}, bf16[96,1024]{1,0:T(8,128)(2,1)S(1)}, u32[]{:S(2)}, u32[]{:S(2)}) collective-permute-start(bf16[96,1024]{1,0:T(8,128)(2,1)S(1)} %get-tuple-element.71), channel_id=1, source_target_pairs={{0,1},{1,0},{2,3},{3,2},{4,5},{5,4},{6,7},{7,6},{8,9},{9,8},{10,11... | collective-permute-start | bytes 589832 | tf_op jit(solution)/shard_map/ppermute | solution.py:610
  28.4 1.3 %collective-permute-start.11 = (bf16[16,1024]{1,0:T(8,128)(2,1)S(1)}, bf16[16,1024]{1,0:T(8,128)(2,1)S(1)}, u32[]{:S(2)}, u32[]{:S(2)}) collective-permute-start(bf16[16,1024]{1,0:T(8,128)(2,1)S(1)} %collective-permute-done.10.refs_1_), channel_id=1, source_target_pairs={{0,1},{1,0},{2,3},{3,2},{4,5},{5,4},{6,7},{7,6},{8,9},{9,8},{10,11... | collective-permute-start | bytes 98312 | tf_op jit(solution)/shard_map/ppermute | solution.py:612
  28.4 1.6 %collective-permute-start.8 = (bf16[112,1024]{1,0:T(8,128)(2,1)S(1)}, bf16[112,1024]{1,0:T(8,128)(2,1)S(1)}, u32[]{:S(2)}, u32[]{:S(2)}) collective-permute-start(bf16[112,1024]{1,0:T(8,128)(2,1)S(1)} %collective-permute-done.7.refs_0_), channel_id=1, source_target_pairs={{0,1},{1,0},{2,3},{3,2},{4,5},{5,4},{6,7},{7,6},{8,9},{9,8},{10,11... | collective-permute-start | bytes 688136 | tf_op jit(solution)/shard_map/ppermute | solution.py:611

commit v9 on v7

--- a/solution.py
+++ b/solution.py
@@ -423,19 +423,30 @@
     peak = jnp.maximum(one[0], two[0])
     fades = [jnp.exp2((part[0] - peak) * score_factor(head_dim)) for part in (one, two)]
     old = [peak] + [one[i] * fades[0] + two[i] * fades[1] for i in (1, 2)]
-    _, total, mixed = attend(
-        blended, blended[:, head_dim:].T, place_ref[:, :1], own_q[...], limit, old
-    )
-    flat = (mixed * (1.0 / total)).T
+    flat, copies, done = None, [pages_copy], 0
+    cut = round_up(query_rows // 2, LANES)
     sel = out_ref.shape[0]
-    for h in range(GROUP):
-        out_scratch[:, h * head_dim : (h + 1) * head_dim] = flat[
-            h * sel : (h + 1) * sel, :
-        ].astype(bf16)
-    out_copy = pltpu.make_async_copy(out_scratch, out_ref, sems.at[1])
-    out_copy.start()
-    pages_copy.wait()
-    out_copy.wait()
+    for columns in (slice(0, cut), slice(cut, query_rows)):
+        _, total, mixed = attend(
+            blended, blended[:, head_dim:].T, place_ref[:, :1], own_q[columns, :],
+            limit[:, columns], [part[:, columns] for part in old],
+        )
+        rows = (mixed * (1.0 / total)).T
+        flat = rows if flat is None else jnp.concatenate([flat, rows], axis=0)
+        ready = flat.shape[0] // sel
+        for h in range(done, ready):
+            out_scratch[:, h * head_dim : (h + 1) * head_dim] = flat[
+                h * sel : (h + 1) * sel, :
+            ].astype(bf16)
+        lanes = pl.ds(done * head_dim, (ready - done) * head_dim)
+        copy = pltpu.make_async_copy(
+            out_scratch.at[:, lanes], out_ref.at[:, lanes], sems.at[len(copies)]
+        )
+        copy.start()
+        copies.append(copy)
+        done = ready
+    for copy in copies:
+        copy.wait()
 
 
 def shards(
@@ -592,7 +603,7 @@
         close_kernel, [(half, (half - 1,), farthest), (None, (half,), fresh_farthest)], operands, close_shapes, "close", weight=10
     )
     scratch = [pltpu.VMEM(x.shape, x.dtype) for x in out_shapes]
-    scratch.append(pltpu.SemaphoreType.DMA((2,)))
+    scratch.append(pltpu.SemaphoreType.DMA((3,)))
     operands = [queries, facts, *state, place, choice, got, got_pages]
     return run(
         finish_kernel, [(half, (half - 1,), other_farthest), (None, (half,), other_fresh)], operands, out_shapes, "finish",

time: 31.7 us -> 31.6 us (level)
  no operation moved by 1% of the time
where the time goes in v9:
time: 31.6 us; the launch traced here: 31.5 us
  starting transfers between devices  14.4 us (46%)
  Pallas kernels  12.7 us (40%)
  waiting for transfers between devices  3.16 us (10%)
  between operations  0.77 us (2%)
  other arithmetic  0.46 us (1%)
    pallas_call x6, Pallas kernels, run(): pl.pallas_call(partial(kernel, seq_count, tokens, extra, layout), out_sha...  10.9 us
    ppermute x2, starting transfers between devices, shards(): ahead = lax.ppermute(ahead, 'seq', forward)  3.39 us
    ppermute x1, starting transfers between devices, shards(): ahead = lax.ppermute(pool_kv, 'seq', forward)  3.08 us
    ppermute x1, starting transfers between devices, shards(): block = lax.ppermute(own_block, 'seq', backward)  1.99 us
    ppermute x1, starting transfers between devices, shards(): fresh_farthest = lax.ppermute(behind[pages:], 'seq', backward)  1.95 us
    ppermute x2, starting transfers between devices, shards(): behind = lax.ppermute(behind, 'seq', backward)  1.87 us
    ppermute x2, waiting for transfers between devices, shards(): ahead = lax.ppermute(ahead, 'seq', forward)  1.74 us
    pallas_call x1, Pallas kernels, shards(): pl.pallas_call(partial(plan_kernel, seq_count, tokens), out_shape=(jax.Sh...  1.52 us
  transfers between devices with their start and end apart: 14, of which 7 were waited for; matrix products, arithmetic and copies ran while one was open for 2% of the time, Pallas kernels for 35%

profile of v9, /device:TPU:0, one launch (start us, length us, event | category | flops | bytes accessed | tf_op | source)
XLA Modules:
  0.0 31.5 jit_solution(8406170075369431584)
XLA Ops:
  0.6 3.1 %collective-permute-start = (bf16[96,1024]{1,0:T(8,128)(2,1)}, bf16[96,1024]{1,0:T(8,128)(2,1)S(1)}, u32[]{:S(2)}, u32[]{:S(2)}) collective-permute-start(bf16[96,1024]{1,0:T(8,128)(2,1)} %refs_7_.1), channel_id=1, source_target_pairs={{0,4},{1,5},{4,8},{5,9},{8,12},{9,13},{12,14},{13,15},{14,10},{15,... | collective-permute-start | bytes 589832 | tf_op jit(solution)/shard_map/ppermute | solution.py:473
  3.7 1.5 %plan.1 = (bf16[448,128]{1,0:T(8,128)(2,1)S(1)}, f32[32,128]{1,0:T(8,128)S(1)}, f32[192,128]{1,0:T(8,128)S(1)}, bf16[112,1024]{1,0:T(8,128)(2,1)S(1)}, s32[1536]{0:T(1024)S(1)}) custom-call(s32[16]{0:T(128)} %refs_0_.1, s32[16]{0:T(128)} %refs_1_.1, s32[16]{0:T(128)} %refs_2_.1, f32[1,128]{1,0:T(1,128)} %constant.14.clone.refs_3_, s32[16,56]{1,0:T(8,128)} %refs_4_.1, ...), custom_call_target="tpu_custom_call" | custom-call | flops 100000000 | bytes 6291456 | tf_op jit(solution)/shard_map/plan/pallas_call | solution.py:482
  5.2 0.1 collective-permute-start.1
  5.3 2.0 %collective-permute-start.4 = (bf16[16,1024]{1,0:T(8,128)(2,1)S(1)}, bf16[16,1024]{1,0:T(8,128)(2,1)S(1)}, u32[]{:S(2)}, u32[]{:S(2)}) collective-permute-start(bf16[16,1024]{1,0:T(8,128)(2,1)S(1)} %slice.6.block_ref), channel_id=1, source_target_pairs={{0,2},{1,3},{4,0},{5,1},{8,4},{9,5},{12,8},{13,9},{14,12},{15,13},... | collective-permute-start | bytes 98312 | tf_op jit(solution)/shard_map/ppermute | solution.py:582
  7.3 0.1 add_multiply_fusion
  7.4 0.1 iota_add_fusion
  7.5 0.3 select_reduce_fusion
  7.8 1.0 %collective-permute-done.pool_ref = bf16[96,1024]{1,0:T(8,128)(2,1)S(1)} collective-permute-done((bf16[96,1024]{1,0:T(8,128)(2,1)}, bf16[96,1024]{1,0:T(8,128)(2,1)S(1)}, u32[]{:S(2)}, u32[]{:S(2)}) %collective-permute-start) | collective-permute-done | bytes 196640 | tf_op jit(solution)/shard_map/ppermute | solution.py:473
  8.7 0.1 merge.2.refs_0_
  8.9 1.9 %collective-permute-start.2 = (bf16[112,1024]{1,0:T(8,128)(2,1)S(1)}, bf16[112,1024]{1,0:T(8,128)(2,1)S(1)}, u32[]{:S(2)}, u32[]{:S(2)}) collective-permute-start(bf16[112,1024]{1,0:T(8,128)(2,1)S(1)} %merge.2.refs_0_), channel_id=1, source_target_pairs={{0,4},{1,5},{4,8},{5,9},{8,12},{9,13},{12,14},{13,15},{14,10},{15,... | collective-permute-start | bytes 688136 | tf_op jit(solution)/shard_map/ppermute | solution.py:589
  10.7 0.1 convert_element_type.14.refs_4_.refs_5_
  10.8 0.2 collective-permute-done.4.block_ref
  11.0 0.1 merge.3.refs_1_
  11.1 0.4 %collective-permute-start.6 = (bf16[112,1024]{1,0:T(8,128)(2,1)S(1)}, bf16[112,1024]{1,0:T(8,128)(2,1)S(1)}, u32[]{:S(2)}, u32[]{:S(2)}) collective-permute-start(bf16[112,1024]{1,0:T(8,128)(2,1)S(1)} %merge.3.refs_1_), channel_id=1, source_target_pairs={{0,2},{1,3},{4,0},{5,1},{8,4},{9,5},{12,8},{13,9},{14,12},{15,13},... | collective-permute-start | bytes 688136 | tf_op jit(solution)/shard_map/ppermute | solution.py:590
  11.5 1.3 %visit.4 = (f32[136,896]{1,0:T(8,128)S(1)}, bf16[256,768]{1,0:T(8,128)(2,1)S(1)}) custom-call(bf16[112,1024]{1,0:T(8,128)(2,1)S(1)} %get-tuple-element.31.refs_0_, bf16[448,128]{1,0:T(8,128)(2,1)S(1)} %get-tuple-element.34.refs_1_.refs_2_, bf16[448,128]{1,0:T(8,128)(2,1)S(1)} %collective-permute-done.1.refs_2_.refs_3_, ...), custom_call_target="tpu_custom_call" | custom-call | flops 381681664 | bytes 4194304 | tf_op jit(solution)/shard_map/visit/pallas_call | solution.py:552
  12.8 2.3 %visit.5 = (f32[136,896]{1,0:T(8,128)S(1)}, bf16[256,768]{1,0:T(8,128)(2,1)S(1)}) custom-call(bf16[112,1024]{1,0:T(8,128)(2,1)S(1)} %merge.2.refs_0_, bf16[112,1024]{1,0:T(8,128)(2,1)S(1)} %merge.3.refs_1_, bf16[448,128]{1,0:T(8,128)(2,1)S(1)} %get-tuple-element.34.refs_1_.refs_2_, ...), custom_call_target="tpu_custom_call", output_to_operand_aliasing={{0}: (6, {}), {1}: (7, {})} | custom-call | flops 763363328 | bytes 4194304 | tf_op jit(solution)/shard_map/visit/pallas_call | solution.py:552
  15.1 0.6 %collective-permute-done.2.refs_0_ = bf16[112,1024]{1,0:T(8,128)(2,1)S(1)} collective-permute-done((bf16[112,1024]{1,0:T(8,128)(2,1)S(1)}, bf16[112,1024]{1,0:T(8,128)(2,1)S(1)}, u32[]{:S(2)}, u32[]{:S(2)}) %collective-permute-start.2) | collective-permute-done | bytes 229408 | tf_op jit(solution)/shard_map/ppermute | solution.py:589
  15.7 1.5 %collective-permute-start.5 = (bf16[112,1024]{1,0:T(8,128)(2,1)S(1)}, bf16[112,1024]{1,0:T(8,128)(2,1)S(1)}, u32[]{:S(2)}, u32[]{:S(2)}) collective-permute-start(bf16[112,1024]{1,0:T(8,128)(2,1)S(1)} %collective-permute-done.2.refs_0_), channel_id=1, source_target_pairs={{0,4},{1,5},{4,8},{5,9},{8,12},{9,13},{12,14},{13,15},{14,10},{15,... | collective-permute-start | bytes 688136 | tf_op jit(solution)/shard_map/ppermute | solution.py:589
  17.2 0.1 collective-permute-done.6.refs_1_
  17.3 1.5 %collective-permute-start.9 = (bf16[112,1024]{1,0:T(8,128)(2,1)S(1)}, bf16[112,1024]{1,0:T(8,128)(2,1)S(1)}, u32[]{:S(2)}, u32[]{:S(2)}) collective-permute-start(bf16[112,1024]{1,0:T(8,128)(2,1)S(1)} %collective-permute-done.6.refs_1_), channel_id=1, source_target_pairs={{0,2},{1,3},{4,0},{5,1},{8,4},{9,5},{12,8},{13,9},{14,12},{15,13},... | collective-permute-start | bytes 688136 | tf_op jit(solution)/shard_map/ppermute | solution.py:590
  18.8 2.3 %visit.6 = (f32[136,896]{1,0:T(8,128)S(1)}, bf16[256,768]{1,0:T(8,128)(2,1)S(1)}) custom-call(bf16[112,1024]{1,0:T(8,128)(2,1)S(1)} %collective-permute-done.2.refs_0_, bf16[112,1024]{1,0:T(8,128)(2,1)S(1)} %collective-permute-done.6.refs_1_, bf16[448,128]{1,0:T(8,128)(2,1)S(1)} %get-tuple-element.34.refs_1_.refs_2_, ...), custom_call_target="tpu_custom_call", output_to_operand_aliasing={{0}: (6, {}), {1}: (7, {})} | custom-call | flops 763363328 | bytes 4194304 | tf_op jit(solution)/shard_map/visit/pallas_call | solution.py:552
  21.1 1.1 %collective-permute-done.5.refs_0_ = bf16[112,1024]{1,0:T(8,128)(2,1)S(1)} collective-permute-done((bf16[112,1024]{1,0:T(8,128)(2,1)S(1)}, bf16[112,1024]{1,0:T(8,128)(2,1)S(1)}, u32[]{:S(2)}, u32[]{:S(2)}) %collective-permute-start.5) | collective-permute-done | bytes 229408 | tf_op jit(solution)/shard_map/ppermute | solution.py:589
  22.2 1.0 %collective-permute-start.7 = (bf16[112,1024]{1,0:T(8,128)(2,1)S(1)}, bf16[112,1024]{1,0:T(8,128)(2,1)S(1)}, u32[]{:S(2)}, u32[]{:S(2)}) collective-permute-start(bf16[112,1024]{1,0:T(8,128)(2,1)S(1)} %collective-permute-done.5.refs_0_), channel_id=1, source_target_pairs={{0,4},{1,5},{4,8},{5,9},{8,12},{9,13},{12,14},{13,15},{14,10},{15,... | collective-permute-start | bytes 688136 | tf_op jit(solution)/shard_map/ppermute | solution.py:594
  23.2 0.1 collective-permute-done.9.refs_1_
  23.3 1.9 %collective-permute-start.10 = (bf16[16,1024]{1,0:T(8,128)(2,1)S(1)}, bf16[16,1024]{1,0:T(8,128)(2,1)S(1)}, u32[]{:S(2)}, u32[]{:S(2)}) collective-permute-start(bf16[16,1024]{1,0:T(8,128)(2,1)S(1)} %slice.8), channel_id=1, source_target_pairs={{0,2},{1,3},{4,0},{5,1},{8,4},{9,5},{12,8},{13,9},{14,12},{15,13},... | collective-permute-start | bytes 98312 | tf_op jit(solution)/shard_map/ppermute | solution.py:595
  25.3 2.2 %visit.7 = (f32[136,448]{1,0:T(8,128)S(1)}, bf16[96,1024]{1,0:T(8,128)(2,1)S(1)}, f32[136,448]{1,0:T(8,128)S(1)}, bf16[96,1024]{1,0:T(8,128)(2,1)S(1)}) custom-call(bf16[112,1024]{1,0:T(8,128)(2,1)S(1)} %collective-permute-done.5.refs_0_, bf16[112,1024]{1,0:T(8,128)(2,1)S(1)} %collective-permute-done.9.refs_1_, ...), custom_call_target="tpu_custom_call" | custom-call | flops 763363328 | bytes 4194304 | tf_op jit(solution)/shard_map/visit/pallas_call | solution.py:552
  27.5 0.5 %collective-permute-start.13 = (bf16[96,1024]{1,0:T(8,128)(2,1)S(1)}, bf16[96,1024]{1,0:T(8,128)(2,1)S(1)}, u32[]{:S(2)}, u32[]{:S(2)}) collective-permute-start(bf16[96,1024]{1,0:T(8,128)(2,1)S(1)} %get-tuple-element.59), channel_id=1, source_target_pairs={{0,1},{1,0},{2,3},{3,2},{4,5},{5,4},{6,7},{7,6},{8,9},{9,8},{10,11... | collective-permute-start | bytes 589832 | tf_op jit(solution)/shard_map/ppermute | solution.py:598
  28.0 0.1 collective-permute-start.11
  28.1 0.1 collective-permute-done.7.refs_0_
  28.2 0.3 %collective-permute-start.8 = (bf16[112,1024]{1,0:T(8,128)(2,1)S(1)}, bf16[112,1024]{1,0:T(8,128)(2,1)S(1)}, u32[]{:S(2)}, u32[]{:S(2)}) collective-permute-start(bf16[112,1024]{1,0:T(8,128)(2,1)S(1)} %collective-permute-done.7.refs_0_), channel_id=1, source_target_pairs={{0,1},{1,0},{2,3},{3,2},{4,5},{5,4},{6,7},{7,6},{8,9},{9,8},{10,11... | collective-permute-start | bytes 688136 | tf_op jit(solution)/shard_map/ppermute | solution.py:599
  28.6 1.4 %close.1 = (f32[136,448]{1,0:T(8,128)S(1)}, bf16[96,1024]{1,0:T(8,128)(2,1)S(1)}, f32[512,128]{1,0:T(8,128)S(1)}, bf16[384,512]{1,0:T(8,128)(2,1)S(1)}) custom-call(bf16[112,1024]{1,0:T(8,128)(2,1)S(1)} %collective-permute-done.7.refs_0_, bf16[16,1024]{1,0:T(8,128)(2,1)S(1)} %collective-permute-done.10.refs_1_, ...), custom_call_target="tpu_custom_call" | custom-call | flops 4362076160 | bytes 41943040 | tf_op jit(solution)/shard_map/close/pallas_call | solution.py:552
  30.0 1.5 %finish.1 = (bf16[56,1024]{1,0:T(8,128)(2,1)}, bf16[96,1024]{1,0:T(8,128)(2,1)}) custom-call(bf16[112,1024]{1,0:T(8,128)(2,1)S(1)} %collective-permute-done.8.refs_0_, bf16[16,1024]{1,0:T(8,128)(2,1)S(1)} %collective-permute-done.11.refs_1_, bf16[448,128]{1,0:T(8,128)(2,1)S(1)} %get-tuple-element.34.refs_1_.refs_2_, ...), custom_call_target="tpu_custom_call" | custom-call | flops 436207616 | bytes 4194304 | tf_op jit(solution)/shard_map/finish/pallas_call | solution.py:552
  (13 shorter events, 0.1 us)
Async XLA Ops:
  0.6 8.1 %collective-permute-start = (bf16[96,1024]{1,0:T(8,128)(2,1)}, bf16[96,1024]{1,0:T(8,128)(2,1)S(1)}, u32[]{:S(2)}, u32[]{:S(2)}) collective-permute-start(bf16[96,1024]{1,0:T(8,128)(2,1)} %refs_7_.1), channel_id=1, source_target_pairs={{0,4},{1,5},{4,8},{5,9},{8,12},{9,13},{12,14},{13,15},{14,10},{15,... | collective-permute-start | bytes 589832 | tf_op jit(solution)/shard_map/ppermute | solution.py:473
  3.7 7.3 %collective-permute-start.3 = (bf16[96,1024]{1,0:T(8,128)(2,1)}, bf16[96,1024]{1,0:T(8,128)(2,1)S(1)}, u32[]{:S(2)}, u32[]{:S(2)}) collective-permute-start(bf16[96,1024]{1,0:T(8,128)(2,1)} %refs_7_.1), channel_id=1, source_target_pairs={{0,2},{1,3},{4,0},{5,1},{8,4},{9,5},{12,8},{13,9},{14,12},{15,13},... | collective-permute-start | bytes 589832 | tf_op jit(solution)/shard_map/ppermute | solution.py:474
  5.2 3.6 %collective-permute-start.1 = (bf16[448,128]{1,0:T(8,128)(2,1)S(1)}, bf16[448,128]{1,0:T(8,128)(2,1)S(1)}, u32[]{:S(2)}, u32[]{:S(2)}) collective-permute-start(bf16[448,128]{1,0:T(8,128)(2,1)S(1)} %get-tuple-element.34.refs_1_.refs_2_), channel_id=1, source_target_pairs={{0,1},{1,0},{2,3},{3,2},{4,5},{5,4},{6,7},{7,6},{8,9},{9,8},{10,11... | collective-permute-start | bytes 344072 | tf_op jit(solution)/shard_map/ppermute | solution.py:527
  5.3 5.7 %collective-permute-start.4 = (bf16[16,1024]{1,0:T(8,128)(2,1)S(1)}, bf16[16,1024]{1,0:T(8,128)(2,1)S(1)}, u32[]{:S(2)}, u32[]{:S(2)}) collective-permute-start(bf16[16,1024]{1,0:T(8,128)(2,1)S(1)} %slice.6.block_ref), channel_id=1, source_target_pairs={{0,2},{1,3},{4,0},{5,1},{8,4},{9,5},{12,8},{13,9},{14,12},{15,13},... | collective-permute-start | bytes 98312 | tf_op jit(solution)/shard_map/ppermute | solution.py:582
  8.9 6.8 %collective-permute-start.2 = (bf16[112,1024]{1,0:T(8,128)(2,1)S(1)}, bf16[112,1024]{1,0:T(8,128)(2,1)S(1)}, u32[]{:S(2)}, u32[]{:S(2)}) collective-permute-start(bf16[112,1024]{1,0:T(8,128)(2,1)S(1)} %merge.2.refs_0_), channel_id=1, source_target_pairs={{0,4},{1,5},{4,8},{5,9},{8,12},{9,13},{12,14},{13,15},{14,10},{15,... | collective-permute-start | bytes 688136 | tf_op jit(solution)/shard_map/ppermute | solution.py:589
  11.1 6.2 %collective-permute-start.6 = (bf16[112,1024]{1,0:T(8,128)(2,1)S(1)}, bf16[112,1024]{1,0:T(8,128)(2,1)S(1)}, u32[]{:S(2)}, u32[]{:S(2)}) collective-permute-start(bf16[112,1024]{1,0:T(8,128)(2,1)S(1)} %merge.3.refs_1_), channel_id=1, source_target_pairs={{0,2},{1,3},{4,0},{5,1},{8,4},{9,5},{12,8},{13,9},{14,12},{15,13},... | collective-permute-start | bytes 688136 | tf_op jit(solution)/shard_map/ppermute | solution.py:590
  15.7 6.5 %collective-permute-start.5 = (bf16[112,1024]{1,0:T(8,128)(2,1)S(1)}, bf16[112,1024]{1,0:T(8,128)(2,1)S(1)}, u32[]{:S(2)}, u32[]{:S(2)}) collective-permute-start(bf16[112,1024]{1,0:T(8,128)(2,1)S(1)} %collective-permute-done.2.refs_0_), channel_id=1, source_target_pairs={{0,4},{1,5},{4,8},{5,9},{8,12},{9,13},{12,14},{13,15},{14,10},{15,... | collective-permute-start | bytes 688136 | tf_op jit(solution)/shard_map/ppermute | solution.py:589
  17.3 6.0 %collective-permute-start.9 = (bf16[112,1024]{1,0:T(8,128)(2,1)S(1)}, bf16[112,1024]{1,0:T(8,128)(2,1)S(1)}, u32[]{:S(2)}, u32[]{:S(2)}) collective-permute-start(bf16[112,1024]{1,0:T(8,128)(2,1)S(1)} %collective-permute-done.6.refs_1_), channel_id=1, source_target_pairs={{0,2},{1,3},{4,0},{5,1},{8,4},{9,5},{12,8},{13,9},{14,12},{15,13},... | collective-permute-start | bytes 688136 | tf_op jit(solution)/shard_map/ppermute | solution.py:590
  22.2 6.0 %collective-permute-start.7 = (bf16[112,1024]{1,0:T(8,128)(2,1)S(1)}, bf16[112,1024]{1,0:T(8,128)(2,1)S(1)}, u32[]{:S(2)}, u32[]{:S(2)}) collective-permute-start(bf16[112,1024]{1,0:T(8,128)(2,1)S(1)} %collective-permute-done.5.refs_0_), channel_id=1, source_target_pairs={{0,4},{1,5},{4,8},{5,9},{8,12},{9,13},{12,14},{13,15},{14,10},{15,... | collective-permute-start | bytes 688136 | tf_op jit(solution)/shard_map/ppermute | solution.py:594
  23.3 4.7 %collective-permute-start.10 = (bf16[16,1024]{1,0:T(8,128)(2,1)S(1)}, bf16[16,1024]{1,0:T(8,128)(2,1)S(1)}, u32[]{:S(2)}, u32[]{:S(2)}) collective-permute-start(bf16[16,1024]{1,0:T(8,128)(2,1)S(1)} %slice.8), channel_id=1, source_target_pairs={{0,2},{1,3},{4,0},{5,1},{8,4},{9,5},{12,8},{13,9},{14,12},{15,13},... | collective-permute-start | bytes 98312 | tf_op jit(solution)/shard_map/ppermute | solution.py:595
  27.5 2.5 %collective-permute-start.12 = (f32[136,448]{1,0:T(8,128)S(1)}, f32[136,448]{1,0:T(8,128)S(1)}, u32[]{:S(2)}, u32[]{:S(2)}) collective-permute-start(f32[136,448]{1,0:T(8,128)S(1)} %get-tuple-element.58), channel_id=1, source_target_pairs={{0,1},{1,0},{2,3},{3,2},{4,5},{5,4},{6,7},{7,6},{8,9},{9,8},{10,11... | collective-permute-start | bytes 731144 | tf_op jit(solution)/shard_map/ppermute | solution.py:597
  27.5 2.4 %collective-permute-start.13 = (bf16[96,1024]{1,0:T(8,128)(2,1)S(1)}, bf16[96,1024]{1,0:T(8,128)(2,1)S(1)}, u32[]{:S(2)}, u32[]{:S(2)}) collective-permute-start(bf16[96,1024]{1,0:T(8,128)(2,1)S(1)} %get-tuple-element.59), channel_id=1, source_target_pairs={{0,1},{1,0},{2,3},{3,2},{4,5},{5,4},{6,7},{7,6},{8,9},{9,8},{10,11... | collective-permute-start | bytes 589832 | tf_op jit(solution)/shard_map/ppermute | solution.py:598
  28.0 1.9 %collective-permute-start.11 = (bf16[16,1024]{1,0:T(8,128)(2,1)S(1)}, bf16[16,1024]{1,0:T(8,128)(2,1)S(1)}, u32[]{:S(2)}, u32[]{:S(2)}) collective-permute-start(bf16[16,1024]{1,0:T(8,128)(2,1)S(1)} %collective-permute-done.10.refs_1_), channel_id=1, source_target_pairs={{0,1},{1,0},{2,3},{3,2},{4,5},{5,4},{6,7},{7,6},{8,9},{9,8},{10,11... | collective-permute-start | bytes 98312 | tf_op jit(solution)/shard_map/ppermute | solution.py:600
  28.2 1.7 %collective-permute-start.8 = (bf16[112,1024]{1,0:T(8,128)(2,1)S(1)}, bf16[112,1024]{1,0:T(8,128)(2,1)S(1)}, u32[]{:S(2)}, u32[]{:S(2)}) collective-permute-start(bf16[112,1024]{1,0:T(8,128)(2,1)S(1)} %collective-permute-done.7.refs_0_), channel_id=1, source_target_pairs={{0,1},{1,0},{2,3},{3,2},{4,5},{5,4},{6,7},{7,6},{8,9},{9,8},{10,11... | collective-permute-start | bytes 688136 | tf_op jit(solution)/shard_map/ppermute | solution.py:599
